TPU v7x, 32 devices: a whole 2x2x4 slice. The times are simulated.
32 devices in a mesh: stream: 8 (over z, x), span: 4 (over y, core).
Axes of the slice: x: 2, y: 2, z: 4, core: 2. Of those that a mesh axis runs over, the one named last changes fastest.
Arguments:
- rhs: float32 [8, 4, 2, 320, 128], P('stream', 'span'), may hold values from -6 to 6
- inv_blocks: bfloat16 [8, 4, 2, 320, 320], P('stream', 'span')
- coupling: bfloat16 [6, 320, 320], replicated, may hold values from -0.109375 to 0.109375
- trace_ops: bfloat16 [4, 80, 320], replicated, may hold values from -0.3125 to 0.3125
- lift_ops: bfloat16 [4, 320, 80], replicated
- order: int32 [8, 4, 2], P('stream', 'span'), may hold values from 0 to 1, each once within a row
- counts: int32 [8, 4], P('stream', 'span'), may hold values from 1 to 2, as said below
- neighbours: int32 [8, 4, 2, 2], P('stream', 'span'), may hold values from 0 to 2, as said below
- face_ids: int32 [8, 4, 2, 2], P('stream', 'span'), may hold values from 0 to 5
Outputs:
- solution: float32 [8, 4, 2, 320, 128], P('stream', 'span')
Inputs may be any that keep to these rules, and one draw needn't show every extreme that they name: order[i, j] lists each of the 2 slots of line (i, j) once. `counts`: some line holds 2 live elements and some line 1. `neighbours`: a slot of the same line other than the element's own, or 2 where the face has no in-line neighbour.
All inputs are finite; a program needn't handle non-finite values.
Results may differ from a plain program's by a relative error of at most 0.00075.
Values sent between devices are 32-bit elements; how exact they have to be, the bound alone decides.
No kernel may reach another device: no remote copies, remote signals or barrier semaphores. Data moves between devices by JAX's collectives and lax.ppermute only.
A program may use at most 64 MiB of HBM per device.

v0:
```python
from functools import partial

import jax
import jax.numpy as jnp
from jax import lax
from jax.sharding import PartitionSpec as P

SWEEPS = 2


HIGH = lax.Precision.HIGHEST


def passed_along(block, axis, distance):
    devices = range(lax.axis_size(axis))
    route = [((i - distance) % len(devices), i) for i in devices]
    return lax.ppermute(block, axis, route)


def passed_along_2(block, axis, distance):
    devices = range(lax.axis_size(axis))
    route = [(i - distance, i) for i in devices if i - distance in devices]
    return lax.ppermute(block, axis, route)


def prefix(part, axis, combine, identity, reverse):
    count = lax.axis_size(axis)
    place = lax.axis_index(axis)
    ahead = count - 1 - place if reverse else place
    gathered = jax.tree.map(lambda a: lax.all_gather(a, axis), part)
    state = jax.tree.map(lambda a, e: jnp.zeros_like(a) + jnp.asarray(e, a.dtype), part, identity)

    def one(lap, state):
        source = count - 1 - lap if reverse else lap
        return combine(
            state, jax.tree.map(lambda a: lax.dynamic_index_in_dim(a, source, 0, False), gathered)
        )

    return lax.fori_loop(0, ahead, one, state)


def column_sweep(
    solution, residual, inverse, order, count, neighbours, face_ids, coupling, backward
):
    slot_count = solution.shape[0]
    positions = range(slot_count - 1, -1, -1) if backward else range(slot_count)
    for position in positions:
        slot_index = order[position]
        residual_now = lax.dynamic_index_in_dim(residual, slot_index, 0, keepdims=False)
        for face_index in range(neighbours.shape[1]):
            neighbour_slot = neighbours[slot_index, face_index]
            present = neighbour_slot < slot_count
            neighbour_block = lax.dynamic_index_in_dim(
                solution, jnp.minimum(neighbour_slot, slot_count - 1), 0, keepdims=False
            )
            coupling_block = lax.dynamic_index_in_dim(
                coupling, face_ids[slot_index, face_index], 0, keepdims=False
            )
            product = jnp.dot(coupling_block, neighbour_block, precision=HIGH)
            residual_now = residual_now - jnp.where(present, product, jnp.zeros_like(product))
        inverse_block = lax.dynamic_index_in_dim(inverse, slot_index, 0, keepdims=False).astype(
            jnp.float32
        )
        live_factor = (position < count).astype(jnp.float32)
        updated = jnp.dot(inverse_block, residual_now, precision=HIGH) * live_factor
        solution = lax.dynamic_update_index_in_dim(solution, updated, slot_index, 0)
    return solution


def apply_trace(operator, values):
    return jnp.einsum("tb,ebr->etr", operator, values, precision=HIGH)


def apply_lift(operator, traces):
    return jnp.einsum("bt,etr->ebr", operator, traces, precision=HIGH)


def compose(earlier, later):
    first_map, first_shift = earlier
    second_map, second_shift = later
    joined_map = jnp.dot(second_map, first_map, precision=HIGH)
    joined_shift = jnp.dot(second_map, first_shift, precision=HIGH) + second_shift
    return (joined_map, joined_shift)


def local(rhs, inv_blocks, coupling, trace_ops, lift_ops, order, counts, neighbours, face_ids):
    source = rhs[0, 0]
    inverse = inv_blocks[0, 0]
    sweep_order = order[0, 0]
    live_count = counts[0, 0]
    line_links = neighbours[0, 0]
    link_types = face_ids[0, 0]
    coupling_table = coupling.astype(jnp.float32)
    traces_op = trace_ops.astype(jnp.float32)
    lifts = lift_ops.astype(jnp.float32)
    slot_count, block_width, columns = source.shape
    face_width = traces_op.shape[1]
    state_width = slot_count * face_width
    line_sweep = partial(
        column_sweep,
        inverse=inverse,
        order=sweep_order,
        count=live_count,
        neighbours=line_links,
        face_ids=link_types,
        coupling=coupling_table,
    )
    selector = jnp.eye(slot_count, dtype=jnp.float32)

    def response(inflow_lift, outflow_trace, backward):
        entry_terms = -jnp.einsum("ef,bt->ebft", selector, inflow_lift, precision=HIGH).reshape(
            slot_count, block_width, state_width
        )
        response_field = line_sweep(jnp.zeros_like(entry_terms), entry_terms, backward=backward)
        transfer_map = apply_trace(outflow_trace, response_field).reshape(state_width, state_width)
        return (response_field, transfer_map)

    forward_maps = response(lifts[0], traces_op[1], False)
    backward_maps = response(lifts[1], traces_op[0], True)
    identity_pair = (
        jnp.eye(state_width, dtype=jnp.float32),
        jnp.zeros((state_width, columns), jnp.float32),
    )

    def half_sweep(solution, backward, first):
        residual_base = source
        if not first:
            from_left = passed_along(solution, "span", 1)
            from_right = passed_along(solution, "span", -1)
            left_traces = apply_trace(traces_op[3], from_left)
            right_traces = apply_trace(traces_op[2], from_right)
            residual_base = (
                residual_base
                - apply_lift(lifts[2], left_traces)
                - apply_lift(lifts[3], right_traces)
            )
            if backward:
                behind = passed_along_2(apply_trace(traces_op[1], solution), "stream", 1)
                residual_base = residual_base - apply_lift(lifts[0], behind)
            else:
                downstream = passed_along_2(apply_trace(traces_op[0], solution), "stream", -1)
                residual_base = residual_base - apply_lift(lifts[1], downstream)
        if backward:
            response_field, transfer_map = backward_maps
            outflow = traces_op[0]
        else:
            response_field, transfer_map = forward_maps
            outflow = traces_op[1]
        local_field = line_sweep(solution, residual_base, backward=backward)
        local_shift = apply_trace(outflow, local_field).reshape(state_width, columns)
        if backward:
            inflow_pair = prefix(
                (transfer_map, local_shift), "stream", compose, identity_pair, True
            )
        else:
            inflow_pair = prefix(
                (transfer_map, local_shift), "stream", compose, identity_pair, False
            )
        inflow = inflow_pair[1]
        return local_field + jnp.einsum("ebs,sr->ebr", response_field, inflow, precision=HIGH)

    solution = jnp.zeros_like(source)
    for sweep_index in range(SWEEPS):
        solution = half_sweep(solution, False, sweep_index == 0)
        solution = half_sweep(solution, True, False)
    return solution[None, None]


def solution(mesh):
    placed = (
        P("stream", "span", None, None, None),
        P("stream", "span", None, None, None),
        P(),
        P(),
        P(),
        P("stream", "span", None),
        P("stream", "span"),
        P("stream", "span", None, None),
        P("stream", "span", None, None),
    )
    return jax.shard_map(
        local,
        mesh=mesh,
        in_specs=placed,
        out_specs=P("stream", "span", None, None, None),
        check_vma=False,
    )
```

profile of v0, /device:TPU:0, one launch (start us, length us, event | category | flops | bytes accessed | tf_op | source)
XLA Modules:
  0.0 321.9 jit_solution(8907868941289521261)
XLA Ops:
  0.0 1.4 fusion.278
  5.0 1.5 constant_dynamic-slice_fusion
  24.8 37.7 %all_gather.20 = f32[8,160,160]{2,1,0:T(8,128)} all-gather(f32[1,160,160]{2,1,0:T(8,128)S(1)} %bitcast.487), channel_id=1, replica_groups=mesh['stream'=8,'span'=4] {'stream'}, dimensions={0}, use_global_device_ids=true | all-gather | bytes 921600 | tf_op jit(solution)/shard_map/all_gather | solution.py:30
  64.5 33.8 %all_gather.21 = f32[8,160,128]{2,1,0:T(8,128)} all-gather(f32[1,160,128]{2,1,0:T(8,128)S(1)} %bitcast.488), channel_id=1, replica_groups=mesh['stream'=8,'span'=4] {'stream'}, dimensions={0}, use_global_device_ids=true | all-gather | bytes 737280 | tf_op jit(solution)/shard_map/all_gather | solution.py:30
  98.3 1.3 convolution_add_fusion.7
  99.7 1.7 collective-permute-start.1
  102.4 4.9 %collective-permute-start.2 = (f32[2,80,128]{2,1,0:T(8,128)}, f32[2,80,128]{2,1,0:T(8,128)}, u32[]{:S(2)}, u32[]{:S(2)}) collective-permute-start(f32[2,80,128]{2,1,0:T(8,128)} %convolution_bitcast_fusion.15), channel_id=1, source_target_pairs={{0,4},{4,8},{8,12},{12,16},{16,20},{20,24},{24,28},{1,5},{5,9},{9,... | collective-permute-start | bytes 245768 | tf_op jit(solution)/shard_map/ppermute | solution.py:23
  110.6 1.4 fusion.25
  112.5 2.1 fusion.29
  114.6 1.4 fusion.28
  117.6 44.2 %all_gather.22 = f32[8,160,160]{2,1,0:T(8,128)} all-gather(f32[1,160,160]{2,1,0:T(8,128)} %bitcast.486), channel_id=1, replica_groups=mesh['stream'=8,'span'=4] {'stream'}, dimensions={0}, use_global_device_ids=true | all-gather | bytes 921600 | tf_op jit(solution)/shard_map/all_gather | solution.py:30
  168.4 33.5 %all_gather.23 = f32[8,160,128]{2,1,0:T(8,128)} all-gather(f32[1,160,128]{2,1,0:T(8,128)S(1)} %bitcast.489), channel_id=1, replica_groups=mesh['stream'=8,'span'=4] {'stream'}, dimensions={0}, use_global_device_ids=true | all-gather | bytes 737280 | tf_op jit(solution)/shard_map/all_gather | solution.py:30
  201.9 9.1 %while.53 = (s32[]{:T(128)}, f32[160,128]{1,0:T(8,128)S(1)}, s32[]{:T(128)}, f32[8,160,160]{2,1,0:T(8,128)}, f32[8,160,128]{2,1,0:T(8,128)}, /*index=5*/s32[]{:T(128)}, s32[]{:T(128)}, s32[]{:T(128)}, s32[]{:T(128)}) while((s32[]{:T(128)}, f32[160,128]{1,0:T(8,128)S(1)}, s32[]{:T(128)}, f32[8,160,160]{2,1,0:T(8,128)}, ...), condition=%wide.region_3.4_spmd, body=%wide.region_2.3_spmd.sunk | while | flops 39342084 | bytes 574603 | solution.py:39
  211.1 1.3 convolution_add_fusion.6
  212.5 1.7 collective-permute-start.4
  217.0 3.7 %collective-permute-done.3 = f32[2,320,128]{2,1,0:T(8,128)S(1)} collective-permute-done((f32[2,320,128]{2,1,0:T(8,128)S(1)}, f32[2,320,128]{2,1,0:T(8,128)S(1)}, u32[]{:S(2)}, u32[]{:S(2)}) %collective-permute-start.3) | collective-permute-done | bytes 327712 | tf_op jit(solution)/shard_map/ppermute | solution.py:17
  225.2 34.0 %all_gather.24 = f32[8,160,128]{2,1,0:T(8,128)} all-gather(f32[1,160,128]{2,1,0:T(8,128)S(1)} %bitcast.490), channel_id=1, replica_groups=mesh['stream'=8,'span'=4] {'stream'}, dimensions={0}, use_global_device_ids=true | all-gather | bytes 737280 | tf_op jit(solution)/shard_map/all_gather | solution.py:30
  259.2 2.4 convolution_add_fusion.5
  261.6 1.7 collective-permute-start.7
  264.4 1.5 collective-permute-start.8
  266.3 3.0 collective-permute-done.6
  274.0 37.1 %all_gather.25 = f32[8,160,128]{2,1,0:T(8,128)S(1)} all-gather(f32[1,160,128]{2,1,0:T(8,128)S(1)} %bitcast.491), channel_id=1, replica_groups=mesh['stream'=8,'span'=4] {'stream'}, dimensions={0}, use_global_device_ids=true | all-gather | bytes 737280 | tf_op jit(solution)/shard_map/all_gather | solution.py:30
  311.1 8.8 %while.55 = (s32[]{:T(128)}, f32[160,128]{1,0:T(8,128)S(1)}, s32[]{:T(128)}, f32[8,160,160]{2,1,0:T(8,128)}, f32[8,160,128]{2,1,0:T(8,128)S(1)}, /*index=5*/s32[]{:T(128)}, s32[]{:T(128)}, s32[]{:T(128)}, s32[]{:T(128)}) while((s32[]{:T(128)}, f32[160,128]{1,0:T(8,128)S(1)}, s32[]{:T(128)}, f32[8,160,160]{2,1,0:T(8,128)}, ...), condition=%wide.region_7.8_spmd, body=%wide.region_6.7_spmd.sunk | while | flops 39342084 | bytes 574603 | solution.py:39
  319.9 2.0 fusion.12
  (140 shorter events, 50.3 us)
Async XLA Ops:
  0.0 15.4 %copy-start = (bf16[6,320,320]{2,1,0:T(8,128)(2,1)S(1)}, bf16[6,320,320]{2,1,0:T(8,128)(2,1)}, u32[]{:S(2)}) copy-start(bf16[6,320,320]{2,1,0:T(8,128)(2,1)} %param.19) | copy-start | bytes 3686404
  16.9 5.5 %copy-start.1 = (bf16[1,1,2,320,320]{4,3,2,1,0:T(8,128)(2,1)S(1)}, bf16[1,1,2,320,320]{4,3,2,1,0:T(8,128)(2,1)}, u32[]{:S(2)}) copy-start(bf16[1,1,2,320,320]{4,3,2,1,0:T(8,128)(2,1)} %param.18) | copy-start | bytes 1228804
  22.9 1.4 copy-start.7
  23.8 38.6 %copy-start.3 = (f32[1,1,2,320,128]{4,3,2,1,0:T(8,128)S(1)}, f32[1,1,2,320,128]{4,3,2,1,0:T(8,128)}, u32[]{:S(2)}) copy-start(f32[1,1,2,320,128]{4,3,2,1,0:T(8,128)} %param.17) | copy-start | bytes 983044
  23.8 38.6 %copy-start.14 = (f32[320,128]{1,0:T(8,128)S(1)}, f32[320,128]{1,0:T(8,128)}, u32[]{:S(2)}) copy-start(f32[320,128]{1,0:T(8,128)} %convolution_select_fusion.8) | copy-start | bytes 491524
  99.7 11.0 %copy-start.10 = (f32[2,2,320,80]{2,3,1,0:T(8,128)S(1)}, f32[2,2,320,80]{2,3,1,0:T(8,128)}, u32[]{:S(2)}) copy-start(f32[2,2,320,80]{2,3,1,0:T(8,128)} %get-tuple-element.307) | copy-start | bytes 1228804
  99.7 62.2 %collective-permute-start = (f32[2,320,128]{2,1,0:T(8,128)S(1)}, f32[2,320,128]{2,1,0:T(8,128)}, u32[]{:S(2)}, u32[]{:S(2)}) collective-permute-start(f32[2,320,128]{2,1,0:T(8,128)S(1)} %convolution_add_fusion.7), channel_id=1, source_target_pairs={{3,0},{0,1},{1,2},{2,3},{7,4},{4,5},{5,6},{6,7},{11,8},{8,9},{9,10... | collective-permute-start | bytes 983048 | tf_op jit(solution)/shard_map/ppermute | solution.py:17
  99.7 63.8 %collective-permute-start.1 = (f32[2,320,128]{2,1,0:T(8,128)S(1)}, f32[2,320,128]{2,1,0:T(8,128)}, u32[]{:S(2)}, u32[]{:S(2)}) collective-permute-start(f32[2,320,128]{2,1,0:T(8,128)S(1)} %convolution_add_fusion.7), channel_id=1, source_target_pairs={{1,0},{2,1},{3,2},{0,3},{5,4},{6,5},{7,6},{4,7},{9,8},{10,9},{11,1... | collective-permute-start | bytes 983048 | tf_op jit(solution)/shard_map/ppermute | solution.py:17
  102.4 62.7 %collective-permute-start.2 = (f32[2,80,128]{2,1,0:T(8,128)}, f32[2,80,128]{2,1,0:T(8,128)}, u32[]{:S(2)}, u32[]{:S(2)}) collective-permute-start(f32[2,80,128]{2,1,0:T(8,128)} %convolution_bitcast_fusion.15), channel_id=1, source_target_pairs={{0,4},{4,8},{8,12},{12,16},{16,20},{20,24},{24,28},{1,5},{5,9},{9,... | collective-permute-start | bytes 245768 | tf_op jit(solution)/shard_map/ppermute | solution.py:23
  117.6 45.5 %copy-start.4 = (f32[1,1,2,320,128]{4,3,2,1,0:T(8,128)S(1)}, f32[1,1,2,320,128]{4,3,2,1,0:T(8,128)}, u32[]{:S(2)}) copy-start(f32[1,1,2,320,128]{4,3,2,1,0:T(8,128)} %param.17) | copy-start | bytes 983044
  117.6 45.5 %copy-start.11 = (bf16[4,320,80]{1,2,0:T(8,128)(2,1)S(1)}, bf16[4,320,80]{1,2,0:T(8,128)(2,1)}, u32[]{:S(2)}) copy-start(bf16[4,320,80]{1,2,0:T(8,128)(2,1)} %param.21) | copy-start | bytes 614404
  163.1 3.2 %copy-start.15 = (f32[320,128]{1,0:T(8,128)S(1)}, f32[320,128]{1,0:T(8,128)}, u32[]{:S(2)}) copy-start(f32[320,128]{1,0:T(8,128)} %convolution_select_fusion.21) | copy-start | bytes 491524
  211.1 9.6 %copy-start.8 = (bf16[4,80,320]{2,1,0:T(8,128)(2,1)S(1)}, bf16[4,80,320]{2,1,0:T(8,128)(2,1)}, u32[]{:S(2)}) copy-start(bf16[4,80,320]{2,1,0:T(8,128)(2,1)} %param.20) | copy-start | bytes 614404
  211.1 9.9 %copy-start.5 = (f32[1,1,2,320,128]{4,3,2,1,0:T(8,128)S(1)}, f32[1,1,2,320,128]{4,3,2,1,0:T(8,128)}, u32[]{:S(2)}) copy-start(f32[1,1,2,320,128]{4,3,2,1,0:T(8,128)} %param.17) | copy-start | bytes 983044
  211.1 9.9 %copy-start.12 = (bf16[4,320,80]{1,2,0:T(8,128)(2,1)S(1)}, bf16[4,320,80]{1,2,0:T(8,128)(2,1)}, u32[]{:S(2)}) copy-start(bf16[4,320,80]{1,2,0:T(8,128)(2,1)} %param.21) | copy-start | bytes 614404
  212.4 8.3 %collective-permute-start.3 = (f32[2,320,128]{2,1,0:T(8,128)S(1)}, f32[2,320,128]{2,1,0:T(8,128)S(1)}, u32[]{:S(2)}, u32[]{:S(2)}) collective-permute-start(f32[2,320,128]{2,1,0:T(8,128)S(1)} %convolution_add_fusion.6), channel_id=1, source_target_pairs={{3,0},{0,1},{1,2},{2,3},{7,4},{4,5},{5,6},{6,7},{11,8},{8,9},{9,10... | collective-permute-start | bytes 983048 | tf_op jit(solution)/shard_map/ppermute | solution.py:17
  212.5 8.9 %collective-permute-start.4 = (f32[2,320,128]{2,1,0:T(8,128)S(1)}, f32[2,320,128]{2,1,0:T(8,128)S(1)}, u32[]{:S(2)}, u32[]{:S(2)}) collective-permute-start(f32[2,320,128]{2,1,0:T(8,128)S(1)} %convolution_add_fusion.6), channel_id=1, source_target_pairs={{1,0},{2,1},{3,2},{0,3},{5,4},{6,5},{7,6},{4,7},{9,8},{10,9},{11,1... | collective-permute-start | bytes 983048 | tf_op jit(solution)/shard_map/ppermute | solution.py:17
  215.3 6.7 %collective-permute-start.5 = (f32[2,80,128]{2,1,0:T(8,128)S(1)}, f32[2,80,128]{2,1,0:T(8,128)S(1)}, u32[]{:S(2)}, u32[]{:S(2)}) collective-permute-start(f32[2,80,128]{2,1,0:T(8,128)S(1)} %convolution_bitcast_fusion.12), channel_id=1, source_target_pairs={{4,0},{8,4},{12,8},{16,12},{20,16},{24,20},{28,24},{5,1},{9,5},{13... | collective-permute-start | bytes 245768 | tf_op jit(solution)/shard_map/ppermute | solution.py:23
  259.1 10.2 %copy-start.9 = (bf16[4,80,320]{2,1,0:T(8,128)(2,1)S(1)}, bf16[4,80,320]{2,1,0:T(8,128)(2,1)}, u32[]{:S(2)}) copy-start(bf16[4,80,320]{2,1,0:T(8,128)(2,1)} %param.20) | copy-start | bytes 614404
  259.1 10.4 %copy-start.6 = (f32[1,1,2,320,128]{4,3,2,1,0:T(8,128)S(1)}, f32[1,1,2,320,128]{4,3,2,1,0:T(8,128)}, u32[]{:S(2)}) copy-start(f32[1,1,2,320,128]{4,3,2,1,0:T(8,128)} %param.17) | copy-start | bytes 983044
  259.2 10.4 %copy-start.13 = (bf16[4,320,80]{1,2,0:T(8,128)(2,1)S(1)}, bf16[4,320,80]{1,2,0:T(8,128)(2,1)}, u32[]{:S(2)}) copy-start(bf16[4,320,80]{1,2,0:T(8,128)(2,1)} %param.21) | copy-start | bytes 614404
  261.5 7.8 %collective-permute-start.6 = (f32[2,320,128]{2,1,0:T(8,128)S(1)}, f32[2,320,128]{2,1,0:T(8,128)S(1)}, u32[]{:S(2)}, u32[]{:S(2)}) collective-permute-start(f32[2,320,128]{2,1,0:T(8,128)S(1)} %convolution_add_fusion.5), channel_id=1, source_target_pairs={{3,0},{0,1},{1,2},{2,3},{7,4},{4,5},{5,6},{6,7},{11,8},{8,9},{9,10... | collective-permute-start | bytes 983048 | tf_op jit(solution)/shard_map/ppermute | solution.py:17
  261.6 9.4 %collective-permute-start.7 = (f32[2,320,128]{2,1,0:T(8,128)S(1)}, f32[2,320,128]{2,1,0:T(8,128)S(1)}, u32[]{:S(2)}, u32[]{:S(2)}) collective-permute-start(f32[2,320,128]{2,1,0:T(8,128)S(1)} %convolution_add_fusion.5), channel_id=1, source_target_pairs={{1,0},{2,1},{3,2},{0,3},{5,4},{6,5},{7,6},{4,7},{9,8},{10,9},{11,1... | collective-permute-start | bytes 983048 | tf_op jit(solution)/shard_map/ppermute | solution.py:17
  264.4 7.2 %collective-permute-start.8 = (f32[2,80,128]{2,1,0:T(8,128)S(1)}, f32[2,80,128]{2,1,0:T(8,128)S(1)}, u32[]{:S(2)}, u32[]{:S(2)}) collective-permute-start(f32[2,80,128]{2,1,0:T(8,128)S(1)} %convolution_bitcast_fusion.9), channel_id=1, source_target_pairs={{0,4},{4,8},{8,12},{12,16},{16,20},{20,24},{24,28},{1,5},{5,9},{9,... | collective-permute-start | bytes 245768 | tf_op jit(solution)/shard_map/ppermute | solution.py:23
  (1 other events, 0.7 us)
where the time goes:
time: 323 us; the launch traced here: 322 us
  blocking collectives  220 us (68%)
  matrix products  56.6 us (18%)
  between operations  17.8 us (6%)
  starting transfers between devices  13.1 us (4%)
  waiting for transfers between devices  7.91 us (2%)
  local copies, waits for them, and re-layouts  3.85 us (1%)
    all_gather x6, blocking collectives, prefix(): gathered = jax.tree.map(lambda a: lax.all_gather(a, axis), part)  220 us
    dot_general x14, matrix products, compose(): jnp.dot(second_map, first_shift, precision=HIGH) + second_shift  17.2 us
    dot_general x24, matrix products, column_sweep(): product = jnp.dot(coupling_block, neighbour_block, precision=HIGH)  14.7 us
    dot_general x15, matrix products, apply_trace(): return jnp.einsum('tb,ebr->etr', operator, values, precision=HIGH)  9.17 us
    ppermute x6, waiting for transfers between devices, passed_along(): return lax.ppermute(block, axis, route)  7.9 us
    ppermute x3, starting transfers between devices, passed_along_2(): return lax.ppermute(block, axis, route)  7.68 us
    dot_general x4, matrix products, half_sweep(): jnp.einsum('ebs,sr->ebr', response_field, inflow, precision=HIGH)  7.01 us
  transfers between devices with their start and end apart: 9, of which 4 were waited for; matrix products, arithmetic and copies ran while one was open for 6% of the time, Pallas kernels for 0%

commit v1 on v0

v1 whole, which is shorter than its diff:
```python
from functools import partial

import jax
import jax.numpy as jnp
from jax import lax
from jax.experimental import pallas as pl
from jax.experimental.pallas import tpu as pltpu
from jax.sharding import PartitionSpec as P

SWEEPS = 2
LANES = 128
F32 = jnp.float32
BF16 = jnp.bfloat16


def mm(a, b):
    return jnp.dot(a, b, preferred_element_type=F32)


def two(x):
    high = x.astype(BF16)
    low = (x - high.astype(F32)).astype(BF16)
    return high, low


def exact_times(operator, x):
    n = x.shape[1]
    both = mm(operator, jnp.concatenate(two(x), axis=1))
    return both[:, :n] + both[:, n:]


def map_times(high, low, x):
    n = x.shape[1]
    x_high, x_low = two(x)
    both = mm(high, jnp.concatenate([x_high, x_low], axis=1))
    return both[:, :n] + both[:, n:] + mm(low, x_high)


def spread(x, slots, width):
    gap = jnp.zeros((LANES - width, x.shape[1]), x.dtype)
    parts = []
    for s in range(slots):
        parts += [x[s * width : (s + 1) * width], gap]
    return jnp.concatenate(parts, axis=0)


def call(body, outs, ins, scalars=0, scratch=(), flops=0):
    vmem, smem = pl.BlockSpec(memory_space=pltpu.VMEM), pl.BlockSpec(memory_space=pltpu.SMEM)
    moved = sum(x.size * x.dtype.itemsize for x in ins)
    moved += sum(o.size * o.dtype.itemsize for o in outs)
    return pl.pallas_call(
        body,
        out_shape=list(outs),
        in_specs=[smem] * scalars + [vmem] * (len(ins) - scalars),
        out_specs=[vmem] * len(outs),
        scratch_shapes=list(scratch),
        compiler_params=pltpu.CompilerParams(vmem_limit_bytes=24 * 2**20),
        cost_estimate=pl.CostEstimate(flops=flops, bytes_accessed=moved, transcendentals=0),
    )(*ins)


def shape(*dims, dtype=F32):
    return jax.ShapeDtypeStruct(dims, dtype)


def neighbour_sum(slot, links, types, table, read, slots):
    total = None
    for m in range(links.shape[1]):
        n = links[slot, m]
        product = exact_times(table[types[slot, m]], read(jnp.minimum(n, slots - 1)))
        product = jnp.where(n < slots, product, 0.0)
        total = product if total is None else total + product
    return total


def sweep_line(x, residual, inverse, order, count, links, types, table, backward, fresh):
    slots = x.shape[0]
    for step, q in enumerate(reversed(range(slots)) if backward else range(slots)):
        s = order[q]
        rest = residual[s]
        if not (fresh and step == 0):
            rest = rest - neighbour_sum(s, links, types, table, lambda n: x[n], slots)
        x[s] = exact_times(inverse[s], rest) * (q < count).astype(F32)


def line_response(out, lift, inverse, order, count, links, types, table, backward):
    slots = out.shape[0]
    out[...] = jnp.zeros_like(out)
    done = []
    for q in reversed(range(slots)) if backward else range(slots):
        s = order[q]
        live = (q < count).astype(F32)
        out[s, q] = mm(inverse[s], lift) * -live
        if done:
            read = lambda n: jnp.concatenate([out[n, p] for p in done], axis=1)
            rest = neighbour_sum(s, links, types, table, read, slots)
            rest = exact_times(inverse[s], rest) * -live
            for i, p in enumerate(done):
                out[s, p] = rest[:, i * LANES : (i + 1) * LANES]
        done.append(q)


def padded_lift(lift_ref, index, pad):
    pad[...] = jnp.zeros_like(pad)
    pad[:, : lift_ref.shape[2]] = lift_ref[index].astype(F32)
    return pad[...].astype(BF16)


def store_map(out, base, response, trace, order):
    slots, width = response.shape[0], trace.shape[0]
    for p in range(slots):
        f = order[p]
        for s in range(slots):
            row = pl.multiple_of(base + (f * slots + s) * width, 8)
            out[pl.ds(row, width), :] = exact_times(trace, response[s, p])


def first_kernel(order, count, links, types, rhs, inverse, table, traces, lifts,
                 packed, x, response, pad):
    slots, width = x.shape[0], traces.shape[1]
    live = count[0]
    x[...] = jnp.zeros_like(x)
    sweep_line(x, rhs, inverse, order, live, links, types, table, False, True)
    for s in range(slots):
        packed[s * width : (s + 1) * width, :] = exact_times(traces[1], x[s])
    lift = padded_lift(lifts, 0, pad)
    line_response(response, lift, inverse, order, live, links, types, table, False)
    store_map(packed, slots * width, response, traces[1], order)


def side_traces(out, traces, x):
    slots, width = x.shape[0], traces.shape[1]
    for s in range(slots):
        for face in (2, 3):
            out[face - 2, s * width : (s + 1) * width, :] = exact_times(traces[face], x[s])


def side_map(high, low, response, traces, order):
    slots, width = response.shape[0], traces.shape[1]
    for p in range(slots):
        f = order[p]
        for face in (2, 3):
            for s in range(slots):
                a, b = two(exact_times(traces[face], response[s, p]))
                row = ((face - 2) * slots + s) * width
                high[f, row : row + width, :] = a
                low[f, row : row + width, :] = b


def maps_kernel(order, count, links, types, inverse, table, traces, lifts, response, x,
                side_f_high, side_f_low, side_b_high, side_b_low, back_map, side, back, pad):
    live = count[0]
    side_traces(side, traces, x)
    side_map(side_f_high, side_f_low, response, traces, order)
    lift = padded_lift(lifts, 1, pad)
    line_response(back, lift, inverse, order, live, links, types, table, True)
    store_map(back_map, 0, back, traces[0], order)
    side_map(side_b_high, side_b_low, back, traces, order)


def local_kernel(backward, involution, order, count, links, types, rhs, old, inverse, table,
                 traces, lifts, first, second, outflow, side, residual, x):
    slots, width = x.shape[0], traces.shape[1]
    odd = lax.rem(lax.axis_index("span"), 2) if involution else 1
    x[...] = old[...]
    for s in range(slots):
        rows = slice(s * width, (s + 1) * width)
        residual[s] = (
            rhs[s]
            - exact_times(lifts[3 - odd], first[rows, :])
            - exact_times(lifts[2 + odd], second[rows, :])
        )
    sweep_line(x, residual, inverse, order, count[0], links, types, table, backward, False)
    out_trace = traces[0 if backward else 1]
    for s in range(slots):
        outflow[s * width : (s + 1) * width, :] = exact_times(out_trace, x[s])
    side_traces(side, traces, x)


def finish_kernel(backward, order, count, links, types, rhs, residual, old, inflow, inverse,
                  table, lifts, x, rhs_next, rest):
    slots, width = x.shape[0], lifts.shape[2]
    lift = lifts[1 if backward else 0]
    x[...] = old[...]
    for s in range(slots):
        entered = exact_times(lift, inflow[s * width : (s + 1) * width, :])
        rest[s] = residual[s] - entered
        if rhs_next is not None:
            rhs_next[s] = rhs[s] - entered
    sweep_line(x, rest, inverse, order, count[0], links, types, table, backward, False)


def digit_of(size, stride, backward):
    digit = lax.rem(lax.div(lax.axis_index("stream"), stride), size)
    return digit


def source_digit(digit, size, k):
    if size & (size - 1) == 0:
        return digit ^ k
    return lax.rem(digit - k + size, size)


def fold_kernel(size, stride, backward, first, slots, *refs):
    parts, refs = refs[:size], refs[size:]
    if first:
        total, before, high, low, held = refs
    else:
        high, low, total, before, held = refs
    rows = total.shape[0]
    width = rows // slots
    digit = digit_of(size, stride, backward)
    place = size - 1 - digit if backward else digit
    for k, part in enumerate(parts):
        m = source_digit(digit, size, k)
        m = size - 1 - m if backward else m
        held[m] = part[:rows, :]
        if first:
            for f in range(slots):
                base = rows * (1 + f)
                a, b = two(part[base : base + rows, :])
                high[m, f] = a
                low[m, f] = b
    state = held[0]
    below = jnp.zeros_like(state)
    for m in range(1, size):
        below = jnp.where(place == m, state, below)
        state = held[m] + wide_times(high, low, m, state, slots, width)
    total[...] = state
    before[...] = below


def wide(ref, m, slots):
    return jnp.concatenate([ref[m, f] for f in range(slots)], axis=1)


def wide_times(high, low, m, x, slots, width):
    return map_times(wide(high, m, slots), wide(low, m, slots), spread(x, slots, width))


def passage_kernel(size, stride, backward, slots, high, low, pass_high, pass_low, whole):
    rows = high.shape[2]
    width = rows // slots
    digit = digit_of(size, stride, backward)
    place = size - 1 - digit if backward else digit
    row = lax.broadcasted_iota(jnp.int32, (rows, slots * LANES), 0)
    lane = lax.broadcasted_iota(jnp.int32, (rows, slots * LANES), 1)
    state = jnp.zeros((rows, slots * LANES), F32)
    for s in range(slots):
        hit = (row - s * width == lane - s * LANES) & (row >= s * width) & (row < (s + 1) * width)
        state = jnp.where(hit, 1.0, state)
    kept = state
    for m in range(size):
        kept = jnp.where(place == m, state, kept)
        if m < size - 1 or whole is not None:
            state = wide_times(high, low, m, state, slots, width)
    a, b = two(kept)
    for f in range(slots):
        pass_high[0, f] = a[:, f * LANES : (f + 1) * LANES]
        pass_low[0, f] = b[:, f * LANES : (f + 1) * LANES]
        if whole is not None:
            whole[f * rows : (f + 1) * rows, :] = state[:, f * LANES : (f + 1) * LANES]


def enter_kernel(depth, last_stride, backward, involution, slots, *refs):
    befores, refs = refs[:depth], refs[depth:]
    passes, refs = refs[: 2 * depth], refs[2 * depth :]
    arrived, side, high, low, inflow, first, second = refs
    rows = inflow.shape[0]
    width = rows // slots
    if last_stride:
        upper = digit_of(2, last_stride, backward) == (0 if backward else 1)
        state = jnp.where(upper, arrived[:rows, :], 0.0)
    else:
        state = jnp.zeros((rows, inflow.shape[1]), F32)
    for level in reversed(range(depth)):
        state = befores[level][...] + wide_times(
            passes[2 * level], passes[2 * level + 1], 0, state, slots, width
        )
    inflow[...] = state
    if first is None:
        return
    hidden = spread(state, slots, width)
    both = map_times(
        jnp.concatenate([high[f] for f in range(slots)], axis=1),
        jnp.concatenate([low[f] for f in range(slots)], axis=1),
        hidden,
    )
    lower_face = side[0] + both[:rows]
    upper_face = side[1] + both[rows:]
    if involution:
        odd = lax.rem(lax.axis_index("span"), 2) == 1
        first[...] = jnp.where(odd, lower_face, upper_face)
        second[...] = jnp.where(odd, upper_face, lower_face)
    else:
        first[...] = upper_face
        second[...] = lower_face


def levels_of(count):
    sizes, left = [], count
    for factor in (4, 2):
        while left % factor == 0:
            sizes.append(factor)
            left //= factor
    factor = 3
    while left > 1:
        while left % factor == 0:
            sizes.insert(0, factor)
            left //= factor
        factor += 2
    strides, stride = [], 1
    for size in sizes:
        strides.append(stride)
        stride *= size
    return list(zip(sizes, strides))


def exchange(block, axis, size, stride, k):
    pairs = []
    for i in range(lax.axis_size(axis)):
        digit = (i // stride) % size
        target = digit ^ k if size & (size - 1) == 0 else (digit + k) % size
        pairs.append((i, i + (target - digit) * stride))
    return lax.ppermute(block, axis, pairs)


def side_exchange(first, second, involution):
    n = lax.axis_size("span")
    if involution:
        pairs = [(j, j ^ 1) for j in range(n)]
        across = [(j, (j + 1) % n if j % 2 else (j - 1) % n) for j in range(n)]
        second = lax.ppermute(second, "span", across)
        first = lax.ppermute(first, "span", pairs)
        return first, second
    return (
        lax.ppermute(first, "span", [(j, (j + 1) % n) for j in range(n)]),
        lax.ppermute(second, "span", [(j, (j - 1) % n) for j in range(n)]),
    )


def optional(body, at):
    def run(*refs):
        return body(*refs[:at], None, *refs[at:])

    return run


def local(rhs, inv_blocks, coupling, trace_ops, lift_ops, order, counts, neighbours, face_ids):
    source, inverse = rhs[0, 0], inv_blocks[0, 0]
    scalars = (order[0, 0], counts[0], neighbours[0, 0], face_ids[0, 0])
    slots, block, columns = source.shape
    width = trace_ops.shape[1]
    rows = slots * width
    levels = levels_of(lax.axis_size("stream"))
    span = lax.axis_size("span")
    involution = span % 2 == 0 and span > 2

    field = shape(slots, block, columns)
    trace = shape(rows, columns)
    sweep_flops = 2 * slots * 3 * 2 * block * block * columns
    map_shape = shape(rows * slots, LANES)
    side_shape = shape(slots, 2 * rows, LANES, dtype=BF16)
    pad = pltpu.VMEM((block, LANES), F32)

    packed, x_local, response = call(
        first_kernel,
        [shape(rows * (1 + slots), LANES), field, shape(slots, slots, block, LANES)],
        (*scalars, source, inverse, coupling, trace_ops, lift_ops),
        4, [pad], 3 * sweep_flops,
    )
    store = {}

    def maps():
        out = call(
            maps_kernel,
            [side_shape] * 4 + [map_shape, shape(2, rows, columns)],
            (*scalars, inverse, coupling, trace_ops, lift_ops, response, x_local),
            4, [pltpu.VMEM((slots, slots, block, LANES), F32), pad], 6 * sweep_flops,
        )
        store["side", False], store["side", True] = out[0:2], out[2:4]
        store["map"], store["first side"] = out[4], out[5]

    def carried(outflow, backward, whole):
        befores, passes, arrived = [], [], None
        total = outflow
        last_stride = 0
        for level, (size, stride) in enumerate(levels):
            last = level == len(levels) - 1
            if last and size == 2:
                arrived, last_stride = exchange(total, "stream", size, stride, 1), stride
                break
            key = ("fold", backward, level)
            first = key not in store
            if first:
                total = jnp.concatenate([total, whole], axis=0) if level else packed_of(total, whole)
            parts = [total] + [exchange(total, "stream", size, stride, k) for k in range(1, size)]
            held = pltpu.VMEM((size, rows, columns), F32)
            kinds = [shape(size, slots, rows, LANES, dtype=BF16)] * 2
            body = partial(fold_kernel, size, stride, backward, first, slots)
            if first:
                total, before, high, low = call(body, [trace, trace] + kinds, parts, 0, [held], 10**8)
                store[key] = (high, low)
                outs = [shape(1, slots, rows, LANES, dtype=BF16)] * 2
                body = partial(passage_kernel, size, stride, backward, slots)
                if last or (level == len(levels) - 2 and levels[-1][0] == 2):
                    store["pass", backward, level] = call(optional(body, 4), outs, (high, low), 0, (), 10**8)
                else:
                    *passed, whole = call(body, outs + [map_shape], (high, low), 0, (), 10**8)
                    store["pass", backward, level] = passed
            else:
                total, before = call(body, [trace, trace], (*parts, *store[key]), 0, [held], 10**8)
            befores.append(before)
            passes += store["pass", backward, level]
        if arrived is None:
            arrived = total
        return befores, passes, arrived, last_stride

    def packed_of(outflow, whole):
        return outflow if whole is None else jnp.concatenate([outflow, whole], axis=0)

    x = None
    rhs_now = source
    halves = [backward for _ in range(SWEEPS) for backward in (False, True)]
    for number, backward in enumerate(halves):
        final = number == len(halves) - 1
        if number == 0:
            residual, x_old = source, jnp.zeros_like(source)
            befores, passes, arrived, last_stride = carried(packed, backward, None)
            maps()
            side = store["first side"]
        else:
            x_old = x
            outflow, side, residual = call(
                partial(local_kernel, backward, involution),
                [trace, shape(2, rows, columns), field],
                (*scalars, rhs_now, x_old, inverse, coupling, trace_ops, lift_ops, first, second),
                4, [pltpu.VMEM(source.shape, F32)], 2 * sweep_flops,
            )
            befores, passes, arrived, last_stride = carried(outflow, backward, store["map"])
        depth = len(befores)
        body = partial(enter_kernel, depth, last_stride, backward, involution, slots)
        ins = (*befores, *passes, arrived, side, *store["side", backward])
        if final:
            def alone(*refs):
                return body(*refs, None, None)
            (inflow,) = call(alone, [trace], ins, 0, (), 10**8)
        else:
            inflow, first, second = call(body, [trace] * 3, ins, 0, (), 10**8)
            first, second = side_exchange(first, second, involution)
        body = partial(finish_kernel, backward)
        ins = (*scalars, source, residual, x_old, inflow, inverse, coupling, lift_ops)
        scratch = [pltpu.VMEM(source.shape, F32)]
        if final:
            (x,) = call(optional(body, len(ins) + 1), [field], ins, 4, scratch, 2 * sweep_flops)
        else:
            x, rhs_now = call(body, [field, field], ins, 4, scratch, 2 * sweep_flops)
    return x[None, None]


def solution(mesh):
    placed = (
        P("stream", "span", None, None, None),
        P("stream", "span", None, None, None),
        P(),
        P(),
        P(),
        P("stream", "span", None),
        P("stream", "span"),
        P("stream", "span", None, None),
        P("stream", "span", None, None),
    )
    return jax.shard_map(
        local,
        mesh=mesh,
        in_specs=placed,
        out_specs=P("stream", "span", None, None, None),
        check_vma=False,
    )
```

time: 323 us -> 110 us (0.34)
  blocking collectives: 220 us -> 0 us
  matrix products: 56.6 us -> 0 us
  waiting for transfers between devices: 7.91 us -> 48.1 us
  Pallas kernels: 0 us -> 25.9 us
  between operations: 17.8 us -> 0.92 us
  starting transfers between devices: 13.1 us -> 27.4 us
  local copies, waits for them, and re-layouts: 3.85 us -> 7.56 us
    all_gather x6 -> x0, blocking collectives: 220 us -> none  [prefix(): gathered = jax.tree.map(lambda a: lax.all_gather(a, axis), part)]
    dot_general x78 -> x0, matrix products: 56.6 us -> none  [the longest x14 17.2 us: compose(): jnp.dot(second_map, first_shift, precision=HIGH) + second_shift]
    ppermute x9 -> x22, waiting for transfers between devices: 7.91 us -> 48.1 us  [the longest x16 46 us: exchange(): return lax.ppermute(block, axis, pairs)]
    pallas_call x0 -> x19, Pallas kernels: none -> 25.9 us  [call(): pl.pallas_call(body, out_shape=list(outs), in_specs=[smem] * scalars + [v...]
    ppermute x9 -> x22, starting transfers between devices: 13.1 us -> 27.4 us  [the longest x16 22.2 us: exchange(): return lax.ppermute(block, axis, pairs)]
    unnamed x32 -> x30, local copies, waits for them, and re-layouts: 0.8 us -> 7.52 us
  transfers between devices with their start and end apart: 9 -> 22, of which waited for: 4 -> 17; matrix products, arithmetic and copies ran while one was open for 6% -> 0% of each run, Pallas kernels for 0% -> 9%
where the time goes in v1:
time: 110 us
  waiting for transfers between devices  48.1 us (44%)
  starting transfers between devices  27.4 us (25%)
  Pallas kernels  25.9 us (24%)
  local copies, waits for them, and re-layouts  7.56 us (7%)
    ppermute x16, waiting for transfers between devices, exchange(): return lax.ppermute(block, axis, pairs)  46 us
    pallas_call x19, Pallas kernels, call(): pl.pallas_call(body, out_shape=list(outs), in_specs=[smem] * scalars + [v...  25.9 us
    ppermute x16, starting transfers between devices, exchange(): return lax.ppermute(block, axis, pairs)  22.2 us
    unnamed x30, local copies, waits for them, and re-layouts  7.52 us
    ppermute x3, starting transfers between devices, side_exchange(): second = lax.ppermute(second, 'span', across)  4.92 us
  transfers between devices with their start and end apart: 22, of which 17 were waited for; matrix products, arithmetic and copies ran while one was open for 0% of the time, Pallas kernels for 9%

profile of v1, /device:TPU:0, one launch (start us, length us, event | category | flops | bytes accessed | tf_op | source)
XLA Modules:
  0.0 109.8 jit_solution(16650337874845520774)
XLA Ops:
  8.2 2.8 %shard_map.91 = (f32[480,128]{1,0:T(8,128)S(1)}, f32[2,320,128]{2,1,0:T(8,128)S(1)}, f32[2,2,320,128]{3,2,1,0:T(8,128)S(1)}) custom-call(s32[2]{0:T(128)S(1)} %bitcast.49, s32[1]{0:T(128)} %bitcast.7.count, s32[2,2]{1,0:T(2,128)S(1)} %bitcast.31, s32[2,2]{1,0:T(2,128)S(1)} %bitcast.40, f32[2,320,128]{2,1,0:T(8,128)S(1)} %bitcast.25, ...), custom_call_target="tpu_custom_call" | custom-call | flops 943718400 | bytes 3604524 | tf_op jit(solution)/shard_map/pallas_call | solution.py:51
  11.0 4.0 %collective-permute-start.2 = (f32[480,128]{1,0:T(8,128)S(1)}, f32[480,128]{1,0:T(8,128)S(1)}, u32[]{:S(2)}, u32[]{:S(2)}) collective-permute-start(f32[480,128]{1,0:T(8,128)S(1)} %get-tuple-element.54.refs_0_), channel_id=1, source_target_pairs={{0,12},{4,8},{8,4},{12,0},{16,28},{20,24},{24,20},{28,16},{1,13},{... | collective-permute-start | bytes 737288 | tf_op jit(solution)/shard_map/ppermute | solution.py:325
  15.7 6.2 %collective-permute-done.2.refs_3_ = f32[480,128]{1,0:T(8,128)S(1)} collective-permute-done((f32[480,128]{1,0:T(8,128)S(1)}, f32[480,128]{1,0:T(8,128)S(1)}, u32[]{:S(2)}, u32[]{:S(2)}) %collective-permute-start.2) | collective-permute-done | bytes 245792 | tf_op jit(solution)/shard_map/ppermute | solution.py:325
  21.9 4.6 %collective-permute-done.1.refs_2_ = f32[480,128]{1,0:T(8,128)S(1)} collective-permute-done((f32[480,128]{1,0:T(8,128)S(1)}, f32[480,128]{1,0:T(8,128)S(1)}, u32[]{:S(2)}, u32[]{:S(2)}) %collective-permute-start.1) | collective-permute-done | bytes 245792 | tf_op jit(solution)/shard_map/ppermute | solution.py:325
  27.1 2.7 %collective-permute-start.3 = (f32[160,128]{1,0:T(8,128)S(1)}, f32[160,128]{1,0:T(8,128)S(1)}, u32[]{:S(2)}, u32[]{:S(2)}) collective-permute-start(f32[160,128]{1,0:T(8,128)S(1)} %get-tuple-element.60), channel_id=1, source_target_pairs={{0,16},{4,20},{8,24},{12,28},{16,0},{20,4},{24,8},{28,12},{1,17},{... | collective-permute-start | bytes 245768 | tf_op jit(solution)/shard_map/ppermute | solution.py:325
  29.8 2.5 %shard_map.94 = (bf16[2,320,128]{2,1,0:T(8,128)(2,1)S(1)}, bf16[2,320,128]{2,1,0:T(8,128)(2,1)S(1)}, bf16[2,320,128]{2,1,0:T(8,128)(2,1)S(1)}, bf16[2,320,128]{2...) custom-call(s32[2]{0:T(128)S(1)} %bitcast.50, s32[1]{0:T(128)} %bitcast.8.count, ...), custom_call_target="tpu_custom_call" | custom-call | flops 1887436800 | bytes 4014124 | tf_op jit(solution)/shard_map/pallas_call | solution.py:51
  34.8 1.6 %collective-permute-start.5 = (f32[160,128]{1,0:T(8,128)S(1)}, f32[160,128]{1,0:T(8,128)S(1)}, u32[]{:S(2)}, u32[]{:S(2)}) collective-permute-start(f32[160,128]{1,0:T(8,128)S(1)} %get-tuple-element.70), channel_id=1, source_target_pairs={{0,3},{1,2},{2,1},{3,0},{4,7},{5,6},{6,5},{7,4},{8,11},{9,10},{10,... | collective-permute-start | bytes 245768 | tf_op jit(solution)/shard_map/ppermute | solution.py:333
  36.5 1.9 %shard_map.96 = (f32[2,320,128]{2,1,0:T(8,128)S(1)}, f32[2,320,128]{2,1,0:T(8,128)S(1)}) custom-call(s32[2]{0:T(128)S(1)} %bitcast.51, s32[1]{0:T(128)} %bitcast.9.count, s32[2,2]{1,0:T(2,128)S(1)} %bitcast.33, s32[2,2]{1,0:T(2,128)S(1)} %bitcast.42, f32[2,320,128]{2,1,0:T(8,128)S(1)} %bitcast.26, f32[2,320,128]{2,1,0:T(8,128)S(1)} %bitcast.27, ...), custom_call_target="tpu_custom_call" | custom-call | flops 629145600 | bytes 3563564 | tf_op jit(solution)/shard_map/pallas_call | solution.py:51
  39.0 2.3 %shard_map.97 = (f32[160,128]{1,0:T(8,128)S(1)}, f32[2,160,128]{2,1,0:T(8,128)S(1)}, f32[2,320,128]{2,1,0:T(8,128)S(1)}) custom-call(s32[2]{0:T(128)S(1)} %bitcast.52, s32[1]{0:T(128)} %bitcast.10.count, s32[2,2]{1,0:T(2,128)S(1)} %bitcast.34, s32[2,2]{1,0:T(2,128)S(1)} %bitcast.43, f32[2,320,128]{2,1,0:T(8,128)S(1)} %get-tuple-element.67.rhs, ...), custom_call_target="tpu_custom_call" | custom-call | flops 629145600 | bytes 3440684 | tf_op jit(solution)/shard_map/pallas_call | solution.py:51
  44.9 6.2 %collective-permute-done.8.refs_3_ = f32[480,128]{1,0:T(8,128)S(1)} collective-permute-done((f32[480,128]{1,0:T(8,128)S(1)}, f32[480,128]{1,0:T(8,128)S(1)}, u32[]{:S(2)}, u32[]{:S(2)}) %collective-permute-start.8) | collective-permute-done | bytes 245792 | tf_op jit(solution)/shard_map/ppermute | solution.py:325
  51.2 4.7 %collective-permute-done.7.refs_2_ = f32[480,128]{1,0:T(8,128)S(1)} collective-permute-done((f32[480,128]{1,0:T(8,128)S(1)}, f32[480,128]{1,0:T(8,128)S(1)}, u32[]{:S(2)}, u32[]{:S(2)}) %collective-permute-start.7) | collective-permute-done | bytes 245792 | tf_op jit(solution)/shard_map/ppermute | solution.py:325
  56.5 2.3 %collective-permute-start.9 = (f32[160,128]{1,0:T(8,128)S(1)}, f32[160,128]{1,0:T(8,128)S(1)}, u32[]{:S(2)}, u32[]{:S(2)}) collective-permute-start(f32[160,128]{1,0:T(8,128)S(1)} %get-tuple-element.79), channel_id=1, source_target_pairs={{0,16},{4,20},{8,24},{12,28},{16,0},{20,4},{24,8},{28,12},{1,17},{... | collective-permute-start | bytes 245768 | tf_op jit(solution)/shard_map/ppermute | solution.py:325
  59.5 4.1 %collective-permute-done.9.refs_3_ = f32[160,128]{1,0:T(8,128)S(1)} collective-permute-done((f32[160,128]{1,0:T(8,128)S(1)}, f32[160,128]{1,0:T(8,128)S(1)}, u32[]{:S(2)}, u32[]{:S(2)}) %collective-permute-start.9) | collective-permute-done | bytes 81952 | tf_op jit(solution)/shard_map/ppermute | solution.py:325
  65.8 1.8 %shard_map.101 = (f32[2,320,128]{2,1,0:T(8,128)S(1)}, f32[2,320,128]{2,1,0:T(8,128)S(1)}) custom-call(s32[2]{0:T(128)S(1)} %bitcast.53, s32[1]{0:T(128)} %bitcast.11.count, s32[2,2]{1,0:T(2,128)S(1)} %bitcast.35, s32[2,2]{1,0:T(2,128)S(1)} %bitcast.44, f32[2,320,128]{2,1,0:T(8,128)S(1)} %bitcast.28, f32[2,320,128]{2,1,0:T(8,128)S(1)} %get-tuple-element.71.residual, ...), custom_call_target="tpu_custom_call" | custom-call | flops 629145600 | bytes 3563564 | tf_op jit(solution)/shard_map/pallas_call | solution.py:51
  68.4 2.3 %shard_map.102 = (f32[160,128]{1,0:T(8,128)S(1)}, f32[2,160,128]{2,1,0:T(8,128)S(1)}, f32[2,320,128]{2,1,0:T(8,128)S(1)}) custom-call(s32[2]{0:T(128)S(1)} %bitcast.54, s32[1]{0:T(128)} %bitcast.12.count, s32[2,2]{1,0:T(2,128)S(1)} %bitcast.36, s32[2,2]{1,0:T(2,128)S(1)} %bitcast.45, f32[2,320,128]{2,1,0:T(8,128)S(1)} %get-tuple-element.84.rhs, ...), custom_call_target="tpu_custom_call" | custom-call | flops 629145600 | bytes 3440684 | tf_op jit(solution)/shard_map/pallas_call | solution.py:51
  71.3 2.4 %collective-permute-start.13 = (f32[160,128]{1,0:T(8,128)S(1)}, f32[160,128]{1,0:T(8,128)S(1)}, u32[]{:S(2)}, u32[]{:S(2)}) collective-permute-start(f32[160,128]{1,0:T(8,128)S(1)} %get-tuple-element.89.refs_0_), channel_id=1, source_target_pairs={{0,8},{4,12},{8,0},{12,4},{16,24},{20,28},{24,16},{28,20},{1,9},{5... | collective-permute-start | bytes 245768 | tf_op jit(solution)/shard_map/ppermute | solution.py:325
  74.2 2.7 %collective-permute-done.14.refs_3_ = f32[160,128]{1,0:T(8,128)S(1)} collective-permute-done((f32[160,128]{1,0:T(8,128)S(1)}, f32[160,128]{1,0:T(8,128)S(1)}, u32[]{:S(2)}, u32[]{:S(2)}) %collective-permute-start.14) | collective-permute-done | bytes 81952 | tf_op jit(solution)/shard_map/ppermute | solution.py:325
  80.0 5.4 %collective-permute-done.15.refs_3_ = f32[160,128]{1,0:T(8,128)S(1)} collective-permute-done((f32[160,128]{1,0:T(8,128)S(1)}, f32[160,128]{1,0:T(8,128)S(1)}, u32[]{:S(2)}, u32[]{:S(2)}) %collective-permute-start.15) | collective-permute-done | bytes 81952 | tf_op jit(solution)/shard_map/ppermute | solution.py:325
  87.5 1.8 %shard_map.105 = (f32[2,320,128]{2,1,0:T(8,128)S(1)}, f32[2,320,128]{2,1,0:T(8,128)S(1)}) custom-call(s32[2]{0:T(128)S(1)} %bitcast.55, s32[1]{0:T(128)} %bitcast.13.count, s32[2,2]{1,0:T(2,128)S(1)} %bitcast.37, s32[2,2]{1,0:T(2,128)S(1)} %bitcast.46, f32[2,320,128]{2,1,0:T(8,128)S(1)} %bitcast.29, f32[2,320,128]{2,1,0:T(8,128)S(1)} %get-tuple-element.88.residual, ...), custom_call_target="tpu_custom_call" | custom-call | flops 629145600 | bytes 3563564 | tf_op jit(solution)/shard_map/pallas_call | solution.py:51
  90.1 2.3 %shard_map.106 = (f32[160,128]{1,0:T(8,128)S(1)}, f32[2,160,128]{2,1,0:T(8,128)S(1)}, f32[2,320,128]{2,1,0:T(8,128)S(1)}) custom-call(s32[2]{0:T(128)S(1)} %bitcast.56, s32[1]{0:T(128)} %bitcast.14.count, s32[2,2]{1,0:T(2,128)S(1)} %bitcast.38, s32[2,2]{1,0:T(2,128)S(1)} %bitcast.47, f32[2,320,128]{2,1,0:T(8,128)S(1)} %get-tuple-element.94.rhs, ...), custom_call_target="tpu_custom_call" | custom-call | flops 629145600 | bytes 3440684 | tf_op jit(solution)/shard_map/pallas_call | solution.py:51
  92.5 2.5 %collective-permute-start.19 = (f32[160,128]{1,0:T(8,128)S(1)}, f32[160,128]{1,0:T(8,128)S(1)}, u32[]{:S(2)}, u32[]{:S(2)}) collective-permute-start(f32[160,128]{1,0:T(8,128)S(1)} %get-tuple-element.99.refs_0_), channel_id=1, source_target_pairs={{0,8},{4,12},{8,0},{12,4},{16,24},{20,28},{24,16},{28,20},{1,9},{5... | collective-permute-start | bytes 245768 | tf_op jit(solution)/shard_map/ppermute | solution.py:325
  96.0 2.7 %collective-permute-done.20.refs_3_ = f32[160,128]{1,0:T(8,128)S(1)} collective-permute-done((f32[160,128]{1,0:T(8,128)S(1)}, f32[160,128]{1,0:T(8,128)S(1)}, u32[]{:S(2)}, u32[]{:S(2)}) %collective-permute-start.20) | collective-permute-done | bytes 81952 | tf_op jit(solution)/shard_map/ppermute | solution.py:325
  101.3 5.7 %collective-permute-done.21.refs_3_ = f32[160,128]{1,0:T(8,128)S(1)} collective-permute-done((f32[160,128]{1,0:T(8,128)S(1)}, f32[160,128]{1,0:T(8,128)S(1)}, u32[]{:S(2)}, u32[]{:S(2)}) %collective-permute-start.21) | collective-permute-done | bytes 81952 | tf_op jit(solution)/shard_map/ppermute | solution.py:325
  107.2 2.6 %shard_map.109 = f32[2,320,128]{2,1,0:T(8,128)} custom-call(s32[2]{0:T(128)S(1)} %bitcast.57, s32[1]{0:T(128)} %bitcast.15.refs_1_, s32[2,2]{1,0:T(2,128)S(1)} %bitcast.39, s32[2,2]{1,0:T(2,128)S(1)} %bitcast.48, f32[2,320,128]{2,1,0:T(8,128)S(1)} %bitcast.30, f32[2,320,128]{2,1,0:T(8,128)S(1)} %get-tuple-element.98.refs_5_, ...), custom_call_target="tpu_custom_call" | custom-call | flops 629145600 | bytes 3235884 | tf_op jit(solution)/shard_map/pallas_call | solution.py:51
  (71 shorter events, 30.9 us)
Async XLA Ops:
  8.2 21.6 %copy-start.11 = (s32[1,1,2,2]{3,2,1,0:T(2,128)S(1)}, s32[1,1,2,2]{3,2,1,0:T(2,128)}, u32[]{:S(2)}) copy-start(s32[1,1,2,2]{3,2,1,0:T(2,128)} %param.17) | copy-start | bytes 52
  8.2 21.6 %copy-start.13 = (s32[1,1,2]{2,1,0:T(1,128)S(1)}, s32[1,1,2]{2,1,0:T(1,128)}, u32[]{:S(2)}) copy-start(s32[1,1,2]{2,1,0:T(1,128)} %param.14) | copy-start | bytes 28
  11.0 10.8 %collective-permute-start.2 = (f32[480,128]{1,0:T(8,128)S(1)}, f32[480,128]{1,0:T(8,128)S(1)}, u32[]{:S(2)}, u32[]{:S(2)}) collective-permute-start(f32[480,128]{1,0:T(8,128)S(1)} %get-tuple-element.54.refs_0_), channel_id=1, source_target_pairs={{0,12},{4,8},{8,4},{12,0},{16,28},{20,24},{24,20},{28,16},{1,13},{... | collective-permute-start | bytes 737288 | tf_op jit(solution)/shard_map/ppermute | solution.py:325
  15.0 11.4 %collective-permute-start.1 = (f32[480,128]{1,0:T(8,128)S(1)}, f32[480,128]{1,0:T(8,128)S(1)}, u32[]{:S(2)}, u32[]{:S(2)}) collective-permute-start(f32[480,128]{1,0:T(8,128)S(1)} %get-tuple-element.54.refs_0_), channel_id=1, source_target_pairs={{0,8},{4,12},{8,0},{12,4},{16,24},{20,28},{24,16},{28,20},{1,9},{5... | collective-permute-start | bytes 737288 | tf_op jit(solution)/shard_map/ppermute | solution.py:325
  15.5 11.0 %collective-permute-start = (f32[480,128]{1,0:T(8,128)S(1)}, f32[480,128]{1,0:T(8,128)S(1)}, u32[]{:S(2)}, u32[]{:S(2)}) collective-permute-start(f32[480,128]{1,0:T(8,128)S(1)} %get-tuple-element.54.refs_0_), channel_id=1, source_target_pairs={{0,4},{4,0},{8,12},{12,8},{16,20},{20,16},{24,28},{28,24},{1,5},{5... | collective-permute-start | bytes 737288 | tf_op jit(solution)/shard_map/ppermute | solution.py:325
  27.1 7.1 %collective-permute-start.3 = (f32[160,128]{1,0:T(8,128)S(1)}, f32[160,128]{1,0:T(8,128)S(1)}, u32[]{:S(2)}, u32[]{:S(2)}) collective-permute-start(f32[160,128]{1,0:T(8,128)S(1)} %get-tuple-element.60), channel_id=1, source_target_pairs={{0,16},{4,20},{8,24},{12,28},{16,0},{20,4},{24,8},{28,12},{1,17},{... | collective-permute-start | bytes 245768 | tf_op jit(solution)/shard_map/ppermute | solution.py:325
  34.7 3.6 %collective-permute-start.4 = (f32[160,128]{1,0:T(8,128)S(1)}, f32[160,128]{1,0:T(8,128)S(1)}, u32[]{:S(2)}, u32[]{:S(2)}) collective-permute-start(f32[160,128]{1,0:T(8,128)S(1)} %get-tuple-element.69), channel_id=1, source_target_pairs={{0,1},{1,0},{2,3},{3,2},{4,5},{5,4},{6,7},{7,6},{8,9},{9,8},{10,11... | collective-permute-start | bytes 245768 | tf_op jit(solution)/shard_map/ppermute | solution.py:334
  34.8 4.2 %collective-permute-start.5 = (f32[160,128]{1,0:T(8,128)S(1)}, f32[160,128]{1,0:T(8,128)S(1)}, u32[]{:S(2)}, u32[]{:S(2)}) collective-permute-start(f32[160,128]{1,0:T(8,128)S(1)} %get-tuple-element.70), channel_id=1, source_target_pairs={{0,3},{1,2},{2,1},{3,0},{4,7},{5,6},{6,5},{7,4},{8,11},{9,10},{10,... | collective-permute-start | bytes 245768 | tf_op jit(solution)/shard_map/ppermute | solution.py:333
  41.4 9.8 %collective-permute-start.8 = (f32[480,128]{1,0:T(8,128)S(1)}, f32[480,128]{1,0:T(8,128)S(1)}, u32[]{:S(2)}, u32[]{:S(2)}) collective-permute-start(f32[480,128]{1,0:T(8,128)S(1)} %constant_dynamic-update-slice_fusion.refs_0_), channel_id=1, source_target_pairs={{0,12},{4,8},{8,4},{12,0},{16,28},{20,24},{24,20},{28,16},{1,13},{... | collective-permute-start | bytes 737288 | tf_op jit(solution)/shard_map/ppermute | solution.py:325
  42.9 12.9 %collective-permute-start.7 = (f32[480,128]{1,0:T(8,128)S(1)}, f32[480,128]{1,0:T(8,128)S(1)}, u32[]{:S(2)}, u32[]{:S(2)}) collective-permute-start(f32[480,128]{1,0:T(8,128)S(1)} %constant_dynamic-update-slice_fusion.refs_0_), channel_id=1, source_target_pairs={{0,8},{4,12},{8,0},{12,4},{16,24},{20,28},{24,16},{28,20},{1,9},{5... | collective-permute-start | bytes 737288 | tf_op jit(solution)/shard_map/ppermute | solution.py:325
  44.4 11.5 %collective-permute-start.6 = (f32[480,128]{1,0:T(8,128)S(1)}, f32[480,128]{1,0:T(8,128)S(1)}, u32[]{:S(2)}, u32[]{:S(2)}) collective-permute-start(f32[480,128]{1,0:T(8,128)S(1)} %constant_dynamic-update-slice_fusion.refs_0_), channel_id=1, source_target_pairs={{0,4},{4,0},{8,12},{12,8},{16,20},{20,16},{24,28},{28,24},{1,5},{5... | collective-permute-start | bytes 737288 | tf_op jit(solution)/shard_map/ppermute | solution.py:325
  56.5 7.1 %collective-permute-start.9 = (f32[160,128]{1,0:T(8,128)S(1)}, f32[160,128]{1,0:T(8,128)S(1)}, u32[]{:S(2)}, u32[]{:S(2)}) collective-permute-start(f32[160,128]{1,0:T(8,128)S(1)} %get-tuple-element.79), channel_id=1, source_target_pairs={{0,16},{4,20},{8,24},{12,28},{16,0},{20,4},{24,8},{28,12},{1,17},{... | collective-permute-start | bytes 245768 | tf_op jit(solution)/shard_map/ppermute | solution.py:325
  64.0 3.6 %collective-permute-start.10 = (f32[160,128]{1,0:T(8,128)S(1)}, f32[160,128]{1,0:T(8,128)S(1)}, u32[]{:S(2)}, u32[]{:S(2)}) collective-permute-start(f32[160,128]{1,0:T(8,128)S(1)} %get-tuple-element.86), channel_id=1, source_target_pairs={{0,1},{1,0},{2,3},{3,2},{4,5},{5,4},{6,7},{7,6},{8,9},{9,8},{10,11... | collective-permute-start | bytes 245768 | tf_op jit(solution)/shard_map/ppermute | solution.py:334
  64.1 4.2 %collective-permute-start.11 = (f32[160,128]{1,0:T(8,128)S(1)}, f32[160,128]{1,0:T(8,128)S(1)}, u32[]{:S(2)}, u32[]{:S(2)}) collective-permute-start(f32[160,128]{1,0:T(8,128)S(1)} %get-tuple-element.87), channel_id=1, source_target_pairs={{0,3},{1,2},{2,1},{3,0},{4,7},{5,6},{6,5},{7,4},{8,11},{9,10},{10,... | collective-permute-start | bytes 245768 | tf_op jit(solution)/shard_map/ppermute | solution.py:333
  70.7 6.3 %collective-permute-start.14 = (f32[160,128]{1,0:T(8,128)S(1)}, f32[160,128]{1,0:T(8,128)S(1)}, u32[]{:S(2)}, u32[]{:S(2)}) collective-permute-start(f32[160,128]{1,0:T(8,128)S(1)} %get-tuple-element.89.refs_0_), channel_id=1, source_target_pairs={{0,12},{4,8},{8,4},{12,0},{16,28},{20,24},{24,20},{28,16},{1,13},{... | collective-permute-start | bytes 245768 | tf_op jit(solution)/shard_map/ppermute | solution.py:325
  71.3 6.8 %collective-permute-start.13 = (f32[160,128]{1,0:T(8,128)S(1)}, f32[160,128]{1,0:T(8,128)S(1)}, u32[]{:S(2)}, u32[]{:S(2)}) collective-permute-start(f32[160,128]{1,0:T(8,128)S(1)} %get-tuple-element.89.refs_0_), channel_id=1, source_target_pairs={{0,8},{4,12},{8,0},{12,4},{16,24},{20,28},{24,16},{28,20},{1,9},{5... | collective-permute-start | bytes 245768 | tf_op jit(solution)/shard_map/ppermute | solution.py:325
  73.7 4.6 %collective-permute-start.12 = (f32[160,128]{1,0:T(8,128)S(1)}, f32[160,128]{1,0:T(8,128)S(1)}, u32[]{:S(2)}, u32[]{:S(2)}) collective-permute-start(f32[160,128]{1,0:T(8,128)S(1)} %get-tuple-element.89.refs_0_), channel_id=1, source_target_pairs={{0,4},{4,0},{8,12},{12,8},{16,20},{20,16},{24,28},{28,24},{1,5},{5... | collective-permute-start | bytes 245768 | tf_op jit(solution)/shard_map/ppermute | solution.py:325
  78.9 6.5 %collective-permute-start.15 = (f32[160,128]{1,0:T(8,128)S(1)}, f32[160,128]{1,0:T(8,128)S(1)}, u32[]{:S(2)}, u32[]{:S(2)}) collective-permute-start(f32[160,128]{1,0:T(8,128)S(1)} %get-tuple-element.91), channel_id=1, source_target_pairs={{0,16},{4,20},{8,24},{12,28},{16,0},{20,4},{24,8},{28,12},{1,17},{... | collective-permute-start | bytes 245768 | tf_op jit(solution)/shard_map/ppermute | solution.py:325
  85.8 3.6 %collective-permute-start.16 = (f32[160,128]{1,0:T(8,128)S(1)}, f32[160,128]{1,0:T(8,128)S(1)}, u32[]{:S(2)}, u32[]{:S(2)}) collective-permute-start(f32[160,128]{1,0:T(8,128)S(1)} %get-tuple-element.96), channel_id=1, source_target_pairs={{0,1},{1,0},{2,3},{3,2},{4,5},{5,4},{6,7},{7,6},{8,9},{9,8},{10,11... | collective-permute-start | bytes 245768 | tf_op jit(solution)/shard_map/ppermute | solution.py:334
  85.9 4.2 %collective-permute-start.17 = (f32[160,128]{1,0:T(8,128)S(1)}, f32[160,128]{1,0:T(8,128)S(1)}, u32[]{:S(2)}, u32[]{:S(2)}) collective-permute-start(f32[160,128]{1,0:T(8,128)S(1)} %get-tuple-element.97), channel_id=1, source_target_pairs={{0,3},{1,2},{2,1},{3,0},{4,7},{5,6},{6,5},{7,4},{8,11},{9,10},{10,... | collective-permute-start | bytes 245768 | tf_op jit(solution)/shard_map/ppermute | solution.py:333
  92.4 6.3 %collective-permute-start.20 = (f32[160,128]{1,0:T(8,128)S(1)}, f32[160,128]{1,0:T(8,128)S(1)}, u32[]{:S(2)}, u32[]{:S(2)}) collective-permute-start(f32[160,128]{1,0:T(8,128)S(1)} %get-tuple-element.99.refs_0_), channel_id=1, source_target_pairs={{0,12},{4,8},{8,4},{12,0},{16,28},{20,24},{24,20},{28,16},{1,13},{... | collective-permute-start | bytes 245768 | tf_op jit(solution)/shard_map/ppermute | solution.py:325
  92.5 7.0 %collective-permute-start.19 = (f32[160,128]{1,0:T(8,128)S(1)}, f32[160,128]{1,0:T(8,128)S(1)}, u32[]{:S(2)}, u32[]{:S(2)}) collective-permute-start(f32[160,128]{1,0:T(8,128)S(1)} %get-tuple-element.99.refs_0_), channel_id=1, source_target_pairs={{0,8},{4,12},{8,0},{12,4},{16,24},{20,28},{24,16},{28,20},{1,9},{5... | collective-permute-start | bytes 245768 | tf_op jit(solution)/shard_map/ppermute | solution.py:325
  95.0 4.8 %collective-permute-start.18 = (f32[160,128]{1,0:T(8,128)S(1)}, f32[160,128]{1,0:T(8,128)S(1)}, u32[]{:S(2)}, u32[]{:S(2)}) collective-permute-start(f32[160,128]{1,0:T(8,128)S(1)} %get-tuple-element.99.refs_0_), channel_id=1, source_target_pairs={{0,4},{4,0},{8,12},{12,8},{16,20},{20,16},{24,28},{28,24},{1,5},{5... | collective-permute-start | bytes 245768 | tf_op jit(solution)/shard_map/ppermute | solution.py:325
  100.5 6.6 %collective-permute-start.21 = (f32[160,128]{1,0:T(8,128)S(1)}, f32[160,128]{1,0:T(8,128)S(1)}, u32[]{:S(2)}, u32[]{:S(2)}) collective-permute-start(f32[160,128]{1,0:T(8,128)S(1)} %get-tuple-element.101), channel_id=1, source_target_pairs={{0,16},{4,20},{8,24},{12,28},{16,0},{20,4},{24,8},{28,12},{1,17},{... | collective-permute-start | bytes 245768 | tf_op jit(solution)/shard_map/ppermute | solution.py:325
  (12 other events, 97.0 us)

commit v2 on v1

v2 whole, which is shorter than its diff:
```python
from functools import partial

import jax
import jax.numpy as jnp
from jax import lax
from jax.experimental import pallas as pl
from jax.experimental.pallas import tpu as pltpu
from jax.sharding import PartitionSpec as P

SWEEPS = 2
LANES = 128
F32 = jnp.float32
BF16 = jnp.bfloat16


def mm(a, b):
    return jnp.dot(a, b, preferred_element_type=F32)


def mm_t(a, b):
    return lax.dot_general(a, b, (((1,), (1,)), ((), ())), preferred_element_type=F32)


def two(x):
    high = x.astype(BF16)
    low = (x - high.astype(F32)).astype(BF16)
    return high, low


def exact_times(operator, x):
    n = x.shape[1]
    both = mm(operator, jnp.concatenate(two(x), axis=1))
    return both[:, :n] + both[:, n:]


def map_times(high, low, x):
    n = x.shape[1]
    x_high, x_low = two(x)
    both = mm(high, jnp.concatenate([x_high, x_low], axis=1))
    return both[:, :n] + both[:, n:] + mm(low, x_high)


def pad_rows(x):
    gap = jnp.zeros((LANES - x.shape[0], x.shape[1]), x.dtype)
    return jnp.concatenate([x, gap], axis=0)


def spread(x):
    width = x.shape[0] // 2
    return jnp.concatenate([pad_rows(x[:width]), pad_rows(x[width:])], axis=0)


def pick(flag, yes, no):
    return jnp.where(flag, yes, no)


def by_position(flag, x):
    width = x.shape[0] // 2
    return (
        pad_rows(pick(flag, x[:width], x[width:])),
        pad_rows(pick(flag, x[width:], x[:width])),
    )


def slot_map(flag, first, second, across, backward):
    none = jnp.zeros_like(across)
    if backward:
        lower, upper = pick(flag, none, across), pick(flag, across, none)
    else:
        lower, upper = pick(flag, across, none), pick(flag, none, across)
    return (
        jnp.concatenate([pick(flag, first, second), upper], axis=1),
        jnp.concatenate([lower, pick(flag, second, first)], axis=1),
    )


def pack_map(first, second, across, flag_value):
    width = first.shape[0]
    spare = LANES - width
    lane = lax.broadcasted_iota(jnp.int32, first.shape, 1)
    one = jnp.where(lane >= width, pltpu.roll(across, width, 1), first)
    rest = jnp.where(lane >= width, pltpu.roll(across, width - spare, 1), second)
    return one, jnp.where(lane >= 2 * width - spare, flag_value, rest)


def unpack_map(one, two_):
    width = one.shape[0]
    spare = LANES - width
    lane = lax.broadcasted_iota(jnp.int32, one.shape, 1)
    none = jnp.zeros_like(one)
    first = jnp.where(lane < width, one, none)
    second = jnp.where(lane < width, two_, none)
    across = jnp.where(lane < spare, pltpu.roll(one, LANES - width, 1), none)
    rest = pltpu.roll(two_, LANES - (width - spare), 1)
    across = jnp.where((lane >= spare) & (lane < width), rest, across)
    flag = jnp.broadcast_to(two_[0:1, LANES - 1 : LANES], (1, LANES)) > 0.5
    return first, second, across, flag


def call(body, outs, ins, flops=0, scratch=(), spaces=None):
    vmem = pl.BlockSpec(memory_space=pltpu.VMEM)
    moved = sum(x.size * x.dtype.itemsize for x in ins)
    moved += sum(o.size * o.dtype.itemsize for o in outs)
    return pl.pallas_call(
        body,
        out_shape=list(outs),
        in_specs=spaces or [vmem] * len(ins),
        out_specs=[vmem] * len(outs),
        scratch_shapes=list(scratch),
        compiler_params=pltpu.CompilerParams(vmem_limit_bytes=24 * 2**20),
        cost_estimate=pl.CostEstimate(flops=flops, bytes_accessed=moved, transcendentals=0),
    )(*ins)


def shape(*dims, dtype=F32):
    return jax.ShapeDtypeStruct(dims, dtype)


def pair(*dims):
    return [shape(*dims, dtype=BF16)] * 2


def face(ref, q, f, count=1):
    return ref[q, :, f * LANES : (f + count) * LANES]


def lift_times(high, low, q, f, x, count=1):
    return map_times(face(high, q, f, count), face(low, q, f, count), x)


def joined_coupling(blocks, flags, q):
    total = None
    for m in range(blocks.shape[1]):
        present = flags[2 + q * blocks.shape[1] + m : 3 + q * blocks.shape[1] + m, 0:1]
        block = blocks[q, m].astype(F32) * present
        total = block if total is None else total + block
    return two(total)


def first_kernel(order_in, count_in, links_in, types_in, rhs_in, inverse_in, table_in, traces_in,
                 lifts_in, packed, flags, inverse, blocks, traces, lifts, rhs, now, response,
                 held, order, count, links, types, small, large, table_sems):
    faces = blocks.shape[1]
    width = traces.shape[1]
    scalars = [
        pltpu.make_async_copy(a, b, small.at[i])
        for i, (a, b) in enumerate(
            ((order_in, order), (types_in, types), (links_in, links), (count_in, count))
        )
    ]
    for c in scalars:
        c.start()
    pairs = [(inverse_in, held), (rhs_in, rhs), (traces_in, traces)]
    for f in range(lifts_in.shape[0]):
        pairs.append((lifts_in.at[f], lifts.at[pl.ds(f * LANES, width), :]))
    copies = [pltpu.make_async_copy(a, b, large.at[i]) for i, (a, b) in enumerate(pairs)]
    for c in copies:
        c.start()
    for f in range(lifts_in.shape[0]):
        gap = lifts.at[pl.ds(f * LANES + width, LANES - width), :]
        gap[...] = jnp.zeros(gap.shape, BF16)
    for c in scalars:
        c.wait()
    fetched = {}
    for q in (1, 0):
        for m in range(faces):
            c = pltpu.make_async_copy(
                table_in.at[types[order[q], m]], blocks.at[q, m], table_sems.at[q * faces + m]
            )
            c.start()
            fetched[q, m] = c
    a, b = order[0], order[1]
    alive = (count[0] > 1).astype(F32)
    flags[...] = jnp.zeros_like(flags)
    flags[0:1, :] = jnp.full((1, LANES), (a == 0).astype(F32))
    flags[1:2, :] = jnp.full((1, LANES), alive)
    for q in (0, 1):
        for m in range(faces):
            row = 2 + q * faces + m
            present = (links[order[q], m] < 2).astype(F32)
            flags[row : row + 1, :] = jnp.full((1, LANES), present)
    for c in copies:
        c.wait()
    inverse[0] = held[a]
    inverse[1] = held[b] * alive.astype(BF16)
    head = lifts[0:LANES, :]
    now[0] = exact_times(inverse[0], rhs[a])
    response[0] = mm_t(inverse[0], head)
    response[2] = mm_t(inverse[1], head)
    for m in range(faces):
        fetched[1, m].wait()
    high, low = joined_coupling(blocks, flags, 1)
    met = map_times(high, low, jnp.concatenate([now[0], response[0]], axis=1))
    columns = now.shape[2]
    rest = jnp.concatenate([rhs[b] - met[:, :columns], met[:, columns:]], axis=1)
    rest = exact_times(inverse[1], rest)
    now[1] = rest[:, :columns]
    response[1] = rest[:, columns:]
    shown = exact_times(traces[1], jnp.concatenate([now[0], response[0]], axis=1))
    packed[pl.ds(pl.multiple_of(a * width, 8), width), :] = shown[:, :columns]
    after = jnp.concatenate([now[1], response[1], response[2]], axis=1)
    after = exact_times(traces[1], after)
    packed[pl.ds(pl.multiple_of(b * width, 8), width), :] = after[:, :columns]
    one, rest = pack_map(
        -shown[:, columns:],
        -after[:, columns + LANES :],
        after[:, columns : columns + LANES],
        flags[0:1, :],
    )
    packed[2 * width : 3 * width, :] = one
    packed[3 * width : 4 * width, :] = rest
    for m in range(faces):
        fetched[0, m].wait()


def side_traces(out, traces, flag, first, second):
    width = traces.shape[1]
    n = first.shape[1]
    for f in (2, 3):
        shown = exact_times(traces[f], jnp.concatenate([first, second], axis=1))
        out[f - 2, :width, :] = pick(flag, shown[:, :n], shown[:, n:])
        out[f - 2, width:, :] = pick(flag, shown[:, n:], shown[:, :n])


def store_side_map(high, low, traces, flag, first, second, across, backward):
    width = traces.shape[1]
    for f in (2, 3):
        shown = exact_times(traces[f], jnp.concatenate([first, second, across], axis=1))
        rows = slot_map(
            flag, -shown[:, :LANES], -shown[:, LANES : 2 * LANES], shown[:, 2 * LANES :], backward
        )
        for s in (0, 1):
            place = ((f - 2) * 2 + s) * width
            high[place : place + width, :], low[place : place + width, :] = two(rows[s])


def store_line_map(high, low, flag, first, second, across, backward):
    width = first.shape[0]
    for f in (0, 1):
        lanes = slice(f * LANES, (f + 1) * LANES)
        rows = slot_map(flag, -first[:, lanes], -second[:, lanes], across[:, lanes], backward)
        for s in (0, 1):
            place, held = slice(s * width, (s + 1) * width), slice(2 * f * LANES, 2 * (f + 1) * LANES)
            high[place, held], low[place, held] = two(rows[s])


def maps_kernel(flags, inverse, blocks, traces, lifts, rhs, now, response,
                z, d_high, d_low, e_high, e_low, side, side_high, side_low, back_map,
                q_high, q_low, last_high, last_low):
    flag = flags[0:1, :] > 0.5
    side_traces(side, traces, flag, now[0], now[1])
    store_side_map(
        side_high, side_low, traces, flag, response[0], response[2], response[1], False
    )
    z[0] = now[0]
    z[1] = exact_times(inverse[1], pick(flag, rhs[1], rhs[0]))
    for q in (0, 1):
        d_high[q], d_low[q] = two(mm_t(inverse[q], lifts[...]))
        high, low = joined_coupling(blocks, flags, q)
        e_high[q], e_low[q] = two(mm(inverse[q], high) + mm(inverse[q], low))
    faces = lifts.shape[0] // LANES - 1
    high, low = face(d_high, 1, 1, faces), face(d_low, 1, 1, faces)
    both = mm(e_high[0], jnp.concatenate([high, low], axis=1))
    n = faces * LANES
    across = both[:, :n] + both[:, n:] + mm(e_low[0], high)
    last_high[...], last_low[...] = two(across[:, :LANES])
    shown = []
    for q in (0, 1):
        shown.append(
            mm(traces[0], face(d_high, q, 1, faces)) + mm(traces[0], face(d_low, q, 1, faces))
        )
    shown.append(exact_times(traces[0], across))
    width = traces.shape[1]
    one, rest = pack_map(
        -shown[0][:, :LANES], -shown[1][:, :LANES], shown[2][:, :LANES], flags[0:1, :]
    )
    back_map[:width, :] = one
    back_map[width:, :] = rest
    store_line_map(q_high, q_low, flag, *(s[:, LANES:] for s in shown), True)


def more_maps_kernel(flags, traces, d_high, d_low, e_high, e_low, last_high, last_low,
                     side_high, side_low, q_high, q_low):
    flag = flags[0:1, :] > 0.5

    def joined(q, f, count):
        return face(d_high, q, f, count).astype(F32) + face(d_low, q, f, count).astype(F32)

    across = last_high[...].astype(F32) + last_low[...].astype(F32)
    store_side_map(
        side_high, side_low, traces, flag, joined(0, 1, 1), joined(1, 1, 1), across, True
    )
    high, low = face(d_high, 0, 2, 2), face(d_low, 0, 2, 2)
    both = mm(e_high[1], jnp.concatenate([high, low], axis=1))
    n = 2 * LANES
    across = both[:, :n] + both[:, n:] + mm(e_low[1], high)
    shown = exact_times(
        traces[1], jnp.concatenate([joined(0, 2, 2), joined(1, 2, 2), across], axis=1)
    )
    store_line_map(
        q_high, q_low, flag, shown[:, :n], shown[:, n : 2 * n], shown[:, 2 * n :], False
    )


def prepare_kernel(backward, flags, inflow, line, z, d_high, d_low, e_high, e_low, traces,
                   outflow, field, other):
    p0, p1 = (1, 0) if backward else (0, 1)
    f = 1 if backward else 0
    flag = flags[0:1, :] > 0.5
    entered = by_position(flag, inflow[...])
    width = traces.shape[1]
    lifted = lift_times(d_high, d_low, p0, f, entered[p0])
    y = line[...] - lifted
    start = z[p1] - lift_times(d_high, d_low, p1, f, entered[p1])
    start = start - map_times(e_high[p1], e_low[p1], y)
    field[...] = start
    left = z[p0] - lifted
    other[...] = left
    end = left - map_times(e_high[p0], e_low[p0], start)
    fields = (start, end) if p1 == 0 else (end, start)
    n = start.shape[1]
    shown = exact_times(traces[1 if backward else 0], jnp.concatenate(fields, axis=1))
    outflow[:width, :] = pick(flag, shown[:, :n], shown[:, n:])
    outflow[width:, :] = pick(flag, shown[:, n:], shown[:, :n])


def sides(involution, first, second):
    if not involution:
        return first[...], second[...]
    odd = lax.rem(lax.axis_index("span"), 2) == 1
    return pick(odd, first[...], second[...]), pick(odd, second[...], first[...])


def outflow_kernel(involution, base, q_high, q_low, first, second, outflow):
    arrived = jnp.concatenate([spread(v) for v in sides(involution, first, second)], axis=0)
    outflow[...] = base[...] + map_times(q_high[...], q_low[...], arrived)


def field_kernel(backward, involution, flags, first, second, start, left, d_high, d_low, e_high,
                 e_low, traces, line, second_line, side):
    p0, p1 = (1, 0) if backward else (0, 1)
    flag = flags[0:1, :] > 0.5
    arrived = [by_position(flag, v) for v in sides(involution, first, second)]

    def lifted(q):
        both = jnp.concatenate([v[q] for v in arrived], axis=0)
        return lift_times(d_high, d_low, q, 2, both, 2)

    y0 = start[...] - lifted(p0)
    line[...] = y0
    y1 = left[...] - lifted(p1) - map_times(e_high[p1], e_low[p1], y0)
    if second_line is not None:
        second_line[...] = y1
    if side is not None:
        fields = (y1, y0) if backward else (y0, y1)
        side_traces(side, traces, flag, *fields)


def last_kernel(enter, depth, flags, line, second_line, d_high, d_low, last_high, last_low, *refs):
    out = refs[-1]
    flag = flags[0:1, :] > 0.5
    entered = by_position(flag, enter(*refs[:-1]))
    y1 = second_line[...] + map_times(
        jnp.concatenate([last_high[...], -face(d_high, 0, 1)], axis=1),
        jnp.concatenate([last_low[...], -face(d_low, 0, 1)], axis=1),
        jnp.concatenate([entered[1], entered[0]], axis=0),
    )
    y0 = line[...] - lift_times(d_high, d_low, 1, 1, entered[1])
    out[0] = pick(flag, y1, y0)
    out[1] = pick(flag, y0, y1)


def digit_of(size, stride):
    return lax.rem(lax.div(lax.axis_index("stream"), stride), size)


def source_digit(digit, size, k):
    if size & (size - 1) == 0:
        return digit ^ k
    return lax.rem(digit - k + size, size)


def fold_kernel(size, stride, backward, first, *refs):
    parts, refs = refs[:size], refs[size:]
    if first:
        total, before, high, low, held = refs
    else:
        high, low, total, before, held = refs
    rows = total.shape[0]
    width = rows // 2
    digit = digit_of(size, stride)
    place = size - 1 - digit if backward else digit
    for k, part in enumerate(parts):
        m = source_digit(digit, size, k)
        m = size - 1 - m if backward else m
        held[m] = part[:rows, :]
        if first == "packed":
            a, b, c, flag = unpack_map(part[rows : rows + width, :], part[rows + width :, :])
            for s, row in enumerate(slot_map(flag, a, b, c, backward)):
                high[m, s * width : (s + 1) * width], low[m, s * width : (s + 1) * width] = two(row)
        elif first:
            for f in (0, 1):
                a, b = two(part[rows * (1 + f) : rows * (2 + f), :])
                high[m, :, f * LANES : (f + 1) * LANES] = a
                low[m, :, f * LANES : (f + 1) * LANES] = b
    state = held[0]
    below = jnp.zeros_like(state)
    for m in range(1, size):
        below = jnp.where(place == m, state, below)
        state = held[m] + map_times(high[m], low[m], spread(state))
    total[...] = state
    before[...] = below


def passage_kernel(size, stride, backward, high, low, pass_high, pass_low, whole):
    rows = high.shape[1]
    width = rows // 2
    digit = digit_of(size, stride)
    place = size - 1 - digit if backward else digit
    row = lax.broadcasted_iota(jnp.int32, (rows, 2 * LANES), 0)
    lane = lax.broadcasted_iota(jnp.int32, (rows, 2 * LANES), 1)
    moved = jnp.where(row < width, row, row - width + LANES)
    state = jnp.where(moved == lane, 1.0, 0.0)
    kept = state
    for m in range(size):
        kept = jnp.where(place == m, state, kept)
        if m < size - 1 or whole is not None:
            state = map_times(high[m], low[m], spread(state))
    pass_high[...], pass_low[...] = two(kept)
    if whole is not None:
        whole[:rows, :] = state[:, :LANES]
        whole[rows:, :] = state[:, LANES:]


def inflow_of(depth, last_stride, backward, *refs):
    befores, refs = refs[:depth], refs[depth:]
    passes, arrived = refs[: 2 * depth], refs[2 * depth]
    if last_stride:
        upper = digit_of(2, last_stride) == (0 if backward else 1)
        state = jnp.where(upper, arrived[...], 0.0)
    else:
        state = None
    for level in reversed(range(depth)):
        added = befores[level][...]
        if state is not None:
            high, low = passes[2 * level : 2 * level + 2]
            added = added + map_times(high[...], low[...], spread(state))
        state = added
    return jnp.zeros_like(arrived) if state is None else state


def enter_kernel(enter, involution, high, low, side, *refs):
    inflow, first, second = refs[-3:]
    state = enter(*refs[:-3])
    inflow[...] = state
    rows = state.shape[0]
    both = map_times(high[...], low[...], spread(state))
    lower_face = side[0] + both[:rows]
    upper_face = side[1] + both[rows:]
    if involution:
        odd = lax.rem(lax.axis_index("span"), 2) == 1
        first[...] = pick(odd, lower_face, upper_face)
        second[...] = pick(odd, upper_face, lower_face)
    else:
        first[...] = upper_face
        second[...] = lower_face


def levels_of(count):
    sizes, left = [], count
    for factor in (4, 2):
        while left % factor == 0:
            sizes.append(factor)
            left //= factor
    factor = 3
    while left > 1:
        while left % factor == 0:
            sizes.insert(0, factor)
            left //= factor
        factor += 2
    strides, stride = [], 1
    for size in sizes:
        strides.append(stride)
        stride *= size
    return list(zip(sizes, strides))


def exchange(block, axis, size, stride, k):
    pairs = []
    for i in range(lax.axis_size(axis)):
        digit = (i // stride) % size
        target = digit ^ k if size & (size - 1) == 0 else (digit + k) % size
        pairs.append((i, i + (target - digit) * stride))
    return lax.ppermute(block, axis, pairs)


def side_exchange(first, second, involution):
    n = lax.axis_size("span")
    if involution:
        pairs = [(j, j ^ 1) for j in range(n)]
        across = [(j, (j + 1) % n if j % 2 else (j - 1) % n) for j in range(n)]
        second = lax.ppermute(second, "span", across)
        first = lax.ppermute(first, "span", pairs)
        return first, second
    return (
        lax.ppermute(first, "span", [(j, (j + 1) % n) for j in range(n)]),
        lax.ppermute(second, "span", [(j, (j - 1) % n) for j in range(n)]),
    )


def local(rhs, inv_blocks, coupling, trace_ops, lift_ops, order, counts, neighbours, face_ids):
    source, inverse_in = rhs[0, 0], inv_blocks[0, 0]
    slots, block, columns = source.shape
    faces, width = trace_ops.shape[:2]
    links = neighbours.shape[-1]
    rows = 2 * width
    if slots != 2 or columns % LANES or 3 * width >= 2 * LANES:
        raise ValueError("unsupported sizes")
    levels = levels_of(lax.axis_size("stream"))
    span = lax.axis_size("span")
    involution = span % 2 == 0 and span > 2

    field, trace = shape(block, columns), shape(rows, columns)
    unit = 2 * block * block * LANES
    hbm = pl.BlockSpec(memory_space=pl.ANY)
    ins = (order[0, 0], counts[0], neighbours[0, 0], face_ids[0, 0], source, inverse_in, coupling,
           trace_ops, jnp.swapaxes(lift_ops, 1, 2))
    ins = tuple(
        x if x.size == 1 else pltpu.with_memory_space_constraint(x, pltpu.HBM) for x in ins
    )
    packed, flags, inverse, blocks, traces, lifts, held_rhs, now, response = call(
        first_kernel,
        [
            shape(2 * rows, LANES),
            shape(8 * -(-(2 + 2 * links) // 8), LANES),
            shape(2, block, block, dtype=BF16),
            shape(2, links, block, block, dtype=BF16),
            shape(faces, width, block, dtype=BF16),
            shape(faces * LANES, block, dtype=BF16),
            shape(2, block, columns),
            shape(2, block, columns),
            shape(3, block, LANES),
        ],
        ins,
        20 * unit,
        [
            pltpu.VMEM((2, block, block), BF16),
            *(pltpu.SMEM(x.shape, jnp.int32) for x in ins[:4]),
            pltpu.SemaphoreType.DMA((4,)),
            pltpu.SemaphoreType.DMA((3 + faces,)),
            pltpu.SemaphoreType.DMA((2 * links,)),
        ],
        [hbm] * len(ins),
    )
    table, square = pair(2, block, faces * LANES), pair(2, block, block)
    side_pair, line_pair = pair(2 * rows, 2 * LANES), pair(rows, 4 * LANES)
    store = {}

    def maps():
        return call(
            maps_kernel,
            [shape(2, block, columns), *table, *square, shape(2, rows, columns), *side_pair,
             shape(rows, LANES), *line_pair, *pair(block, LANES)],
            (flags, inverse, blocks, traces, lifts, held_rhs, now, response),
            40 * unit,
        )

    def more_maps():
        return call(
            more_maps_kernel,
            [*side_pair, *line_pair],
            (flags, traces, *store["d"], *store["e"], *store["last"]),
            16 * unit,
        )

    def carried(total, backward, whole, beside, later):
        befores, passes, arrived, done = [], [], total, None
        last_stride = 0
        for level, (size, stride) in enumerate(levels):
            last = level == len(levels) - 1
            if last and size == 2:
                arrived, last_stride = exchange(total, "stream", size, stride, 1), stride
                break
            key = ("fold", backward, level)
            first = key not in store
            if first:
                first = "whole" if level else "packed"
                if whole is not None:
                    total = jnp.concatenate([total, whole], axis=0)
            parts = [exchange(total, "stream", size, stride, k) for k in reversed(range(1, size))]
            parts = [total] + parts[::-1]
            if level == 0:
                parts, done = lax.optimization_barrier((parts, beside()))
            held = pltpu.VMEM((size, rows, columns), F32)
            body = partial(fold_kernel, size, stride, backward, first)
            if first:
                kinds = pair(size, rows, 2 * LANES)
                total, before, *store[key] = call(body, [trace, trace] + kinds, parts, unit, [held])
                body = partial(passage_kernel, size, stride, backward)
                if last or (level == len(levels) - 2 and levels[-1][0] == 2):
                    body, outs = partial(lambda f, *refs: f(*refs, None), body), []
                else:
                    outs = [shape(2 * rows, LANES)]
                outs = pair(rows, 2 * LANES) + outs
                high, low, *whole = call(body, outs, tuple(store[key]), 2 * unit)
                store["pass", backward, level] = (high, low)
                whole = whole[0] if whole else None
            else:
                total, before = call(body, [trace, trace], (*parts, *store[key]), unit, [held])
            befores.append(before)
            passes += store["pass", backward, level]
        done = beside() if done is None else done
        if later is not None:
            arrived, more = lax.optimization_barrier((arrived, later(done)))
            done = (done, more)
        depth = len(befores)
        return partial(inflow_of, depth, last_stride, backward), (*befores, *passes, arrived), done

    halves = [backward for _ in range(SWEEPS) for backward in (False, True)]
    for number, backward in enumerate(halves):
        final = number == len(halves) - 1
        if number == 0:
            enter, parts, done = carried(packed, backward, None, maps, None)
            store["z"], store["d"], store["e"], side = done[0], done[1:3], done[3:5], done[5]
            store["side", False], store["map"], store["line", True] = done[6:8], done[8], done[9:11]
            store["last"] = done[11:13]
            line = now[0]
        else:
            (outflow,) = call(
                partial(outflow_kernel, involution),
                [trace],
                (base, *store["line", backward], first, second),
                unit,
            )
            body = partial(field_kernel, backward, involution)
            outs = [field, field] if final else [field, shape(2, rows, columns)]
            ins = (flags, first, second, start, left, *store["d"], *store["e"], traces)
            cut = len(ins) + (2 if final else 1)
            body = partial(lambda f, n, *refs: f(*refs[:n], None, *refs[n:]), body, cut)
            later = (lambda _: more_maps()) if number == 1 else None
            beside = partial(call, body, outs, ins, 14 * unit)
            enter, parts, done = carried(outflow, backward, store["map"], beside, later)
            if later:
                done, more = done
                store["side", True], store["line", False] = more[:2], more[2:]
            line, side = done
        if final:
            ins = (flags, line, side, *store["d"], *store["last"], *parts)
            (x,) = call(partial(last_kernel, enter, len(parts)), [shape(2, block, columns)], ins, 4 * unit)
            break
        inflow, first, second = call(
            partial(enter_kernel, enter, involution),
            [trace] * 3,
            (*store["side", backward], side, *parts),
            unit,
        )
        first, second = side_exchange(first, second, involution)
        base, start, left = call(
            partial(prepare_kernel, backward),
            [trace, field, field],
            (flags, inflow, line, store["z"], *store["d"], *store["e"], traces),
            14 * unit,
        )
    return x[None, None]


def solution(mesh):
    placed = (
        P("stream", "span", None, None, None),
        P("stream", "span", None, None, None),
        P(),
        P(),
        P(),
        P("stream", "span", None),
        P("stream", "span"),
        P("stream", "span", None, None),
        P("stream", "span", None, None),
    )
    return jax.shard_map(
        local,
        mesh=mesh,
        in_specs=placed,
        out_specs=P("stream", "span", None, None, None),
        check_vma=False,
    )
```

time: 110 us -> 87.8 us (0.80)
  waiting for transfers between devices: 48.1 us -> 34.2 us
  local copies, waits for them, and re-layouts: 7.56 us -> 0.01 us
  Pallas kernels: 25.9 us -> 19.8 us
  starting transfers between devices: 27.4 us -> 32.8 us
    ppermute x16, waiting for transfers between devices: 46 us -> 29.6 us  [exchange(): return lax.ppermute(block, axis, pairs)]
    unnamed x30 -> x0, local copies, waits for them, and re-layouts: 7.52 us -> none
    pallas_call x19 -> x22, Pallas kernels: 25.9 us -> 19.8 us  [call(): pl.pallas_call(body, out_shape=list(outs), in_specs=spaces or [vmem] * le...]
    ppermute x16, starting transfers between devices: 22.2 us -> 27.5 us  [exchange(): return lax.ppermute(block, axis, pairs)]
    ppermute x3, waiting for transfers between devices: 2.15 us -> 4.54 us  [side_exchange(): second = lax.ppermute(second, 'span', across)]
  transfers between devices with their start and end apart: 22 -> 22, of which waited for: 17 -> 19; matrix products, arithmetic and copies ran while one was open for 0% -> 0% of each run, Pallas kernels for 9% -> 12%
where the time goes in v2:
time: 87.8 us; the launch traced here: 87.6 us
  waiting for transfers between devices  34.2 us (39%)
  starting transfers between devices  32.8 us (37%)
  Pallas kernels  19.8 us (23%)
    ppermute x16, waiting for transfers between devices, exchange(): return lax.ppermute(block, axis, pairs)  29.6 us
    ppermute x16, starting transfers between devices, exchange(): return lax.ppermute(block, axis, pairs)  27.5 us
    pallas_call x22, Pallas kernels, call(): pl.pallas_call(body, out_shape=list(outs), in_specs=spaces or [vmem] * le...  19.8 us
    ppermute x3, starting transfers between devices, side_exchange(): second = lax.ppermute(second, 'span', across)  5.05 us
    ppermute x3, waiting for transfers between devices, side_exchange(): second = lax.ppermute(second, 'span', across)  4.54 us
  transfers between devices with their start and end apart: 22, of which 19 were waited for; matrix products, arithmetic and copies ran while one was open for 0% of the time, Pallas kernels for 12%

profile of v2, /device:TPU:0, one launch (start us, length us, event | category | flops | bytes accessed | tf_op | source)
XLA Modules:
  0.0 87.6 jit_solution(15694097542030571570)
XLA Ops:
  0.7 3.5 %shard_map.91 = (f32[320,128]{1,0:T(8,128)S(1)}, f32[8,128]{1,0:T(8,128)S(1)}, bf16[2,320,320]{2,1,0:T(8,128)(2,1)S(1)}, bf16[2,2,320,320]{3,2,1,0:T(8,128)(2,1)...) custom-call(s32[2]{0:T(128)} %bitcast.16, ...), custom_call_target="tpu_custom_call" | custom-call | flops 524288000 | bytes 5451820 | tf_op jit(solution)/shard_map/pallas_call | solution.py:104
  4.2 3.0 %collective-permute-start = (f32[320,128]{1,0:T(8,128)S(1)}, f32[320,128]{1,0:T(8,128)S(1)}, u32[]{:S(2)}, u32[]{:S(2)}) collective-permute-start(f32[320,128]{1,0:T(8,128)S(1)} %get-tuple-element.136.refs_0_), channel_id=1, source_target_pairs={{0,4},{4,0},{8,12},{12,8},{16,20},{20,16},{24,28},{28,24},{1,5},{5... | collective-permute-start | bytes 491528 | tf_op jit(solution)/shard_map/ppermute | solution.py:494
  8.7 2.5 %shard_map.92 = (f32[2,320,128]{2,1,0:T(8,128)S(1)}, bf16[2,320,512]{2,1,0:T(8,128)(2,1)S(1)}, bf16[2,320,512]{2,1,0:T(8,128)(2,1)S(1)}, bf16[2,320,320]{2,1,0:T...) custom-call(f32[8,128]{1,0:T(8,128)S(1)} %get-tuple-element.111.flag, ...), custom_call_target="tpu_custom_call" | custom-call | flops 1048576000 | bytes 6434816 | tf_op jit(solution)/shard_map/pallas_call | solution.py:104
  11.4 2.8 %collective-permute-done.1.refs_2_ = f32[320,128]{1,0:T(8,128)S(1)} collective-permute-done((f32[320,128]{1,0:T(8,128)S(1)}, f32[320,128]{1,0:T(8,128)S(1)}, u32[]{:S(2)}, u32[]{:S(2)}) %collective-permute-start.1) | collective-permute-done | bytes 163872 | tf_op jit(solution)/shard_map/ppermute | solution.py:494
  14.2 1.9 %collective-permute-done.2.refs_3_ = f32[320,128]{1,0:T(8,128)S(1)} collective-permute-done((f32[320,128]{1,0:T(8,128)S(1)}, f32[320,128]{1,0:T(8,128)S(1)}, u32[]{:S(2)}, u32[]{:S(2)}) %collective-permute-start.2) | collective-permute-done | bytes 163872 | tf_op jit(solution)/shard_map/ppermute | solution.py:494
  16.9 2.8 %collective-permute-start.3 = (f32[160,128]{1,0:T(8,128)S(1)}, f32[160,128]{1,0:T(8,128)S(1)}, u32[]{:S(2)}, u32[]{:S(2)}) collective-permute-start(f32[160,128]{1,0:T(8,128)S(1)} %get-tuple-element.145), channel_id=1, source_target_pairs={{0,16},{4,20},{8,24},{12,28},{16,0},{20,4},{24,8},{28,12},{1,17},{... | collective-permute-start | bytes 245768 | tf_op jit(solution)/shard_map/ppermute | solution.py:494
  20.4 1.9 %collective-permute-done.3.refs_3_ = f32[160,128]{1,0:T(8,128)S(1)} collective-permute-done((f32[160,128]{1,0:T(8,128)S(1)}, f32[160,128]{1,0:T(8,128)S(1)}, u32[]{:S(2)}, u32[]{:S(2)}) %collective-permute-start.3) | collective-permute-done | bytes 81952 | tf_op jit(solution)/shard_map/ppermute | solution.py:494
  22.8 1.7 %collective-permute-start.5 = (f32[160,128]{1,0:T(8,128)S(1)}, f32[160,128]{1,0:T(8,128)S(1)}, u32[]{:S(2)}, u32[]{:S(2)}) collective-permute-start(f32[160,128]{1,0:T(8,128)S(1)} %get-tuple-element.156), channel_id=1, source_target_pairs={{0,3},{1,2},{2,1},{3,0},{4,7},{5,6},{6,5},{7,4},{8,11},{9,10},{10,... | collective-permute-start | bytes 245768 | tf_op jit(solution)/shard_map/ppermute | solution.py:502
  27.4 1.8 %collective-permute-start.6 = (f32[320,128]{1,0:T(8,128)S(1)}, f32[320,128]{1,0:T(8,128)S(1)}, u32[]{:S(2)}, u32[]{:S(2)}) collective-permute-start(f32[320,128]{1,0:T(8,128)S(1)} %pad_maximum_fusion.refs_0_), channel_id=1, source_target_pairs={{0,4},{4,0},{8,12},{12,8},{16,20},{20,16},{24,28},{28,24},{1,5},{5... | collective-permute-start | bytes 491528 | tf_op jit(solution)/shard_map/ppermute | solution.py:494
  31.8 2.2 %collective-permute-done.6.refs_1_ = f32[320,128]{1,0:T(8,128)S(1)} collective-permute-done((f32[320,128]{1,0:T(8,128)S(1)}, f32[320,128]{1,0:T(8,128)S(1)}, u32[]{:S(2)}, u32[]{:S(2)}) %collective-permute-start.6) | collective-permute-done | bytes 163872 | tf_op jit(solution)/shard_map/ppermute | solution.py:494
  33.9 2.3 %collective-permute-done.7.refs_2_ = f32[320,128]{1,0:T(8,128)S(1)} collective-permute-done((f32[320,128]{1,0:T(8,128)S(1)}, f32[320,128]{1,0:T(8,128)S(1)}, u32[]{:S(2)}, u32[]{:S(2)}) %collective-permute-start.7) | collective-permute-done | bytes 163872 | tf_op jit(solution)/shard_map/ppermute | solution.py:494
  36.2 2.4 %collective-permute-done.8.refs_3_ = f32[320,128]{1,0:T(8,128)S(1)} collective-permute-done((f32[320,128]{1,0:T(8,128)S(1)}, f32[320,128]{1,0:T(8,128)S(1)}, u32[]{:S(2)}, u32[]{:S(2)}) %collective-permute-start.8) | collective-permute-done | bytes 163872 | tf_op jit(solution)/shard_map/ppermute | solution.py:494
  39.4 3.4 %collective-permute-start.9 = (f32[160,128]{1,0:T(8,128)S(1)}, f32[160,128]{1,0:T(8,128)S(1)}, u32[]{:S(2)}, u32[]{:S(2)}) collective-permute-start(f32[160,128]{1,0:T(8,128)S(1)} %get-tuple-element.166), channel_id=1, source_target_pairs={{0,16},{4,20},{8,24},{12,28},{16,0},{20,4},{24,8},{28,12},{1,17},{... | collective-permute-start | bytes 245768 | tf_op jit(solution)/shard_map/ppermute | solution.py:494
  44.6 2.1 %collective-permute-done.9.refs_3_ = f32[160,128]{1,0:T(8,128)S(1)} collective-permute-done((f32[160,128]{1,0:T(8,128)S(1)}, f32[160,128]{1,0:T(8,128)S(1)}, u32[]{:S(2)}, u32[]{:S(2)}) %collective-permute-start.9) | collective-permute-done | bytes 81952 | tf_op jit(solution)/shard_map/ppermute | solution.py:494
  47.2 1.7 %collective-permute-start.11 = (f32[160,128]{1,0:T(8,128)S(1)}, f32[160,128]{1,0:T(8,128)S(1)}, u32[]{:S(2)}, u32[]{:S(2)}) collective-permute-start(f32[160,128]{1,0:T(8,128)S(1)} %get-tuple-element.188), channel_id=1, source_target_pairs={{0,3},{1,2},{2,1},{3,0},{4,7},{5,6},{6,5},{7,4},{8,11},{9,10},{10,... | collective-permute-start | bytes 245768 | tf_op jit(solution)/shard_map/ppermute | solution.py:502
  51.7 1.6 %collective-permute-start.12 = (f32[160,128]{1,0:T(8,128)S(1)}, f32[160,128]{1,0:T(8,128)S(1)}, u32[]{:S(2)}, u32[]{:S(2)}) collective-permute-start(f32[160,128]{1,0:T(8,128)S(1)} %shard_map.104.refs_0_), channel_id=1, source_target_pairs={{0,4},{4,0},{8,12},{12,8},{16,20},{20,16},{24,28},{28,24},{1,5},{5... | collective-permute-start | bytes 245768 | tf_op jit(solution)/shard_map/ppermute | solution.py:494
  56.5 2.1 %collective-permute-done.13.refs_2_ = f32[160,128]{1,0:T(8,128)S(1)} collective-permute-done((f32[160,128]{1,0:T(8,128)S(1)}, f32[160,128]{1,0:T(8,128)S(1)}, u32[]{:S(2)}, u32[]{:S(2)}) %collective-permute-start.13) | collective-permute-done | bytes 81952 | tf_op jit(solution)/shard_map/ppermute | solution.py:494
  60.1 3.3 %collective-permute-start.15 = (f32[160,128]{1,0:T(8,128)S(1)}, f32[160,128]{1,0:T(8,128)S(1)}, u32[]{:S(2)}, u32[]{:S(2)}) collective-permute-start(f32[160,128]{1,0:T(8,128)S(1)} %get-tuple-element.199), channel_id=1, source_target_pairs={{0,16},{4,20},{8,24},{12,28},{16,0},{20,4},{24,8},{28,12},{1,17},{... | collective-permute-start | bytes 245768 | tf_op jit(solution)/shard_map/ppermute | solution.py:494
  63.4 3.3 %collective-permute-done.15.refs_3_ = f32[160,128]{1,0:T(8,128)S(1)} collective-permute-done((f32[160,128]{1,0:T(8,128)S(1)}, f32[160,128]{1,0:T(8,128)S(1)}, u32[]{:S(2)}, u32[]{:S(2)}) %collective-permute-start.15) | collective-permute-done | bytes 81952 | tf_op jit(solution)/shard_map/ppermute | solution.py:494
  67.2 1.6 %collective-permute-start.17 = (f32[160,128]{1,0:T(8,128)S(1)}, f32[160,128]{1,0:T(8,128)S(1)}, u32[]{:S(2)}, u32[]{:S(2)}) collective-permute-start(f32[160,128]{1,0:T(8,128)S(1)} %get-tuple-element.204), channel_id=1, source_target_pairs={{0,3},{1,2},{2,1},{3,0},{4,7},{5,6},{6,5},{7,4},{8,11},{9,10},{10,... | collective-permute-start | bytes 245768 | tf_op jit(solution)/shard_map/ppermute | solution.py:502
  73.4 1.9 %collective-permute-start.20 = (f32[160,128]{1,0:T(8,128)S(1)}, f32[160,128]{1,0:T(8,128)S(1)}, u32[]{:S(2)}, u32[]{:S(2)}) collective-permute-start(f32[160,128]{1,0:T(8,128)S(1)} %shard_map.109.refs_0_), channel_id=1, source_target_pairs={{0,12},{4,8},{8,4},{12,0},{16,28},{20,24},{24,20},{28,16},{1,13},{... | collective-permute-start | bytes 245768 | tf_op jit(solution)/shard_map/ppermute | solution.py:494
  76.5 1.8 %collective-permute-done.19.refs_2_ = f32[160,128]{1,0:T(8,128)S(1)} collective-permute-done((f32[160,128]{1,0:T(8,128)S(1)}, f32[160,128]{1,0:T(8,128)S(1)}, u32[]{:S(2)}, u32[]{:S(2)}) %collective-permute-start.19) | collective-permute-done | bytes 81952 | tf_op jit(solution)/shard_map/ppermute | solution.py:494
  80.1 2.8 %collective-permute-start.21 = (f32[160,128]{1,0:T(8,128)S(1)}, f32[160,128]{1,0:T(8,128)S(1)}, u32[]{:S(2)}, u32[]{:S(2)}) collective-permute-start(f32[160,128]{1,0:T(8,128)S(1)} %get-tuple-element.216), channel_id=1, source_target_pairs={{0,16},{4,20},{8,24},{12,28},{16,0},{20,4},{24,8},{28,12},{1,17},{... | collective-permute-start | bytes 245768 | tf_op jit(solution)/shard_map/ppermute | solution.py:494
  82.8 3.6 %collective-permute-done.21.refs_3_ = f32[160,128]{1,0:T(8,128)S(1)} collective-permute-done((f32[160,128]{1,0:T(8,128)S(1)}, f32[160,128]{1,0:T(8,128)S(1)}, u32[]{:S(2)}, u32[]{:S(2)}) %collective-permute-start.21) | collective-permute-done | bytes 81952 | tf_op jit(solution)/shard_map/ppermute | solution.py:494
  (44 shorter events, 29.1 us)
Async XLA Ops:
  4.2 7.2 %collective-permute-start = (f32[320,128]{1,0:T(8,128)S(1)}, f32[320,128]{1,0:T(8,128)S(1)}, u32[]{:S(2)}, u32[]{:S(2)}) collective-permute-start(f32[320,128]{1,0:T(8,128)S(1)} %get-tuple-element.136.refs_0_), channel_id=1, source_target_pairs={{0,4},{4,0},{8,12},{12,8},{16,20},{20,16},{24,28},{28,24},{1,5},{5... | collective-permute-start | bytes 491528 | tf_op jit(solution)/shard_map/ppermute | solution.py:494
  7.1 7.1 %collective-permute-start.1 = (f32[320,128]{1,0:T(8,128)S(1)}, f32[320,128]{1,0:T(8,128)S(1)}, u32[]{:S(2)}, u32[]{:S(2)}) collective-permute-start(f32[320,128]{1,0:T(8,128)S(1)} %get-tuple-element.136.refs_0_), channel_id=1, source_target_pairs={{0,8},{4,12},{8,0},{12,4},{16,24},{20,28},{24,16},{28,20},{1,9},{5... | collective-permute-start | bytes 491528 | tf_op jit(solution)/shard_map/ppermute | solution.py:494
  8.7 7.5 %collective-permute-start.2 = (f32[320,128]{1,0:T(8,128)S(1)}, f32[320,128]{1,0:T(8,128)S(1)}, u32[]{:S(2)}, u32[]{:S(2)}) collective-permute-start(f32[320,128]{1,0:T(8,128)S(1)} %get-tuple-element.136.refs_0_), channel_id=1, source_target_pairs={{0,12},{4,8},{8,4},{12,0},{16,28},{20,24},{24,20},{28,16},{1,13},{... | collective-permute-start | bytes 491528 | tf_op jit(solution)/shard_map/ppermute | solution.py:494
  16.9 5.4 %collective-permute-start.3 = (f32[160,128]{1,0:T(8,128)S(1)}, f32[160,128]{1,0:T(8,128)S(1)}, u32[]{:S(2)}, u32[]{:S(2)}) collective-permute-start(f32[160,128]{1,0:T(8,128)S(1)} %get-tuple-element.145), channel_id=1, source_target_pairs={{0,16},{4,20},{8,24},{12,28},{16,0},{20,4},{24,8},{28,12},{1,17},{... | collective-permute-start | bytes 245768 | tf_op jit(solution)/shard_map/ppermute | solution.py:494
  22.8 2.9 %collective-permute-start.4 = (f32[160,128]{1,0:T(8,128)S(1)}, f32[160,128]{1,0:T(8,128)S(1)}, u32[]{:S(2)}, u32[]{:S(2)}) collective-permute-start(f32[160,128]{1,0:T(8,128)S(1)} %get-tuple-element.155), channel_id=1, source_target_pairs={{0,1},{1,0},{2,3},{3,2},{4,5},{5,4},{6,7},{7,6},{8,9},{9,8},{10,11... | collective-permute-start | bytes 245768 | tf_op jit(solution)/shard_map/ppermute | solution.py:503
  22.8 4.2 %collective-permute-start.5 = (f32[160,128]{1,0:T(8,128)S(1)}, f32[160,128]{1,0:T(8,128)S(1)}, u32[]{:S(2)}, u32[]{:S(2)}) collective-permute-start(f32[160,128]{1,0:T(8,128)S(1)} %get-tuple-element.156), channel_id=1, source_target_pairs={{0,3},{1,2},{2,1},{3,0},{4,7},{5,6},{6,5},{7,4},{8,11},{9,10},{10,... | collective-permute-start | bytes 245768 | tf_op jit(solution)/shard_map/ppermute | solution.py:502
  27.4 6.6 %collective-permute-start.6 = (f32[320,128]{1,0:T(8,128)S(1)}, f32[320,128]{1,0:T(8,128)S(1)}, u32[]{:S(2)}, u32[]{:S(2)}) collective-permute-start(f32[320,128]{1,0:T(8,128)S(1)} %pad_maximum_fusion.refs_0_), channel_id=1, source_target_pairs={{0,4},{4,0},{8,12},{12,8},{16,20},{20,16},{24,28},{28,24},{1,5},{5... | collective-permute-start | bytes 491528 | tf_op jit(solution)/shard_map/ppermute | solution.py:494
  29.1 7.1 %collective-permute-start.7 = (f32[320,128]{1,0:T(8,128)S(1)}, f32[320,128]{1,0:T(8,128)S(1)}, u32[]{:S(2)}, u32[]{:S(2)}) collective-permute-start(f32[320,128]{1,0:T(8,128)S(1)} %pad_maximum_fusion.refs_0_), channel_id=1, source_target_pairs={{0,8},{4,12},{8,0},{12,4},{16,24},{20,28},{24,16},{28,20},{1,9},{5... | collective-permute-start | bytes 491528 | tf_op jit(solution)/shard_map/ppermute | solution.py:494
  30.6 8.0 %collective-permute-start.8 = (f32[320,128]{1,0:T(8,128)S(1)}, f32[320,128]{1,0:T(8,128)S(1)}, u32[]{:S(2)}, u32[]{:S(2)}) collective-permute-start(f32[320,128]{1,0:T(8,128)S(1)} %pad_maximum_fusion.refs_0_), channel_id=1, source_target_pairs={{0,12},{4,8},{8,4},{12,0},{16,28},{20,24},{24,20},{28,16},{1,13},{... | collective-permute-start | bytes 491528 | tf_op jit(solution)/shard_map/ppermute | solution.py:494
  39.4 7.3 %collective-permute-start.9 = (f32[160,128]{1,0:T(8,128)S(1)}, f32[160,128]{1,0:T(8,128)S(1)}, u32[]{:S(2)}, u32[]{:S(2)}) collective-permute-start(f32[160,128]{1,0:T(8,128)S(1)} %get-tuple-element.166), channel_id=1, source_target_pairs={{0,16},{4,20},{8,24},{12,28},{16,0},{20,4},{24,8},{28,12},{1,17},{... | collective-permute-start | bytes 245768 | tf_op jit(solution)/shard_map/ppermute | solution.py:494
  47.1 2.8 %collective-permute-start.10 = (f32[160,128]{1,0:T(8,128)S(1)}, f32[160,128]{1,0:T(8,128)S(1)}, u32[]{:S(2)}, u32[]{:S(2)}) collective-permute-start(f32[160,128]{1,0:T(8,128)S(1)} %get-tuple-element.187), channel_id=1, source_target_pairs={{0,1},{1,0},{2,3},{3,2},{4,5},{5,4},{6,7},{7,6},{8,9},{9,8},{10,11... | collective-permute-start | bytes 245768 | tf_op jit(solution)/shard_map/ppermute | solution.py:503
  47.2 4.2 %collective-permute-start.11 = (f32[160,128]{1,0:T(8,128)S(1)}, f32[160,128]{1,0:T(8,128)S(1)}, u32[]{:S(2)}, u32[]{:S(2)}) collective-permute-start(f32[160,128]{1,0:T(8,128)S(1)} %get-tuple-element.188), channel_id=1, source_target_pairs={{0,3},{1,2},{2,1},{3,0},{4,7},{5,6},{6,5},{7,4},{8,11},{9,10},{10,... | collective-permute-start | bytes 245768 | tf_op jit(solution)/shard_map/ppermute | solution.py:502
  51.7 4.8 %collective-permute-start.12 = (f32[160,128]{1,0:T(8,128)S(1)}, f32[160,128]{1,0:T(8,128)S(1)}, u32[]{:S(2)}, u32[]{:S(2)}) collective-permute-start(f32[160,128]{1,0:T(8,128)S(1)} %shard_map.104.refs_0_), channel_id=1, source_target_pairs={{0,4},{4,0},{8,12},{12,8},{16,20},{20,16},{24,28},{28,24},{1,5},{5... | collective-permute-start | bytes 245768 | tf_op jit(solution)/shard_map/ppermute | solution.py:494
  53.3 5.3 %collective-permute-start.13 = (f32[160,128]{1,0:T(8,128)S(1)}, f32[160,128]{1,0:T(8,128)S(1)}, u32[]{:S(2)}, u32[]{:S(2)}) collective-permute-start(f32[160,128]{1,0:T(8,128)S(1)} %shard_map.104.refs_0_), channel_id=1, source_target_pairs={{0,8},{4,12},{8,0},{12,4},{16,24},{20,28},{24,16},{28,20},{1,9},{5... | collective-permute-start | bytes 245768 | tf_op jit(solution)/shard_map/ppermute | solution.py:494
  54.0 5.5 %collective-permute-start.14 = (f32[160,128]{1,0:T(8,128)S(1)}, f32[160,128]{1,0:T(8,128)S(1)}, u32[]{:S(2)}, u32[]{:S(2)}) collective-permute-start(f32[160,128]{1,0:T(8,128)S(1)} %shard_map.104.refs_0_), channel_id=1, source_target_pairs={{0,12},{4,8},{8,4},{12,0},{16,28},{20,24},{24,20},{28,16},{1,13},{... | collective-permute-start | bytes 245768 | tf_op jit(solution)/shard_map/ppermute | solution.py:494
  60.1 6.6 %collective-permute-start.15 = (f32[160,128]{1,0:T(8,128)S(1)}, f32[160,128]{1,0:T(8,128)S(1)}, u32[]{:S(2)}, u32[]{:S(2)}) collective-permute-start(f32[160,128]{1,0:T(8,128)S(1)} %get-tuple-element.199), channel_id=1, source_target_pairs={{0,16},{4,20},{8,24},{12,28},{16,0},{20,4},{24,8},{28,12},{1,17},{... | collective-permute-start | bytes 245768 | tf_op jit(solution)/shard_map/ppermute | solution.py:494
  67.1 2.7 %collective-permute-start.16 = (f32[160,128]{1,0:T(8,128)S(1)}, f32[160,128]{1,0:T(8,128)S(1)}, u32[]{:S(2)}, u32[]{:S(2)}) collective-permute-start(f32[160,128]{1,0:T(8,128)S(1)} %get-tuple-element.203), channel_id=1, source_target_pairs={{0,1},{1,0},{2,3},{3,2},{4,5},{5,4},{6,7},{7,6},{8,9},{9,8},{10,11... | collective-permute-start | bytes 245768 | tf_op jit(solution)/shard_map/ppermute | solution.py:503
  67.2 4.2 %collective-permute-start.17 = (f32[160,128]{1,0:T(8,128)S(1)}, f32[160,128]{1,0:T(8,128)S(1)}, u32[]{:S(2)}, u32[]{:S(2)}) collective-permute-start(f32[160,128]{1,0:T(8,128)S(1)} %get-tuple-element.204), channel_id=1, source_target_pairs={{0,3},{1,2},{2,1},{3,0},{4,7},{5,6},{6,5},{7,4},{8,11},{9,10},{10,... | collective-permute-start | bytes 245768 | tf_op jit(solution)/shard_map/ppermute | solution.py:502
  71.7 4.8 %collective-permute-start.18 = (f32[160,128]{1,0:T(8,128)S(1)}, f32[160,128]{1,0:T(8,128)S(1)}, u32[]{:S(2)}, u32[]{:S(2)}) collective-permute-start(f32[160,128]{1,0:T(8,128)S(1)} %shard_map.109.refs_0_), channel_id=1, source_target_pairs={{0,4},{4,0},{8,12},{12,8},{16,20},{20,16},{24,28},{28,24},{1,5},{5... | collective-permute-start | bytes 245768 | tf_op jit(solution)/shard_map/ppermute | solution.py:494
  73.0 5.3 %collective-permute-start.19 = (f32[160,128]{1,0:T(8,128)S(1)}, f32[160,128]{1,0:T(8,128)S(1)}, u32[]{:S(2)}, u32[]{:S(2)}) collective-permute-start(f32[160,128]{1,0:T(8,128)S(1)} %shard_map.109.refs_0_), channel_id=1, source_target_pairs={{0,8},{4,12},{8,0},{12,4},{16,24},{20,28},{24,16},{28,20},{1,9},{5... | collective-permute-start | bytes 245768 | tf_op jit(solution)/shard_map/ppermute | solution.py:494
  73.4 6.0 %collective-permute-start.20 = (f32[160,128]{1,0:T(8,128)S(1)}, f32[160,128]{1,0:T(8,128)S(1)}, u32[]{:S(2)}, u32[]{:S(2)}) collective-permute-start(f32[160,128]{1,0:T(8,128)S(1)} %shard_map.109.refs_0_), channel_id=1, source_target_pairs={{0,12},{4,8},{8,4},{12,0},{16,28},{20,24},{24,20},{28,16},{1,13},{... | collective-permute-start | bytes 245768 | tf_op jit(solution)/shard_map/ppermute | solution.py:494
  80.1 6.3 %collective-permute-start.21 = (f32[160,128]{1,0:T(8,128)S(1)}, f32[160,128]{1,0:T(8,128)S(1)}, u32[]{:S(2)}, u32[]{:S(2)}) collective-permute-start(f32[160,128]{1,0:T(8,128)S(1)} %get-tuple-element.216), channel_id=1, source_target_pairs={{0,16},{4,20},{8,24},{12,28},{16,0},{20,4},{24,8},{28,12},{1,17},{... | collective-permute-start | bytes 245768 | tf_op jit(solution)/shard_map/ppermute | solution.py:494

commit v3 on v2

--- a/solution.py
+++ b/solution.py
@@ -356,28 +356,66 @@
         side_traces(side, traces, flag, *fields)
 
 
-def last_kernel(enter, depth, flags, line, second_line, d_high, d_low, last_high, last_low, *refs):
-    out = refs[-1]
+def last_response_kernel(depth, flags, d_high, d_low, last_high, last_low, *refs):
+    passes, (high, low, far_high, far_low) = refs[:-4], refs[-4:]
     flag = flags[0:1, :] > 0.5
-    entered = by_position(flag, enter(*refs[:-1]))
-    y1 = second_line[...] + map_times(
-        jnp.concatenate([last_high[...], -face(d_high, 0, 1)], axis=1),
-        jnp.concatenate([last_low[...], -face(d_low, 0, 1)], axis=1),
-        jnp.concatenate([entered[1], entered[0]], axis=0),
-    )
-    y0 = line[...] - lift_times(d_high, d_low, 1, 1, entered[1])
-    out[0] = pick(flag, y1, y0)
-    out[1] = pick(flag, y0, y1)
+    none = jnp.zeros((d_high.shape[1], LANES), F32)
+
+    def joined(h, l):
+        return h.astype(F32) + l.astype(F32)
+
+    own = -joined(face(d_high, 0, 1), face(d_low, 0, 1))
+    other = -joined(face(d_high, 1, 1), face(d_low, 1, 1))
+    across = joined(last_high[...], last_low[...])
+    rows = slot_map(flag, own, other, across, True)
+    for s in (0, 1):
+        high[s], low[s] = two(rows[s])
+        far_high[s], far_low[s] = two(through(high[s], low[s], depth, passes))
+
+
+def last_base_kernel(flags, line, second_line, high, low, inflow, out):
+    flag = flags[0:1, :] > 0.5
+    entered = spread(inflow[...])
+    out[0] = pick(flag, second_line[...], line[...]) + map_times(high[0], low[0], entered)
+    out[1] = pick(flag, line[...], second_line[...]) + map_times(high[1], low[1], entered)
+
+
+def last_kernel(stride, backward, base, high, low, arrived, out):
+    entered = spread(last_arrived(stride, backward, arrived))
+    for s in (0, 1):
+        out[s] = base[s] + map_times(high[s], low[s], entered)
 
 
 def digit_of(size, stride):
     return lax.rem(lax.div(lax.axis_index("stream"), stride), size)
 
 
-def source_digit(digit, size, k):
-    if size & (size - 1) == 0:
-        return digit ^ k
-    return lax.rem(digit - k + size, size)
+def place_of(size, stride, backward):
+    digit = digit_of(size, stride)
+    return size - 1 - digit if backward else digit
+
+
+def source_place(size, stride, backward, i):
+    digit, k = digit_of(size, stride), (size - i) % size
+    m = digit ^ k if size & (size - 1) == 0 else lax.rem(digit - k + size, size)
+    return size - 1 - m if backward else m
+
+
+def store_packed(high, low, m, packed, backward):
+    width = packed.shape[0] // 2
+    a, b, c, flag = unpack_map(packed[:width], packed[width:])
+    for s, row in enumerate(slot_map(flag, a, b, c, backward)):
+        high[m, s * width : (s + 1) * width], low[m, s * width : (s + 1) * width] = two(row)
+
+
+def in_turn(size, place, values, high, low):
+    state = values[0]
+    below = jnp.zeros_like(state)
+    for m in range(1, size):
+        below = jnp.where(place == m, state, below)
+        if m < size:
+            state = values[m] + map_times(high[m], low[m], spread(state))
+    return state, below
 
 
 def fold_kernel(size, stride, backward, first, *refs):
@@ -387,36 +425,53 @@
     else:
         high, low, total, before, held = refs
     rows = total.shape[0]
-    width = rows // 2
-    digit = digit_of(size, stride)
-    place = size - 1 - digit if backward else digit
-    for k, part in enumerate(parts):
-        m = source_digit(digit, size, k)
-        m = size - 1 - m if backward else m
+    for i, part in enumerate(parts):
+        m = source_place(size, stride, backward, i)
         held[m] = part[:rows, :]
         if first == "packed":
-            a, b, c, flag = unpack_map(part[rows : rows + width, :], part[rows + width :, :])
-            for s, row in enumerate(slot_map(flag, a, b, c, backward)):
-                high[m, s * width : (s + 1) * width], low[m, s * width : (s + 1) * width] = two(row)
+            store_packed(high, low, m, part[rows:, :], backward)
         elif first:
             for f in (0, 1):
                 a, b = two(part[rows * (1 + f) : rows * (2 + f), :])
                 high[m, :, f * LANES : (f + 1) * LANES] = a
                 low[m, :, f * LANES : (f + 1) * LANES] = b
-    state = held[0]
-    below = jnp.zeros_like(state)
-    for m in range(1, size):
-        below = jnp.where(place == m, state, below)
-        state = held[m] + map_times(high[m], low[m], spread(state))
-    total[...] = state
-    before[...] = below
+    place = place_of(size, stride, backward)
+    total[...], before[...] = in_turn(size, place, held, high, low)
+
+
+def unpack_kernel(size, stride, backward, *refs):
+    parts, (high, low) = refs[:size], refs[size:]
+    for i, part in enumerate(parts):
+        store_packed(high, low, source_place(size, stride, backward, i), part[...], backward)
+
+
+def total_kernel(size, stride, backward, *refs):
+    parts, (high, low, total, held) = refs[:size], refs[size:]
+    for i, part in enumerate(parts):
+        held[source_place(size, stride, backward, i)] = part[...]
+    below = jnp.concatenate([spread(held[m]) for m in range(size - 1)], axis=0)
+    total[...] = held[size - 1] + map_times(high[...], low[...], below)
+
+
+def before_kernel(size, stride, backward, held, high, low, before):
+    place = place_of(size, stride, backward)
+    _, before[...] = in_turn(size, place, held, high, low)
+
+
+def suffix_kernel(size, high, low, out_high, out_low):
+    state_high, state_low = high[size - 1], low[size - 1]
+    for m in reversed(range(size - 1)):
+        lanes = slice(2 * LANES * m, 2 * LANES * (m + 1))
+        out_high[:, lanes], out_low[:, lanes] = state_high, state_low
+        if m:
+            inner = high[m].astype(F32) + low[m].astype(F32)
+            state_high, state_low = two(map_times(state_high, state_low, spread(inner)))
 
 
 def passage_kernel(size, stride, backward, high, low, pass_high, pass_low, whole):
     rows = high.shape[1]
     width = rows // 2
-    digit = digit_of(size, stride)
-    place = size - 1 - digit if backward else digit
+    place = place_of(size, stride, backward)
     row = lax.broadcasted_iota(jnp.int32, (rows, 2 * LANES), 0)
     lane = lax.broadcasted_iota(jnp.int32, (rows, 2 * LANES), 1)
     moved = jnp.where(row < width, row, row - width + LANES)
@@ -425,38 +480,67 @@
     for m in range(size):
         kept = jnp.where(place == m, state, kept)
         if m < size - 1 or whole is not None:
-            state = map_times(high[m], low[m], spread(state))
+            if m:
+                state = map_times(high[m], low[m], spread(state))
+            else:
+                state = high[0].astype(F32) + low[0].astype(F32)
     pass_high[...], pass_low[...] = two(kept)
     if whole is not None:
         whole[:rows, :] = state[:, :LANES]
         whole[rows:, :] = state[:, LANES:]
 
 
-def inflow_of(depth, last_stride, backward, *refs):
+def through(high, low, depth, passes):
+    state = None
+    for level in range(depth):
+        if state is not None:
+            high, low = two(state)
+        inner = passes[2 * level][...].astype(F32) + passes[2 * level + 1][...].astype(F32)
+        state = map_times(high, low, spread(inner))
+    return high.astype(F32) + low.astype(F32) if state is None else state
+
+
+def join_kernel(depth, side_high, side_low, *refs):
+    passes, (high, low) = refs[:-2], refs[-2:]
+    rows = side_high.shape[0]
+    high[:rows], low[:rows] = two(through(side_high[...], side_low[...], depth, passes))
+    if depth == 1:
+        high[rows:], low[rows:] = passes[0][...], passes[1][...]
+    else:
+        high[rows:], low[rows:] = two(through(passes[0][...], passes[1][...], depth - 1, passes[2:]))
+
+
+def base_kernel(depth, *refs):
     befores, refs = refs[:depth], refs[depth:]
-    passes, arrived = refs[: 2 * depth], refs[2 * depth]
-    if last_stride:
-        upper = digit_of(2, last_stride) == (0 if backward else 1)
-        state = jnp.where(upper, arrived[...], 0.0)
-    else:
-        state = None
-    for level in reversed(range(depth)):
-        added = befores[level][...]
-        if state is not None:
-            high, low = passes[2 * level : 2 * level + 2]
-            added = added + map_times(high[...], low[...], spread(state))
-        state = added
-    return jnp.zeros_like(arrived) if state is None else state
-
-
-def enter_kernel(enter, involution, high, low, side, *refs):
-    inflow, first, second = refs[-3:]
-    state = enter(*refs[:-3])
+    passes, refs = refs[: 2 * depth], refs[2 * depth :]
+    side, high, low, base, inflow = refs
+    state = befores[depth - 1][...]
+    for level in reversed(range(depth - 1)):
+        inner = map_times(passes[2 * level][...], passes[2 * level + 1][...], spread(state))
+        state = befores[level][...] + inner
     inflow[...] = state
-    rows = state.shape[0]
-    both = map_times(high[...], low[...], spread(state))
-    lower_face = side[0] + both[:rows]
-    upper_face = side[1] + both[rows:]
+    if base is not None:
+        both = map_times(high[...], low[...], spread(state))
+        rows = state.shape[0]
+        base[0] = side[0] + both[:rows]
+        base[1] = side[1] + both[rows:]
+
+
+def last_arrived(stride, backward, arrived):
+    if not stride:
+        return jnp.zeros(arrived.shape, F32)
+    upper = digit_of(2, stride) == (0 if backward else 1)
+    return jnp.where(upper, arrived[...], 0.0)
+
+
+def enter_kernel(stride, backward, involution, base, before, high, low, arrived,
+                 inflow, first, second):
+    rows = inflow.shape[0]
+    entered = spread(last_arrived(stride, backward, arrived))
+    added = map_times(high[...], low[...], entered)
+    inflow[...] = before[...] + added[2 * rows :]
+    lower_face = base[0] + added[:rows]
+    upper_face = base[1] + added[rows : 2 * rows]
     if involution:
         odd = lax.rem(lax.axis_index("span"), 2) == 1
         first[...] = pick(odd, lower_face, upper_face)
@@ -573,58 +657,94 @@
             16 * unit,
         )
 
-    def carried(total, backward, whole, beside, later):
-        befores, passes, arrived, done = [], [], total, None
-        last_stride = 0
+    def parts_of(block, size, stride):
+        sent = [exchange(block, "stream", size, stride, k) for k in reversed(range(1, size))]
+        return [block] + sent
+
+    def passage(key, size, stride):
+        backward, level = key
+        body = partial(passage_kernel, size, stride, backward)
+        if level == len(levels) - 1 or (level == len(levels) - 2 and levels[-1][0] == 2):
+            body, outs = partial(lambda f, *refs: f(*refs, None), body), []
+        else:
+            outs = [shape(2 * rows, LANES)]
+        high, low, *whole = call(body, pair(rows, 2 * LANES) + outs, store["maps", key], 2 * unit)
+        store["pass", key] = (high, low)
+        store["whole", key] = whole
+
+    def carried(total, backward, beside):
+        befores, passes, done, stride_of_last = [], [], None, 0
         for level, (size, stride) in enumerate(levels):
-            last = level == len(levels) - 1
-            if last and size == 2:
-                arrived, last_stride = exchange(total, "stream", size, stride, 1), stride
+            key = (backward, level)
+            if level == len(levels) - 1 and size == 2:
+                total, stride_of_last = exchange(total, "stream", size, stride, 1), stride
                 break
-            key = ("fold", backward, level)
-            first = key not in store
+            first = ("maps", key) not in store
             if first:
                 first = "whole" if level else "packed"
-                if whole is not None:
-                    total = jnp.concatenate([total, whole], axis=0)
-            parts = [exchange(total, "stream", size, stride, k) for k in reversed(range(1, size))]
-            parts = [total] + parts[::-1]
+                if level:
+                    total = jnp.concatenate([total, *store["whole", (backward, level - 1)]], axis=0)
+            parts = parts_of(total, size, stride)
             if level == 0:
                 parts, done = lax.optimization_barrier((parts, beside()))
-            held = pltpu.VMEM((size, rows, columns), F32)
+            held = shape(size, rows, columns)
+            scratch = [pltpu.VMEM(held.shape, F32)]
             body = partial(fold_kernel, size, stride, backward, first)
             if first:
-                kinds = pair(size, rows, 2 * LANES)
-                total, before, *store[key] = call(body, [trace, trace] + kinds, parts, unit, [held])
-                body = partial(passage_kernel, size, stride, backward)
-                if last or (level == len(levels) - 2 and levels[-1][0] == 2):
-                    body, outs = partial(lambda f, *refs: f(*refs, None), body), []
-                else:
-                    outs = [shape(2 * rows, LANES)]
-                outs = pair(rows, 2 * LANES) + outs
-                high, low, *whole = call(body, outs, tuple(store[key]), 2 * unit)
-                store["pass", backward, level] = (high, low)
-                whole = whole[0] if whole else None
+                outs = [trace, trace, *pair(size, rows, 2 * LANES)]
+                total, before, *kept = call(body, outs, parts, unit, scratch)
+                store["maps", key] = tuple(kept)
+                passage(key, size, stride)
+            elif ("suffix", key) in store:
+                body = partial(total_kernel, size, stride, backward)
+                total, held = call(body, [trace, held], (*parts, *store["suffix", key]), unit)
+                body = partial(before_kernel, size, stride, backward)
+                (before,) = call(body, [trace], (held, *store["maps", key]), unit)
             else:
-                total, before = call(body, [trace, trace], (*parts, *store[key]), unit, [held])
+                ins = (*parts, *store["maps", key])
+                total, before = call(body, [trace, trace], ins, unit, scratch)
             befores.append(before)
-            passes += store["pass", backward, level]
-        done = beside() if done is None else done
-        if later is not None:
-            arrived, more = lax.optimization_barrier((arrived, later(done)))
-            done = (done, more)
-        depth = len(befores)
-        return partial(inflow_of, depth, last_stride, backward), (*befores, *passes, arrived), done
-
+            passes += store["pass", key]
+        if not befores:
+            befores = [jnp.zeros_like(total)]
+            passes = [jnp.zeros((rows, 2 * LANES), BF16)] * 2
+        return befores, passes, total, stride_of_last, done or beside()
+
+    def suffixes(backward):
+        out = {}
+        for level, (size, _) in enumerate(levels):
+            key = (backward, level)
+            if ("maps", key) in store:
+                outs = pair(rows, 2 * LANES * (size - 1))
+                out["suffix", key] = call(
+                    partial(suffix_kernel, size), outs, store["maps", key], unit
+                )
+        return out
+
+    def send_maps(block):
+        size, stride = levels[0]
+        after = store["pass", (False, 0)]
+        block, store["pass", (False, 0)] = lax.optimization_barrier((block, after))
+        return parts_of(block, size, stride)
+
+    def take_maps(parts):
+        size, stride = levels[0]
+        body = partial(unpack_kernel, size, stride, True)
+        store["maps", (True, 0)] = tuple(call(body, pair(size, rows, 2 * LANES), parts, unit))
+        passage((True, 0), size, stride)
+
+    grouped = levels and not (len(levels) == 1 and levels[0][0] == 2)
     halves = [backward for _ in range(SWEEPS) for backward in (False, True)]
     for number, backward in enumerate(halves):
         final = number == len(halves) - 1
         if number == 0:
-            enter, parts, done = carried(packed, backward, None, maps, None)
+            befores, passes, arrived, stride, done = carried(packed, backward, maps)
             store["z"], store["d"], store["e"], side = done[0], done[1:3], done[3:5], done[5]
-            store["side", False], store["map"], store["line", True] = done[6:8], done[8], done[9:11]
+            store["side", False], store["line", True] = done[6:8], done[9:11]
             store["last"] = done[11:13]
             line = now[0]
+            if grouped:
+                sent = send_maps(done[8])
         else:
             (outflow,) = call(
                 partial(outflow_kernel, involution),
@@ -637,21 +757,49 @@
             ins = (flags, first, second, start, left, *store["d"], *store["e"], traces)
             cut = len(ins) + (2 if final else 1)
             body = partial(lambda f, n, *refs: f(*refs[:n], None, *refs[n:]), body, cut)
-            later = (lambda _: more_maps()) if number == 1 else None
-            beside = partial(call, body, outs, ins, 14 * unit)
-            enter, parts, done = carried(outflow, backward, store["map"], beside, later)
-            if later:
-                done, more = done
-                store["side", True], store["line", False] = more[:2], more[2:]
-            line, side = done
+
+            def beside():
+                more = {}
+                if number == 1:
+                    out = more_maps()
+                    more = {("side", True): out[:2], ("line", False): out[2:]}
+                return call(body, outs, ins, 14 * unit), more
+
+            if number == 1 and grouped:
+                take_maps(sent)
+            befores, passes, arrived, stride, done = carried(outflow, backward, beside)
+            line, side = done[0]
+            store.update(done[1])
+        depth = len(befores)
         if final:
-            ins = (flags, line, side, *store["d"], *store["last"], *parts)
-            (x,) = call(partial(last_kernel, enter, len(parts)), [shape(2, block, columns)], ins, 4 * unit)
+            wide = pair(2, block, 2 * LANES)
+            body = partial(last_response_kernel, depth)
+            out = call(body, wide + wide, (flags, *store["d"], *store["last"], *passes), 4 * unit)
+            near, far = out[:2], out[2:]
+            body = partial(base_kernel, depth)
+            body = partial(lambda f, *refs: f(*refs[:-1], None, None, None, None, refs[-1]), body)
+            (before,) = call(body, [trace], (*befores, *passes), unit)
+            ins = (flags, line, side, *near, before)
+            (base,) = call(last_base_kernel, [shape(2, block, columns)], ins, 2 * unit)
+            body = partial(last_kernel, stride, backward)
+            (x,) = call(body, [shape(2, block, columns)], (base, *far, arrived), 2 * unit)
             break
+        if number < 2:
+            store.update(suffixes(backward))
+        if ("join", backward) not in store:
+            ins = (*store["side", backward], *passes)
+            body = partial(join_kernel, depth)
+            store["join", backward] = call(body, pair(3 * rows, 2 * LANES), ins, unit)
+        base, before = call(
+            partial(base_kernel, depth),
+            [shape(2, rows, columns), trace],
+            (*befores, *passes, side, *store["side", backward]),
+            unit,
+        )
         inflow, first, second = call(
-            partial(enter_kernel, enter, involution),
+            partial(enter_kernel, stride, backward, involution),
             [trace] * 3,
-            (*store["side", backward], side, *parts),
+            (base, before, *store["join", backward], arrived),
             unit,
         )
         first, second = side_exchange(first, second, involution)

time: 87.8 us -> 83.7 us (0.953)
  waiting for transfers between devices: 34.2 us -> 27 us
  Pallas kernels: 19.8 us -> 22.3 us
    ppermute x16 -> x19, waiting for transfers between devices: 29.6 us -> 23.9 us  [exchange(): return lax.ppermute(block, axis, pairs)]
    pallas_call x22 -> x35, Pallas kernels: 19.8 us -> 22.3 us  [call(): pl.pallas_call(body, out_shape=list(outs), in_specs=spaces or [vmem] * le...]
    ppermute x3, waiting for transfers between devices: 4.54 us -> 3.09 us  [side_exchange(): second = lax.ppermute(second, 'span', across)]
    ppermute x16 -> x19, starting transfers between devices: 27.5 us -> 27.9 us  [exchange(): return lax.ppermute(block, axis, pairs)]
  transfers between devices with their start and end apart: 22 -> 25, of which waited for: 19 -> 17; matrix products, arithmetic and copies ran while one was open for 0% -> 0% of each run, Pallas kernels for 12% -> 18%
where the time goes in v3:
time: 83.7 us; the launch traced here: 83.5 us
  starting transfers between devices  33.3 us (40%)
  waiting for transfers between devices  27 us (32%)
  Pallas kernels  22.3 us (27%)
  between operations  0.95 us (1%)
    ppermute x19, starting transfers between devices, exchange(): return lax.ppermute(block, axis, pairs)  27.9 us
    ppermute x19, waiting for transfers between devices, exchange(): return lax.ppermute(block, axis, pairs)  23.9 us
    pallas_call x35, Pallas kernels, call(): pl.pallas_call(body, out_shape=list(outs), in_specs=spaces or [vmem] * le...  22.3 us
    ppermute x3, starting transfers between devices, side_exchange(): second = lax.ppermute(second, 'span', across)  5.16 us
    ppermute x3, waiting for transfers between devices, side_exchange(): second = lax.ppermute(second, 'span', across)  3.09 us
  transfers between devices with their start and end apart: 25, of which 17 were waited for; matrix products, arithmetic and copies ran while one was open for 0% of the time, Pallas kernels for 18%

profile of v3, /device:TPU:0, one launch (start us, length us, event | category | flops | bytes accessed | tf_op | source)
XLA Modules:
  0.0 83.5 jit_solution(7905788280637681922)
XLA Ops:
  0.7 3.5 %shard_map.91 = (f32[320,128]{1,0:T(8,128)S(1)}, f32[8,128]{1,0:T(8,128)S(1)}, bf16[2,320,320]{2,1,0:T(8,128)(2,1)S(1)}, bf16[2,2,320,320]{3,2,1,0:T(8,128)(2,1)...) custom-call(s32[2]{0:T(128)} %bitcast.16, ...), custom_call_target="tpu_custom_call" | custom-call | flops 524288000 | bytes 5451820 | tf_op jit(solution)/shard_map/pallas_call | solution.py:104
  4.1 4.0 %collective-permute-start = (f32[320,128]{1,0:T(8,128)S(1)}, f32[320,128]{1,0:T(8,128)S(1)}, u32[]{:S(2)}, u32[]{:S(2)}) collective-permute-start(f32[320,128]{1,0:T(8,128)S(1)} %get-tuple-element.153.refs_0_), channel_id=1, source_target_pairs={{0,12},{4,8},{8,4},{12,0},{16,28},{20,24},{24,20},{28,16},{1,13},{... | collective-permute-start | bytes 491528 | tf_op jit(solution)/shard_map/ppermute | solution.py:578
  8.8 2.5 %shard_map.92 = (f32[2,320,128]{2,1,0:T(8,128)S(1)}, bf16[2,320,512]{2,1,0:T(8,128)(2,1)S(1)}, bf16[2,320,512]{2,1,0:T(8,128)(2,1)S(1)}, bf16[2,320,320]{2,1,0:T...) custom-call(f32[8,128]{1,0:T(8,128)S(1)} %get-tuple-element.131.flag, ...), custom_call_target="tpu_custom_call" | custom-call | flops 1048576000 | bytes 6434816 | tf_op jit(solution)/shard_map/pallas_call | solution.py:104
  11.2 1.9 %collective-permute-done.refs_1_ = f32[320,128]{1,0:T(8,128)S(1)} collective-permute-done((f32[320,128]{1,0:T(8,128)S(1)}, f32[320,128]{1,0:T(8,128)S(1)}, u32[]{:S(2)}, u32[]{:S(2)}) %collective-permute-start) | collective-permute-done | bytes 163872 | tf_op jit(solution)/shard_map/ppermute | solution.py:578
  13.2 2.9 %collective-permute-done.1.refs_2_ = f32[320,128]{1,0:T(8,128)S(1)} collective-permute-done((f32[320,128]{1,0:T(8,128)S(1)}, f32[320,128]{1,0:T(8,128)S(1)}, u32[]{:S(2)}, u32[]{:S(2)}) %collective-permute-start.1) | collective-permute-done | bytes 163872 | tf_op jit(solution)/shard_map/ppermute | solution.py:578
  16.9 2.6 %collective-permute-start.3 = (f32[160,128]{1,0:T(8,128)S(1)}, f32[160,128]{1,0:T(8,128)S(1)}, u32[]{:S(2)}, u32[]{:S(2)}) collective-permute-start(f32[160,128]{1,0:T(8,128)S(1)} %get-tuple-element.169), channel_id=1, source_target_pairs={{0,16},{4,20},{8,24},{12,28},{16,0},{20,4},{24,8},{28,12},{1,17},{... | collective-permute-start | bytes 245768 | tf_op jit(solution)/shard_map/ppermute | solution.py:578
  20.0 2.5 %collective-permute-start.9 = (f32[160,128]{1,0:T(8,128)S(1)}, f32[160,128]{1,0:T(8,128)S(1)}, u32[]{:S(2)}, u32[]{:S(2)}) collective-permute-start(f32[160,128]{1,0:T(8,128)S(1)} %get-tuple-element.196.refs_0_), channel_id=1, source_target_pairs={{0,12},{4,8},{8,4},{12,0},{16,28},{20,24},{24,20},{28,16},{1,13},{... | collective-permute-start | bytes 245768 | tf_op jit(solution)/shard_map/ppermute | solution.py:578
  24.1 1.6 %collective-permute-start.5 = (f32[160,128]{1,0:T(8,128)S(1)}, f32[160,128]{1,0:T(8,128)S(1)}, u32[]{:S(2)}, u32[]{:S(2)}) collective-permute-start(f32[160,128]{1,0:T(8,128)S(1)} %get-tuple-element.180), channel_id=1, source_target_pairs={{0,3},{1,2},{2,1},{3,0},{4,7},{5,6},{6,5},{7,4},{8,11},{9,10},{10,... | collective-permute-start | bytes 245768 | tf_op jit(solution)/shard_map/ppermute | solution.py:586
  26.2 1.9 %collective-permute-start.11 = (f32[160,128]{1,0:T(8,128)S(1)}, f32[160,128]{1,0:T(8,128)S(1)}, u32[]{:S(2)}, u32[]{:S(2)}) collective-permute-start(f32[160,128]{1,0:T(8,128)S(1)} %get-tuple-element.196.refs_0_), channel_id=1, source_target_pairs={{0,4},{4,0},{8,12},{12,8},{16,20},{20,16},{24,28},{28,24},{1,5},{5... | collective-permute-start | bytes 245768 | tf_op jit(solution)/shard_map/ppermute | solution.py:578
  31.8 1.2 %collective-permute-start.8 = (f32[160,128]{1,0:T(8,128)S(1)}, f32[160,128]{1,0:T(8,128)S(1)}, u32[]{:S(2)}, u32[]{:S(2)}) collective-permute-start(f32[160,128]{1,0:T(8,128)S(1)} %shard_map.99.refs_0_), channel_id=1, source_target_pairs={{0,4},{4,0},{8,12},{12,8},{16,20},{20,16},{24,28},{28,24},{1,5},{5... | collective-permute-start | bytes 245768 | tf_op jit(solution)/shard_map/ppermute | solution.py:578
  37.3 2.8 %collective-permute-start.12 = (f32[160,128]{1,0:T(8,128)S(1)}, f32[160,128]{1,0:T(8,128)S(1)}, u32[]{:S(2)}, u32[]{:S(2)}) collective-permute-start(f32[160,128]{1,0:T(8,128)S(1)} %get-tuple-element.209), channel_id=1, source_target_pairs={{0,16},{4,20},{8,24},{12,28},{16,0},{20,4},{24,8},{28,12},{1,17},{... | collective-permute-start | bytes 245768 | tf_op jit(solution)/shard_map/ppermute | solution.py:578
  41.1 2.9 %collective-permute-done.12.arrived = f32[160,128]{1,0:T(8,128)S(1)} collective-permute-done((f32[160,128]{1,0:T(8,128)S(1)}, f32[160,128]{1,0:T(8,128)S(1)}, u32[]{:S(2)}, u32[]{:S(2)}) %collective-permute-start.12) | collective-permute-done | bytes 81952 | tf_op jit(solution)/shard_map/ppermute | solution.py:578
  44.4 1.6 %collective-permute-start.14 = (f32[160,128]{1,0:T(8,128)S(1)}, f32[160,128]{1,0:T(8,128)S(1)}, u32[]{:S(2)}, u32[]{:S(2)}) collective-permute-start(f32[160,128]{1,0:T(8,128)S(1)} %get-tuple-element.216), channel_id=1, source_target_pairs={{0,3},{1,2},{2,1},{3,0},{4,7},{5,6},{6,5},{7,4},{8,11},{9,10},{10,... | collective-permute-start | bytes 245768 | tf_op jit(solution)/shard_map/ppermute | solution.py:586
  47.0 1.6 %collective-permute-done.14.second.refs_2_ = f32[160,128]{1,0:T(8,128)S(1)} collective-permute-done((f32[160,128]{1,0:T(8,128)S(1)}, f32[160,128]{1,0:T(8,128)S(1)}, u32[]{:S(2)}, u32[]{:S(2)}) %collective-permute-start.14) | collective-permute-done | bytes 81952 | tf_op jit(solution)/shard_map/ppermute | solution.py:586
  49.7 2.4 %collective-permute-start.16 = (f32[160,128]{1,0:T(8,128)S(1)}, f32[160,128]{1,0:T(8,128)S(1)}, u32[]{:S(2)}, u32[]{:S(2)}) collective-permute-start(f32[160,128]{1,0:T(8,128)S(1)} %shard_map.109.refs_0_), channel_id=1, source_target_pairs={{0,8},{4,12},{8,0},{12,4},{16,24},{20,28},{24,16},{28,20},{1,9},{5... | collective-permute-start | bytes 245768 | tf_op jit(solution)/shard_map/ppermute | solution.py:578
  53.8 1.4 %collective-permute-done.15.refs_1_ = f32[160,128]{1,0:T(8,128)S(1)} collective-permute-done((f32[160,128]{1,0:T(8,128)S(1)}, f32[160,128]{1,0:T(8,128)S(1)}, u32[]{:S(2)}, u32[]{:S(2)}) %collective-permute-start.15) | collective-permute-done | bytes 81952 | tf_op jit(solution)/shard_map/ppermute | solution.py:578
  55.1 1.2 %collective-permute-done.16.refs_2_ = f32[160,128]{1,0:T(8,128)S(1)} collective-permute-done((f32[160,128]{1,0:T(8,128)S(1)}, f32[160,128]{1,0:T(8,128)S(1)}, u32[]{:S(2)}, u32[]{:S(2)}) %collective-permute-start.16) | collective-permute-done | bytes 81952 | tf_op jit(solution)/shard_map/ppermute | solution.py:578
  56.9 1.3 %collective-permute-start.18 = (f32[160,128]{1,0:T(8,128)S(1)}, f32[160,128]{1,0:T(8,128)S(1)}, u32[]{:S(2)}, u32[]{:S(2)}) collective-permute-start(f32[160,128]{1,0:T(8,128)S(1)} %get-tuple-element.233), channel_id=1, source_target_pairs={{0,16},{4,20},{8,24},{12,28},{16,0},{20,4},{24,8},{28,12},{1,17},{... | collective-permute-start | bytes 245768 | tf_op jit(solution)/shard_map/ppermute | solution.py:578
  59.0 4.1 %collective-permute-done.18.arrived = f32[160,128]{1,0:T(8,128)S(1)} collective-permute-done((f32[160,128]{1,0:T(8,128)S(1)}, f32[160,128]{1,0:T(8,128)S(1)}, u32[]{:S(2)}, u32[]{:S(2)}) %collective-permute-start.18) | collective-permute-done | bytes 81952 | tf_op jit(solution)/shard_map/ppermute | solution.py:578
  63.6 1.9 %collective-permute-start.20 = (f32[160,128]{1,0:T(8,128)S(1)}, f32[160,128]{1,0:T(8,128)S(1)}, u32[]{:S(2)}, u32[]{:S(2)}) collective-permute-start(f32[160,128]{1,0:T(8,128)S(1)} %get-tuple-element.238), channel_id=1, source_target_pairs={{0,3},{1,2},{2,1},{3,0},{4,7},{5,6},{6,5},{7,4},{8,11},{9,10},{10,... | collective-permute-start | bytes 245768 | tf_op jit(solution)/shard_map/ppermute | solution.py:586
  66.6 1.5 %collective-permute-done.20.second.refs_2_ = f32[160,128]{1,0:T(8,128)S(1)} collective-permute-done((f32[160,128]{1,0:T(8,128)S(1)}, f32[160,128]{1,0:T(8,128)S(1)}, u32[]{:S(2)}, u32[]{:S(2)}) %collective-permute-start.20) | collective-permute-done | bytes 81952 | tf_op jit(solution)/shard_map/ppermute | solution.py:586
  68.6 2.7 %collective-permute-start.22 = (f32[160,128]{1,0:T(8,128)S(1)}, f32[160,128]{1,0:T(8,128)S(1)}, u32[]{:S(2)}, u32[]{:S(2)}) collective-permute-start(f32[160,128]{1,0:T(8,128)S(1)} %shard_map.117.refs_0_), channel_id=1, source_target_pairs={{0,8},{4,12},{8,0},{12,4},{16,24},{20,28},{24,16},{28,20},{1,9},{5... | collective-permute-start | bytes 245768 | tf_op jit(solution)/shard_map/ppermute | solution.py:578
  72.9 1.6 %collective-permute-done.21.refs_1_ = f32[160,128]{1,0:T(8,128)S(1)} collective-permute-done((f32[160,128]{1,0:T(8,128)S(1)}, f32[160,128]{1,0:T(8,128)S(1)}, u32[]{:S(2)}, u32[]{:S(2)}) %collective-permute-start.21) | collective-permute-done | bytes 81952 | tf_op jit(solution)/shard_map/ppermute | solution.py:578
  78.3 4.2 %collective-permute-done.24.arrived = f32[160,128]{1,0:T(8,128)S(1)} collective-permute-done((f32[160,128]{1,0:T(8,128)S(1)}, f32[160,128]{1,0:T(8,128)S(1)}, u32[]{:S(2)}, u32[]{:S(2)}) %collective-permute-start.24) | collective-permute-done | bytes 81952 | tf_op jit(solution)/shard_map/ppermute | solution.py:578
  (62 shorter events, 26.7 us)
Async XLA Ops:
  4.1 9.0 %collective-permute-start = (f32[320,128]{1,0:T(8,128)S(1)}, f32[320,128]{1,0:T(8,128)S(1)}, u32[]{:S(2)}, u32[]{:S(2)}) collective-permute-start(f32[320,128]{1,0:T(8,128)S(1)} %get-tuple-element.153.refs_0_), channel_id=1, source_target_pairs={{0,12},{4,8},{8,4},{12,0},{16,28},{20,24},{24,20},{28,16},{1,13},{... | collective-permute-start | bytes 491528 | tf_op jit(solution)/shard_map/ppermute | solution.py:578
  8.1 8.0 %collective-permute-start.1 = (f32[320,128]{1,0:T(8,128)S(1)}, f32[320,128]{1,0:T(8,128)S(1)}, u32[]{:S(2)}, u32[]{:S(2)}) collective-permute-start(f32[320,128]{1,0:T(8,128)S(1)} %get-tuple-element.153.refs_0_), channel_id=1, source_target_pairs={{0,8},{4,12},{8,0},{12,4},{16,24},{20,28},{24,16},{28,20},{1,9},{5... | collective-permute-start | bytes 491528 | tf_op jit(solution)/shard_map/ppermute | solution.py:578
  8.6 7.5 %collective-permute-start.2 = (f32[320,128]{1,0:T(8,128)S(1)}, f32[320,128]{1,0:T(8,128)S(1)}, u32[]{:S(2)}, u32[]{:S(2)}) collective-permute-start(f32[320,128]{1,0:T(8,128)S(1)} %get-tuple-element.153.refs_0_), channel_id=1, source_target_pairs={{0,4},{4,0},{8,12},{12,8},{16,20},{20,16},{24,28},{28,24},{1,5},{5... | collective-permute-start | bytes 491528 | tf_op jit(solution)/shard_map/ppermute | solution.py:578
  16.9 6.8 %collective-permute-start.3 = (f32[160,128]{1,0:T(8,128)S(1)}, f32[160,128]{1,0:T(8,128)S(1)}, u32[]{:S(2)}, u32[]{:S(2)}) collective-permute-start(f32[160,128]{1,0:T(8,128)S(1)} %get-tuple-element.169), channel_id=1, source_target_pairs={{0,16},{4,20},{8,24},{12,28},{16,0},{20,4},{24,8},{28,12},{1,17},{... | collective-permute-start | bytes 245768 | tf_op jit(solution)/shard_map/ppermute | solution.py:578
  20.0 11.8 %collective-permute-start.9 = (f32[160,128]{1,0:T(8,128)S(1)}, f32[160,128]{1,0:T(8,128)S(1)}, u32[]{:S(2)}, u32[]{:S(2)}) collective-permute-start(f32[160,128]{1,0:T(8,128)S(1)} %get-tuple-element.196.refs_0_), channel_id=1, source_target_pairs={{0,12},{4,8},{8,4},{12,0},{16,28},{20,24},{24,20},{28,16},{1,13},{... | collective-permute-start | bytes 245768 | tf_op jit(solution)/shard_map/ppermute | solution.py:578
  24.0 5.2 %collective-permute-start.4 = (f32[160,128]{1,0:T(8,128)S(1)}, f32[160,128]{1,0:T(8,128)S(1)}, u32[]{:S(2)}, u32[]{:S(2)}) collective-permute-start(f32[160,128]{1,0:T(8,128)S(1)} %get-tuple-element.179), channel_id=1, source_target_pairs={{0,1},{1,0},{2,3},{3,2},{4,5},{5,4},{6,7},{7,6},{8,9},{9,8},{10,11... | collective-permute-start | bytes 245768 | tf_op jit(solution)/shard_map/ppermute | solution.py:587
  24.1 5.1 %collective-permute-start.5 = (f32[160,128]{1,0:T(8,128)S(1)}, f32[160,128]{1,0:T(8,128)S(1)}, u32[]{:S(2)}, u32[]{:S(2)}) collective-permute-start(f32[160,128]{1,0:T(8,128)S(1)} %get-tuple-element.180), channel_id=1, source_target_pairs={{0,3},{1,2},{2,1},{3,0},{4,7},{5,6},{6,5},{7,4},{8,11},{9,10},{10,... | collective-permute-start | bytes 245768 | tf_op jit(solution)/shard_map/ppermute | solution.py:586
  25.7 8.5 %collective-permute-start.10 = (f32[160,128]{1,0:T(8,128)S(1)}, f32[160,128]{1,0:T(8,128)S(1)}, u32[]{:S(2)}, u32[]{:S(2)}) collective-permute-start(f32[160,128]{1,0:T(8,128)S(1)} %get-tuple-element.196.refs_0_), channel_id=1, source_target_pairs={{0,8},{4,12},{8,0},{12,4},{16,24},{20,28},{24,16},{28,20},{1,9},{5... | collective-permute-start | bytes 245768 | tf_op jit(solution)/shard_map/ppermute | solution.py:578
  26.2 7.9 %collective-permute-start.11 = (f32[160,128]{1,0:T(8,128)S(1)}, f32[160,128]{1,0:T(8,128)S(1)}, u32[]{:S(2)}, u32[]{:S(2)}) collective-permute-start(f32[160,128]{1,0:T(8,128)S(1)} %get-tuple-element.196.refs_0_), channel_id=1, source_target_pairs={{0,4},{4,0},{8,12},{12,8},{16,20},{20,16},{24,28},{28,24},{1,5},{5... | collective-permute-start | bytes 245768 | tf_op jit(solution)/shard_map/ppermute | solution.py:578
  29.4 5.9 %collective-permute-start.6 = (f32[160,128]{1,0:T(8,128)S(1)}, f32[160,128]{1,0:T(8,128)S(1)}, u32[]{:S(2)}, u32[]{:S(2)}) collective-permute-start(f32[160,128]{1,0:T(8,128)S(1)} %shard_map.99.refs_0_), channel_id=1, source_target_pairs={{0,12},{4,8},{8,4},{12,0},{16,28},{20,24},{24,20},{28,16},{1,13},{... | collective-permute-start | bytes 245768 | tf_op jit(solution)/shard_map/ppermute | solution.py:578
  30.6 5.6 %collective-permute-start.7 = (f32[160,128]{1,0:T(8,128)S(1)}, f32[160,128]{1,0:T(8,128)S(1)}, u32[]{:S(2)}, u32[]{:S(2)}) collective-permute-start(f32[160,128]{1,0:T(8,128)S(1)} %shard_map.99.refs_0_), channel_id=1, source_target_pairs={{0,8},{4,12},{8,0},{12,4},{16,24},{20,28},{24,16},{28,20},{1,9},{5... | collective-permute-start | bytes 245768 | tf_op jit(solution)/shard_map/ppermute | solution.py:578
  31.8 4.9 %collective-permute-start.8 = (f32[160,128]{1,0:T(8,128)S(1)}, f32[160,128]{1,0:T(8,128)S(1)}, u32[]{:S(2)}, u32[]{:S(2)}) collective-permute-start(f32[160,128]{1,0:T(8,128)S(1)} %shard_map.99.refs_0_), channel_id=1, source_target_pairs={{0,4},{4,0},{8,12},{12,8},{16,20},{20,16},{24,28},{28,24},{1,5},{5... | collective-permute-start | bytes 245768 | tf_op jit(solution)/shard_map/ppermute | solution.py:578
  37.3 6.7 %collective-permute-start.12 = (f32[160,128]{1,0:T(8,128)S(1)}, f32[160,128]{1,0:T(8,128)S(1)}, u32[]{:S(2)}, u32[]{:S(2)}) collective-permute-start(f32[160,128]{1,0:T(8,128)S(1)} %get-tuple-element.209), channel_id=1, source_target_pairs={{0,16},{4,20},{8,24},{12,28},{16,0},{20,4},{24,8},{28,12},{1,17},{... | collective-permute-start | bytes 245768 | tf_op jit(solution)/shard_map/ppermute | solution.py:578
  44.4 4.2 %collective-permute-start.14 = (f32[160,128]{1,0:T(8,128)S(1)}, f32[160,128]{1,0:T(8,128)S(1)}, u32[]{:S(2)}, u32[]{:S(2)}) collective-permute-start(f32[160,128]{1,0:T(8,128)S(1)} %get-tuple-element.216), channel_id=1, source_target_pairs={{0,3},{1,2},{2,1},{3,0},{4,7},{5,6},{6,5},{7,4},{8,11},{9,10},{10,... | collective-permute-start | bytes 245768 | tf_op jit(solution)/shard_map/ppermute | solution.py:586
  48.9 6.3 %collective-permute-start.15 = (f32[160,128]{1,0:T(8,128)S(1)}, f32[160,128]{1,0:T(8,128)S(1)}, u32[]{:S(2)}, u32[]{:S(2)}) collective-permute-start(f32[160,128]{1,0:T(8,128)S(1)} %shard_map.109.refs_0_), channel_id=1, source_target_pairs={{0,12},{4,8},{8,4},{12,0},{16,28},{20,24},{24,20},{28,16},{1,13},{... | collective-permute-start | bytes 245768 | tf_op jit(solution)/shard_map/ppermute | solution.py:578
  49.7 6.6 %collective-permute-start.16 = (f32[160,128]{1,0:T(8,128)S(1)}, f32[160,128]{1,0:T(8,128)S(1)}, u32[]{:S(2)}, u32[]{:S(2)}) collective-permute-start(f32[160,128]{1,0:T(8,128)S(1)} %shard_map.109.refs_0_), channel_id=1, source_target_pairs={{0,8},{4,12},{8,0},{12,4},{16,24},{20,28},{24,16},{28,20},{1,9},{5... | collective-permute-start | bytes 245768 | tf_op jit(solution)/shard_map/ppermute | solution.py:578
  52.1 4.4 %collective-permute-start.17 = (f32[160,128]{1,0:T(8,128)S(1)}, f32[160,128]{1,0:T(8,128)S(1)}, u32[]{:S(2)}, u32[]{:S(2)}) collective-permute-start(f32[160,128]{1,0:T(8,128)S(1)} %shard_map.109.refs_0_), channel_id=1, source_target_pairs={{0,4},{4,0},{8,12},{12,8},{16,20},{20,16},{24,28},{28,24},{1,5},{5... | collective-permute-start | bytes 245768 | tf_op jit(solution)/shard_map/ppermute | solution.py:578
  56.9 6.3 %collective-permute-start.18 = (f32[160,128]{1,0:T(8,128)S(1)}, f32[160,128]{1,0:T(8,128)S(1)}, u32[]{:S(2)}, u32[]{:S(2)}) collective-permute-start(f32[160,128]{1,0:T(8,128)S(1)} %get-tuple-element.233), channel_id=1, source_target_pairs={{0,16},{4,20},{8,24},{12,28},{16,0},{20,4},{24,8},{28,12},{1,17},{... | collective-permute-start | bytes 245768 | tf_op jit(solution)/shard_map/ppermute | solution.py:578
  63.5 3.1 %collective-permute-start.19 = (f32[160,128]{1,0:T(8,128)S(1)}, f32[160,128]{1,0:T(8,128)S(1)}, u32[]{:S(2)}, u32[]{:S(2)}) collective-permute-start(f32[160,128]{1,0:T(8,128)S(1)} %get-tuple-element.237), channel_id=1, source_target_pairs={{0,1},{1,0},{2,3},{3,2},{4,5},{5,4},{6,7},{7,6},{8,9},{9,8},{10,11... | collective-permute-start | bytes 245768 | tf_op jit(solution)/shard_map/ppermute | solution.py:587
  63.6 4.5 %collective-permute-start.20 = (f32[160,128]{1,0:T(8,128)S(1)}, f32[160,128]{1,0:T(8,128)S(1)}, u32[]{:S(2)}, u32[]{:S(2)}) collective-permute-start(f32[160,128]{1,0:T(8,128)S(1)} %get-tuple-element.238), channel_id=1, source_target_pairs={{0,3},{1,2},{2,1},{3,0},{4,7},{5,6},{6,5},{7,4},{8,11},{9,10},{10,... | collective-permute-start | bytes 245768 | tf_op jit(solution)/shard_map/ppermute | solution.py:586
  68.3 6.2 %collective-permute-start.21 = (f32[160,128]{1,0:T(8,128)S(1)}, f32[160,128]{1,0:T(8,128)S(1)}, u32[]{:S(2)}, u32[]{:S(2)}) collective-permute-start(f32[160,128]{1,0:T(8,128)S(1)} %shard_map.117.refs_0_), channel_id=1, source_target_pairs={{0,12},{4,8},{8,4},{12,0},{16,28},{20,24},{24,20},{28,16},{1,13},{... | collective-permute-start | bytes 245768 | tf_op jit(solution)/shard_map/ppermute | solution.py:578
  68.6 7.0 %collective-permute-start.22 = (f32[160,128]{1,0:T(8,128)S(1)}, f32[160,128]{1,0:T(8,128)S(1)}, u32[]{:S(2)}, u32[]{:S(2)}) collective-permute-start(f32[160,128]{1,0:T(8,128)S(1)} %shard_map.117.refs_0_), channel_id=1, source_target_pairs={{0,8},{4,12},{8,0},{12,4},{16,24},{20,28},{24,16},{28,20},{1,9},{5... | collective-permute-start | bytes 245768 | tf_op jit(solution)/shard_map/ppermute | solution.py:578
  71.3 4.5 %collective-permute-start.23 = (f32[160,128]{1,0:T(8,128)S(1)}, f32[160,128]{1,0:T(8,128)S(1)}, u32[]{:S(2)}, u32[]{:S(2)}) collective-permute-start(f32[160,128]{1,0:T(8,128)S(1)} %shard_map.117.refs_0_), channel_id=1, source_target_pairs={{0,4},{4,0},{8,12},{12,8},{16,20},{20,16},{24,28},{28,24},{1,5},{5... | collective-permute-start | bytes 245768 | tf_op jit(solution)/shard_map/ppermute | solution.py:578
  76.1 6.3 %collective-permute-start.24 = (f32[160,128]{1,0:T(8,128)S(1)}, f32[160,128]{1,0:T(8,128)S(1)}, u32[]{:S(2)}, u32[]{:S(2)}) collective-permute-start(f32[160,128]{1,0:T(8,128)S(1)} %get-tuple-element.256), channel_id=1, source_target_pairs={{0,16},{4,20},{8,24},{12,28},{16,0},{20,4},{24,8},{28,12},{1,17},{... | collective-permute-start | bytes 245768 | tf_op jit(solution)/shard_map/ppermute | solution.py:578
  (1 other events, 2.7 us)

commit v4 on v3

--- a/solution.py
+++ b/solution.py
@@ -128,89 +128,72 @@
     return map_times(face(high, q, f, count), face(low, q, f, count), x)
 
 
-def joined_coupling(blocks, flags, q):
-    total = None
-    for m in range(blocks.shape[1]):
-        present = flags[2 + q * blocks.shape[1] + m : 3 + q * blocks.shape[1] + m, 0:1]
-        block = blocks[q, m].astype(F32) * present
-        total = block if total is None else total + block
-    return two(total)
+def times_exact(x, operator):
+    n = x.shape[0]
+    both = mm(jnp.concatenate(two(x), axis=0), operator)
+    return both[:n] + both[n:]
 
 
 def first_kernel(order_in, count_in, links_in, types_in, rhs_in, inverse_in, table_in, traces_in,
-                 lifts_in, packed, flags, inverse, blocks, traces, lifts, rhs, now, response,
-                 held, order, count, links, types, small, large, table_sems):
-    faces = blocks.shape[1]
-    width = traces.shape[1]
+                 lifts_in, packed, flags, inverse, blocks, trace, head, rhs, order, count, links,
+                 types, small, large, own):
+    faces = blocks.shape[0]
+    width = trace.shape[0]
+    columns = rhs.shape[2]
     scalars = [
         pltpu.make_async_copy(a, b, small.at[i])
         for i, (a, b) in enumerate(
             ((order_in, order), (types_in, types), (links_in, links), (count_in, count))
         )
     ]
-    for c in scalars:
+    pairs = [
+        (traces_in.at[1], trace),
+        (inverse_in, inverse),
+        (lifts_in.at[0], head.at[pl.ds(0, width), :]),
+        (rhs_in, rhs),
+    ]
+    copies = [pltpu.make_async_copy(a, b, large.at[i]) for i, (a, b) in enumerate(pairs)]
+    for c in scalars + copies:
         c.start()
-    pairs = [(inverse_in, held), (rhs_in, rhs), (traces_in, traces)]
-    for f in range(lifts_in.shape[0]):
-        pairs.append((lifts_in.at[f], lifts.at[pl.ds(f * LANES, width), :]))
-    copies = [pltpu.make_async_copy(a, b, large.at[i]) for i, (a, b) in enumerate(pairs)]
-    for c in copies:
-        c.start()
-    for f in range(lifts_in.shape[0]):
-        gap = lifts.at[pl.ds(f * LANES + width, LANES - width), :]
-        gap[...] = jnp.zeros(gap.shape, BF16)
+    gap = head.at[pl.ds(width, LANES - width), :]
+    gap[...] = jnp.zeros(gap.shape, BF16)
+    flags[...] = jnp.zeros_like(flags)
     for c in scalars:
         c.wait()
-    fetched = {}
-    for q in (1, 0):
-        for m in range(faces):
-            c = pltpu.make_async_copy(
-                table_in.at[types[order[q], m]], blocks.at[q, m], table_sems.at[q * faces + m]
-            )
-            c.start()
-            fetched[q, m] = c
     a, b = order[0], order[1]
+    fetched = [
+        pltpu.make_async_copy(table_in.at[types[b, m]], blocks.at[m], own.at[m])
+        for m in range(faces)
+    ]
+    for c in fetched:
+        c.start()
     alive = (count[0] > 1).astype(F32)
-    flags[...] = jnp.zeros_like(flags)
     flags[0:1, :] = jnp.full((1, LANES), (a == 0).astype(F32))
     flags[1:2, :] = jnp.full((1, LANES), alive)
-    for q in (0, 1):
+    for q, s in enumerate((a, b)):
         for m in range(faces):
             row = 2 + q * faces + m
-            present = (links[order[q], m] < 2).astype(F32)
-            flags[row : row + 1, :] = jnp.full((1, LANES), present)
+            flags[row : row + 1, :] = jnp.full((1, LANES), (links[s, m] < 2).astype(F32))
     for c in copies:
         c.wait()
-    inverse[0] = held[a]
-    inverse[1] = held[b] * alive.astype(BF16)
-    head = lifts[0:LANES, :]
-    now[0] = exact_times(inverse[0], rhs[a])
-    response[0] = mm_t(inverse[0], head)
-    response[2] = mm_t(inverse[1], head)
+    far = mm(trace[...], inverse[b]) * alive
+    start = jnp.concatenate([exact_times(inverse[a], rhs[a]), mm_t(inverse[a], head[...])], axis=1)
+    near = exact_times(trace[...], start)
+    packed[pl.ds(pl.multiple_of(a * width, 8), width), :] = near[:, :columns]
+    far_high, far_low = two(far)
+    lifted = mm_t(far_high, head[...]) + mm_t(far_low, head[...])
+    shown = map_times(far_high, far_low, rhs[b])
+    met = None
     for m in range(faces):
-        fetched[1, m].wait()
-    high, low = joined_coupling(blocks, flags, 1)
-    met = map_times(high, low, jnp.concatenate([now[0], response[0]], axis=1))
-    columns = now.shape[2]
-    rest = jnp.concatenate([rhs[b] - met[:, :columns], met[:, columns:]], axis=1)
-    rest = exact_times(inverse[1], rest)
-    now[1] = rest[:, :columns]
-    response[1] = rest[:, columns:]
-    shown = exact_times(traces[1], jnp.concatenate([now[0], response[0]], axis=1))
-    packed[pl.ds(pl.multiple_of(a * width, 8), width), :] = shown[:, :columns]
-    after = jnp.concatenate([now[1], response[1], response[2]], axis=1)
-    after = exact_times(traces[1], after)
-    packed[pl.ds(pl.multiple_of(b * width, 8), width), :] = after[:, :columns]
-    one, rest = pack_map(
-        -shown[:, columns:],
-        -after[:, columns + LANES :],
-        after[:, columns : columns + LANES],
-        flags[0:1, :],
-    )
+        fetched[m].wait()
+        product = times_exact(far, blocks[m]) * (links[b, m] < 2).astype(F32)
+        met = product if met is None else met + product
+    met_high, met_low = two(met)
+    met = map_times(met_high, met_low, start)
+    packed[pl.ds(pl.multiple_of(b * width, 8), width), :] = shown - met[:, :columns]
+    one, rest = pack_map(-near[:, columns:], -lifted, met[:, columns:], flags[0:1, :])
     packed[2 * width : 3 * width, :] = one
     packed[3 * width : 4 * width, :] = rest
-    for m in range(faces):
-        fetched[0, m].wait()
 
 
 def side_traces(out, traces, flag, first, second):
@@ -244,20 +227,62 @@
             high[place, held], low[place, held] = two(rows[s])
 
 
-def maps_kernel(flags, inverse, blocks, traces, lifts, rhs, now, response,
-                z, d_high, d_low, e_high, e_low, side, side_high, side_low, back_map,
-                q_high, q_low, last_high, last_low):
+def maps_kernel(order_in, types_in, rhs_in, inverse_in, table_in, traces_in, lifts_in, flags,
+                traces, z, d_high, d_low, e_high, e_low, side, side_high, side_low, back_map,
+                q_high, q_low, last_high, last_low,
+                inverse, rhs, lifts, blocks, order, types, small, large):
+    width = traces.shape[1]
+    links = blocks.shape[1]
+    pairs = [(inverse_in, inverse), (rhs_in, rhs), (traces_in, traces)]
+    for f in range(lifts_in.shape[0]):
+        pairs.append((lifts_in.at[f], lifts.at[pl.ds(f * LANES, width), :]))
+    scalars = [
+        pltpu.make_async_copy(order_in, order, small.at[0]),
+        pltpu.make_async_copy(types_in, types, small.at[1]),
+    ]
+    copies = [pltpu.make_async_copy(a, b, large.at[i]) for i, (a, b) in enumerate(pairs)]
+    for c in scalars + copies:
+        c.start()
+    for f in range(lifts_in.shape[0]):
+        gap = lifts.at[pl.ds(f * LANES + width, LANES - width), :]
+        gap[...] = jnp.zeros(gap.shape, BF16)
+    for c in scalars:
+        c.wait()
+    own = [
+        pltpu.make_async_copy(
+            table_in.at[types[order[q], m]], blocks.at[q, m], large.at[len(pairs) + q * links + m]
+        )
+        for q in (0, 1)
+        for m in range(links)
+    ]
+    for c in own:
+        c.start()
+    for c in copies + own:
+        c.wait()
     flag = flags[0:1, :] > 0.5
-    side_traces(side, traces, flag, now[0], now[1])
+    for q in (0, 1):
+        s = order[q]
+        scale = flags[1:2, 0:1] if q else 1.0
+        z[q] = exact_times(inverse[s], rhs[s]) * scale
+        d_high[q], d_low[q] = two(mm_t(inverse[s], lifts[...]) * scale)
+        total = None
+        for m in range(links):
+            row = 2 + q * links + m
+            block = blocks[q, m].astype(F32) * flags[row : row + 1, 0:1]
+            total = block if total is None else total + block
+        high, low = two(total)
+        e_high[q], e_low[q] = two((mm(inverse[s], high) + mm(inverse[s], low)) * scale)
+
+    def lift_of(q):
+        return face(d_high, q, 0).astype(F32) + face(d_low, q, 0).astype(F32)
+
+    n = z.shape[2]
+    met = jnp.concatenate([z[0], lift_of(0)], axis=1)
+    met = map_times(e_high[1], e_low[1], met)
+    side_traces(side, traces, flag, z[0], z[1] - met[:, :n])
     store_side_map(
-        side_high, side_low, traces, flag, response[0], response[2], response[1], False
-    )
-    z[0] = now[0]
-    z[1] = exact_times(inverse[1], pick(flag, rhs[1], rhs[0]))
-    for q in (0, 1):
-        d_high[q], d_low[q] = two(mm_t(inverse[q], lifts[...]))
-        high, low = joined_coupling(blocks, flags, q)
-        e_high[q], e_low[q] = two(mm(inverse[q], high) + mm(inverse[q], low))
+        side_high, side_low, traces, flag, lift_of(0), lift_of(1), met[:, n:], False
+    )
     faces = lifts.shape[0] // LANES - 1
     high, low = face(d_high, 1, 1, faces), face(d_low, 1, 1, faces)
     both = mm(e_high[0], jnp.concatenate([high, low], axis=1))
@@ -270,7 +295,6 @@
             mm(traces[0], face(d_high, q, 1, faces)) + mm(traces[0], face(d_low, q, 1, faces))
         )
     shown.append(exact_times(traces[0], across))
-    width = traces.shape[1]
     one, rest = pack_map(
         -shown[0][:, :LANES], -shown[1][:, :LANES], shown[2][:, :LANES], flags[0:1, :]
     )
@@ -607,46 +631,52 @@
     field, trace = shape(block, columns), shape(rows, columns)
     unit = 2 * block * block * LANES
     hbm = pl.BlockSpec(memory_space=pl.ANY)
-    ins = (order[0, 0], counts[0], neighbours[0, 0], face_ids[0, 0], source, inverse_in, coupling,
+    given = (order[0, 0], counts[0], neighbours[0, 0], face_ids[0, 0], source, inverse_in, coupling,
            trace_ops, jnp.swapaxes(lift_ops, 1, 2))
-    ins = tuple(
-        x if x.size == 1 else pltpu.with_memory_space_constraint(x, pltpu.HBM) for x in ins
-    )
-    packed, flags, inverse, blocks, traces, lifts, held_rhs, now, response = call(
+    inputs = tuple(
+        x if x.size == 1 else pltpu.with_memory_space_constraint(x, pltpu.HBM) for x in given
+    )
+    packed, flags = call(
         first_kernel,
-        [
-            shape(2 * rows, LANES),
-            shape(8 * -(-(2 + 2 * links) // 8), LANES),
-            shape(2, block, block, dtype=BF16),
-            shape(2, links, block, block, dtype=BF16),
-            shape(faces, width, block, dtype=BF16),
-            shape(faces * LANES, block, dtype=BF16),
-            shape(2, block, columns),
-            shape(2, block, columns),
-            shape(3, block, LANES),
-        ],
-        ins,
+        [shape(2 * rows, LANES), shape(8 * -(-(2 + 2 * links) // 8), LANES)],
+        inputs,
         20 * unit,
         [
             pltpu.VMEM((2, block, block), BF16),
-            *(pltpu.SMEM(x.shape, jnp.int32) for x in ins[:4]),
+            pltpu.VMEM((links, block, block), BF16),
+            pltpu.VMEM((width, block), BF16),
+            pltpu.VMEM((LANES, block), BF16),
+            pltpu.VMEM((2, block, columns), F32),
+            *(pltpu.SMEM(x.shape, jnp.int32) for x in inputs[:4]),
             pltpu.SemaphoreType.DMA((4,)),
-            pltpu.SemaphoreType.DMA((3 + faces,)),
-            pltpu.SemaphoreType.DMA((2 * links,)),
+            pltpu.SemaphoreType.DMA((4,)),
+            pltpu.SemaphoreType.DMA((links,)),
         ],
-        [hbm] * len(ins),
+        [hbm] * len(inputs),
     )
     table, square = pair(2, block, faces * LANES), pair(2, block, block)
     side_pair, line_pair = pair(2 * rows, 2 * LANES), pair(rows, 4 * LANES)
     store = {}
 
     def maps():
+        held = (inputs[0], *inputs[3:])
         return call(
             maps_kernel,
-            [shape(2, block, columns), *table, *square, shape(2, rows, columns), *side_pair,
-             shape(rows, LANES), *line_pair, *pair(block, LANES)],
-            (flags, inverse, blocks, traces, lifts, held_rhs, now, response),
-            40 * unit,
+            [shape(*trace_ops.shape, dtype=BF16), shape(2, block, columns), *table, *square,
+             shape(2, rows, columns), *side_pair, shape(rows, LANES), *line_pair,
+             *pair(block, LANES)],
+            (*held, flags),
+            50 * unit,
+            [
+                pltpu.VMEM((2, block, block), BF16),
+                pltpu.VMEM((2, block, columns), F32),
+                pltpu.VMEM((faces * LANES, block), BF16),
+                pltpu.VMEM((2, links, block, block), BF16),
+                *(pltpu.SMEM(x.shape, jnp.int32) for x in held[:2]),
+                pltpu.SemaphoreType.DMA((2,)),
+                pltpu.SemaphoreType.DMA((3 + faces + 2 * links,)),
+            ],
+            [hbm] * len(held) + [pl.BlockSpec(memory_space=pltpu.VMEM)],
         )
 
     def more_maps():
@@ -739,10 +769,11 @@
         final = number == len(halves) - 1
         if number == 0:
             befores, passes, arrived, stride, done = carried(packed, backward, maps)
+            traces, *done = done
             store["z"], store["d"], store["e"], side = done[0], done[1:3], done[3:5], done[5]
             store["side", False], store["line", True] = done[6:8], done[9:11]
             store["last"] = done[11:13]
-            line = now[0]
+            line = store["z"][0]
             if grouped:
                 sent = send_maps(done[8])
         else:
@@ -767,6 +798,7 @@
 
             if number == 1 and grouped:
                 take_maps(sent)
+                store.update(suffixes(True))
             befores, passes, arrived, stride, done = carried(outflow, backward, beside)
             line, side = done[0]
             store.update(done[1])
@@ -784,8 +816,8 @@
             body = partial(last_kernel, stride, backward)
             (x,) = call(body, [shape(2, block, columns)], (base, *far, arrived), 2 * unit)
             break
-        if number < 2:
-            store.update(suffixes(backward))
+        if number == 0:
+            store.update(suffixes(False))
         if ("join", backward) not in store:
             ins = (*store["side", backward], *passes)
             body = partial(join_kernel, depth)

time: 83.7 us -> 82.4 us (0.984)
  starting transfers between devices: 33.3 us -> 30.4 us
  Pallas kernels: 22.3 us -> 25 us
  waiting for transfers between devices: 27 us -> 25.9 us
    ppermute x19, waiting for transfers between devices: 23.9 us -> 21.2 us  [exchange(): return lax.ppermute(block, axis, pairs)]
    pallas_call x35 -> x36, Pallas kernels: 22.3 us -> 25 us  [call(): pl.pallas_call(body, out_shape=list(outs), in_specs=spaces or [vmem] * le...]
    ppermute x19, starting transfers between devices: 27.9 us -> 25.3 us  [exchange(): return lax.ppermute(block, axis, pairs)]
    ppermute x3, waiting for transfers between devices: 3.09 us -> 4.65 us  [side_exchange(): second = lax.ppermute(second, 'span', across)]
  transfers between devices with their start and end apart: 25 -> 25, of which waited for: 17 -> 14; matrix products, arithmetic and copies ran while one was open for 0% -> 0% of each run, Pallas kernels for 18% -> 22%
where the time goes in v4:
time: 82.4 us; the launch traced here: 82.2 us
  starting transfers between devices  30.4 us (37%)
  waiting for transfers between devices  25.9 us (31%)
  Pallas kernels  25 us (30%)
  between operations  0.98 us (1%)
    ppermute x19, starting transfers between devices, exchange(): return lax.ppermute(block, axis, pairs)  25.3 us
    pallas_call x36, Pallas kernels, call(): pl.pallas_call(body, out_shape=list(outs), in_specs=spaces or [vmem] * le...  25 us
    ppermute x19, waiting for transfers between devices, exchange(): return lax.ppermute(block, axis, pairs)  21.2 us
    ppermute x3, starting transfers between devices, side_exchange(): second = lax.ppermute(second, 'span', across)  4.91 us
    ppermute x3, waiting for transfers between devices, side_exchange(): second = lax.ppermute(second, 'span', across)  4.65 us
  transfers between devices with their start and end apart: 25, of which 14 were waited for; matrix products, arithmetic and copies ran while one was open for 0% of the time, Pallas kernels for 22%

profile of v4, /device:TPU:0, one launch (start us, length us, event | category | flops | bytes accessed | tf_op | source)
XLA Modules:
  0.0 82.2 jit_solution(11492798136253257851)
XLA Ops:
  0.7 2.8 %shard_map.91 = (f32[320,128]{1,0:T(8,128)S(1)}, f32[8,128]{1,0:T(8,128)S(1)}) custom-call(s32[2]{0:T(128)} %bitcast.20, s32[1]{0:T(128)} %bitcast.10.count_in, s32[2,2]{1,0:T(2,128)} %bitcast.17, s32[2,2]{1,0:T(2,128)} %bitcast.18, f32[2,320,128]{2,1,0:T(8,128)} %bitcast.13, bf16[2,320,320]{2,1,0:T(8,128)(2,1)} %bitcast.11, bf16[6,320,320]{2,1,0:T(8,128)(2,1)} %table_in.3, ...), custom_call_target="tpu_custom_call" | custom-call | flops 524288000 | bytes 2543660 | tf_op jit(solution)/shard_map/pallas_call | solution.py:104
  3.5 4.0 %collective-permute-start = (f32[320,128]{1,0:T(8,128)S(1)}, f32[320,128]{1,0:T(8,128)S(1)}, u32[]{:S(2)}, u32[]{:S(2)}) collective-permute-start(f32[320,128]{1,0:T(8,128)S(1)} %get-tuple-element.142.refs_0_), channel_id=1, source_target_pairs={{0,12},{4,8},{8,4},{12,0},{16,28},{20,24},{24,20},{28,16},{1,13},{... | collective-permute-start | bytes 491528 | tf_op jit(solution)/shard_map/ppermute | solution.py:602
  8.1 5.6 %shard_map.92 = (bf16[4,80,320]{2,1,0:T(8,128)(2,1)S(1)}, f32[2,320,128]{2,1,0:T(8,128)S(1)}, bf16[2,320,512]{2,1,0:T(8,128)(2,1)S(1)}, bf16[2,320,512]{2,1,0:T(...) custom-call(s32[2]{0:T(128)} %bitcast.21, ...), custom_call_target="tpu_custom_call" | custom-call | flops 1310720000 | bytes 6107160 | tf_op jit(solution)/shard_map/pallas_call | solution.py:104
  13.7 1.7 %collective-permute-done.1.refs_2_ = f32[320,128]{1,0:T(8,128)S(1)} collective-permute-done((f32[320,128]{1,0:T(8,128)S(1)}, f32[320,128]{1,0:T(8,128)S(1)}, u32[]{:S(2)}, u32[]{:S(2)}) %collective-permute-start.1) | collective-permute-done | bytes 163872 | tf_op jit(solution)/shard_map/ppermute | solution.py:602
  16.2 2.6 %collective-permute-start.3 = (f32[160,128]{1,0:T(8,128)S(1)}, f32[160,128]{1,0:T(8,128)S(1)}, u32[]{:S(2)}, u32[]{:S(2)}) collective-permute-start(f32[160,128]{1,0:T(8,128)S(1)} %get-tuple-element.158), channel_id=1, source_target_pairs={{0,16},{4,20},{8,24},{12,28},{16,0},{20,4},{24,8},{28,12},{1,17},{... | collective-permute-start | bytes 245768 | tf_op jit(solution)/shard_map/ppermute | solution.py:602
  19.3 2.5 %collective-permute-start.9 = (f32[160,128]{1,0:T(8,128)S(1)}, f32[160,128]{1,0:T(8,128)S(1)}, u32[]{:S(2)}, u32[]{:S(2)}) collective-permute-start(f32[160,128]{1,0:T(8,128)S(1)} %get-tuple-element.186.refs_0_), channel_id=1, source_target_pairs={{0,12},{4,8},{8,4},{12,0},{16,28},{20,24},{24,20},{28,16},{1,13},{... | collective-permute-start | bytes 245768 | tf_op jit(solution)/shard_map/ppermute | solution.py:602
  23.9 1.6 %collective-permute-start.5 = (f32[160,128]{1,0:T(8,128)S(1)}, f32[160,128]{1,0:T(8,128)S(1)}, u32[]{:S(2)}, u32[]{:S(2)}) collective-permute-start(f32[160,128]{1,0:T(8,128)S(1)} %get-tuple-element.170), channel_id=1, source_target_pairs={{0,3},{1,2},{2,1},{3,0},{4,7},{5,6},{6,5},{7,4},{8,11},{9,10},{10,... | collective-permute-start | bytes 245768 | tf_op jit(solution)/shard_map/ppermute | solution.py:610
  26.6 1.5 %collective-permute-done.5.second.refs_2_ = f32[160,128]{1,0:T(8,128)S(1)} collective-permute-done((f32[160,128]{1,0:T(8,128)S(1)}, f32[160,128]{1,0:T(8,128)S(1)}, u32[]{:S(2)}, u32[]{:S(2)}) %collective-permute-start.5) | collective-permute-done | bytes 81952 | tf_op jit(solution)/shard_map/ppermute | solution.py:610
  28.4 2.5 %collective-permute-start.6 = (f32[160,128]{1,0:T(8,128)S(1)}, f32[160,128]{1,0:T(8,128)S(1)}, u32[]{:S(2)}, u32[]{:S(2)}) collective-permute-start(f32[160,128]{1,0:T(8,128)S(1)} %shard_map.99.refs_0_), channel_id=1, source_target_pairs={{0,12},{4,8},{8,4},{12,0},{16,28},{20,24},{24,20},{28,16},{1,13},{... | collective-permute-start | bytes 245768 | tf_op jit(solution)/shard_map/ppermute | solution.py:602
  34.6 1.2 %collective-permute-done.7.refs_2_ = f32[160,128]{1,0:T(8,128)S(1)} collective-permute-done((f32[160,128]{1,0:T(8,128)S(1)}, f32[160,128]{1,0:T(8,128)S(1)}, u32[]{:S(2)}, u32[]{:S(2)}) %collective-permute-start.7) | collective-permute-done | bytes 81952 | tf_op jit(solution)/shard_map/ppermute | solution.py:602
  36.2 2.0 %collective-permute-start.12 = (f32[160,128]{1,0:T(8,128)S(1)}, f32[160,128]{1,0:T(8,128)S(1)}, u32[]{:S(2)}, u32[]{:S(2)}) collective-permute-start(f32[160,128]{1,0:T(8,128)S(1)} %get-tuple-element.201), channel_id=1, source_target_pairs={{0,16},{4,20},{8,24},{12,28},{16,0},{20,4},{24,8},{28,12},{1,17},{... | collective-permute-start | bytes 245768 | tf_op jit(solution)/shard_map/ppermute | solution.py:602
  39.8 3.1 %collective-permute-done.12.arrived = f32[160,128]{1,0:T(8,128)S(1)} collective-permute-done((f32[160,128]{1,0:T(8,128)S(1)}, f32[160,128]{1,0:T(8,128)S(1)}, u32[]{:S(2)}, u32[]{:S(2)}) %collective-permute-start.12) | collective-permute-done | bytes 81952 | tf_op jit(solution)/shard_map/ppermute | solution.py:602
  43.3 1.6 %collective-permute-start.14 = (f32[160,128]{1,0:T(8,128)S(1)}, f32[160,128]{1,0:T(8,128)S(1)}, u32[]{:S(2)}, u32[]{:S(2)}) collective-permute-start(f32[160,128]{1,0:T(8,128)S(1)} %get-tuple-element.208), channel_id=1, source_target_pairs={{0,3},{1,2},{2,1},{3,0},{4,7},{5,6},{6,5},{7,4},{8,11},{9,10},{10,... | collective-permute-start | bytes 245768 | tf_op jit(solution)/shard_map/ppermute | solution.py:610
  45.9 1.6 %collective-permute-done.14.second.refs_2_ = f32[160,128]{1,0:T(8,128)S(1)} collective-permute-done((f32[160,128]{1,0:T(8,128)S(1)}, f32[160,128]{1,0:T(8,128)S(1)}, u32[]{:S(2)}, u32[]{:S(2)}) %collective-permute-start.14) | collective-permute-done | bytes 81952 | tf_op jit(solution)/shard_map/ppermute | solution.py:610
  47.8 1.2 %collective-permute-start.15 = (f32[160,128]{1,0:T(8,128)S(1)}, f32[160,128]{1,0:T(8,128)S(1)}, u32[]{:S(2)}, u32[]{:S(2)}) collective-permute-start(f32[160,128]{1,0:T(8,128)S(1)} %shard_map.111.refs_0_), channel_id=1, source_target_pairs={{0,12},{4,8},{8,4},{12,0},{16,28},{20,24},{24,20},{28,16},{1,13},{... | collective-permute-start | bytes 245768 | tf_op jit(solution)/shard_map/ppermute | solution.py:602
  49.0 2.1 %collective-permute-start.16 = (f32[160,128]{1,0:T(8,128)S(1)}, f32[160,128]{1,0:T(8,128)S(1)}, u32[]{:S(2)}, u32[]{:S(2)}) collective-permute-start(f32[160,128]{1,0:T(8,128)S(1)} %shard_map.111.refs_0_), channel_id=1, source_target_pairs={{0,8},{4,12},{8,0},{12,4},{16,24},{20,28},{24,16},{28,20},{1,9},{5... | collective-permute-start | bytes 245768 | tf_op jit(solution)/shard_map/ppermute | solution.py:602
  52.8 1.2 %collective-permute-done.15.refs_1_ = f32[160,128]{1,0:T(8,128)S(1)} collective-permute-done((f32[160,128]{1,0:T(8,128)S(1)}, f32[160,128]{1,0:T(8,128)S(1)}, u32[]{:S(2)}, u32[]{:S(2)}) %collective-permute-start.15) | collective-permute-done | bytes 81952 | tf_op jit(solution)/shard_map/ppermute | solution.py:602
  54.0 1.5 %collective-permute-done.16.refs_2_ = f32[160,128]{1,0:T(8,128)S(1)} collective-permute-done((f32[160,128]{1,0:T(8,128)S(1)}, f32[160,128]{1,0:T(8,128)S(1)}, u32[]{:S(2)}, u32[]{:S(2)}) %collective-permute-start.16) | collective-permute-done | bytes 81952 | tf_op jit(solution)/shard_map/ppermute | solution.py:602
  57.6 4.8 %collective-permute-done.18.arrived = f32[160,128]{1,0:T(8,128)S(1)} collective-permute-done((f32[160,128]{1,0:T(8,128)S(1)}, f32[160,128]{1,0:T(8,128)S(1)}, u32[]{:S(2)}, u32[]{:S(2)}) %collective-permute-start.18) | collective-permute-done | bytes 81952 | tf_op jit(solution)/shard_map/ppermute | solution.py:602
  62.7 1.6 %collective-permute-start.20 = (f32[160,128]{1,0:T(8,128)S(1)}, f32[160,128]{1,0:T(8,128)S(1)}, u32[]{:S(2)}, u32[]{:S(2)}) collective-permute-start(f32[160,128]{1,0:T(8,128)S(1)} %get-tuple-element.230), channel_id=1, source_target_pairs={{0,3},{1,2},{2,1},{3,0},{4,7},{5,6},{6,5},{7,4},{8,11},{9,10},{10,... | collective-permute-start | bytes 245768 | tf_op jit(solution)/shard_map/ppermute | solution.py:610
  65.4 1.6 %collective-permute-done.20.second.refs_2_ = f32[160,128]{1,0:T(8,128)S(1)} collective-permute-done((f32[160,128]{1,0:T(8,128)S(1)}, f32[160,128]{1,0:T(8,128)S(1)}, u32[]{:S(2)}, u32[]{:S(2)}) %collective-permute-start.20) | collective-permute-done | bytes 81952 | tf_op jit(solution)/shard_map/ppermute | solution.py:610
  67.3 2.7 %collective-permute-start.22 = (f32[160,128]{1,0:T(8,128)S(1)}, f32[160,128]{1,0:T(8,128)S(1)}, u32[]{:S(2)}, u32[]{:S(2)}) collective-permute-start(f32[160,128]{1,0:T(8,128)S(1)} %shard_map.119.refs_0_), channel_id=1, source_target_pairs={{0,8},{4,12},{8,0},{12,4},{16,24},{20,28},{24,16},{28,20},{1,9},{5... | collective-permute-start | bytes 245768 | tf_op jit(solution)/shard_map/ppermute | solution.py:602
  71.4 2.1 %collective-permute-done.21.refs_1_ = f32[160,128]{1,0:T(8,128)S(1)} collective-permute-done((f32[160,128]{1,0:T(8,128)S(1)}, f32[160,128]{1,0:T(8,128)S(1)}, u32[]{:S(2)}, u32[]{:S(2)}) %collective-permute-start.21) | collective-permute-done | bytes 81952 | tf_op jit(solution)/shard_map/ppermute | solution.py:602
  76.8 4.3 %collective-permute-done.24.arrived = f32[160,128]{1,0:T(8,128)S(1)} collective-permute-done((f32[160,128]{1,0:T(8,128)S(1)}, f32[160,128]{1,0:T(8,128)S(1)}, u32[]{:S(2)}, u32[]{:S(2)}) %collective-permute-start.24) | collective-permute-done | bytes 81952 | tf_op jit(solution)/shard_map/ppermute | solution.py:602
  (63 shorter events, 23.8 us)
Async XLA Ops:
  3.5 10.2 %collective-permute-start = (f32[320,128]{1,0:T(8,128)S(1)}, f32[320,128]{1,0:T(8,128)S(1)}, u32[]{:S(2)}, u32[]{:S(2)}) collective-permute-start(f32[320,128]{1,0:T(8,128)S(1)} %get-tuple-element.142.refs_0_), channel_id=1, source_target_pairs={{0,12},{4,8},{8,4},{12,0},{16,28},{20,24},{24,20},{28,16},{1,13},{... | collective-permute-start | bytes 491528 | tf_op jit(solution)/shard_map/ppermute | solution.py:602
  7.5 7.9 %collective-permute-start.1 = (f32[320,128]{1,0:T(8,128)S(1)}, f32[320,128]{1,0:T(8,128)S(1)}, u32[]{:S(2)}, u32[]{:S(2)}) collective-permute-start(f32[320,128]{1,0:T(8,128)S(1)} %get-tuple-element.142.refs_0_), channel_id=1, source_target_pairs={{0,8},{4,12},{8,0},{12,4},{16,24},{20,28},{24,16},{28,20},{1,9},{5... | collective-permute-start | bytes 491528 | tf_op jit(solution)/shard_map/ppermute | solution.py:602
  7.9 7.5 %collective-permute-start.2 = (f32[320,128]{1,0:T(8,128)S(1)}, f32[320,128]{1,0:T(8,128)S(1)}, u32[]{:S(2)}, u32[]{:S(2)}) collective-permute-start(f32[320,128]{1,0:T(8,128)S(1)} %get-tuple-element.142.refs_0_), channel_id=1, source_target_pairs={{0,4},{4,0},{8,12},{12,8},{16,20},{20,16},{24,28},{28,24},{1,5},{5... | collective-permute-start | bytes 491528 | tf_op jit(solution)/shard_map/ppermute | solution.py:602
  16.2 7.3 %collective-permute-start.3 = (f32[160,128]{1,0:T(8,128)S(1)}, f32[160,128]{1,0:T(8,128)S(1)}, u32[]{:S(2)}, u32[]{:S(2)}) collective-permute-start(f32[160,128]{1,0:T(8,128)S(1)} %get-tuple-element.158), channel_id=1, source_target_pairs={{0,16},{4,20},{8,24},{12,28},{16,0},{20,4},{24,8},{28,12},{1,17},{... | collective-permute-start | bytes 245768 | tf_op jit(solution)/shard_map/ppermute | solution.py:602
  19.3 12.0 %collective-permute-start.9 = (f32[160,128]{1,0:T(8,128)S(1)}, f32[160,128]{1,0:T(8,128)S(1)}, u32[]{:S(2)}, u32[]{:S(2)}) collective-permute-start(f32[160,128]{1,0:T(8,128)S(1)} %get-tuple-element.186.refs_0_), channel_id=1, source_target_pairs={{0,12},{4,8},{8,4},{12,0},{16,28},{20,24},{24,20},{28,16},{1,13},{... | collective-permute-start | bytes 245768 | tf_op jit(solution)/shard_map/ppermute | solution.py:602
  21.8 11.2 %collective-permute-start.10 = (f32[160,128]{1,0:T(8,128)S(1)}, f32[160,128]{1,0:T(8,128)S(1)}, u32[]{:S(2)}, u32[]{:S(2)}) collective-permute-start(f32[160,128]{1,0:T(8,128)S(1)} %get-tuple-element.186.refs_0_), channel_id=1, source_target_pairs={{0,8},{4,12},{8,0},{12,4},{16,24},{20,28},{24,16},{28,20},{1,9},{5... | collective-permute-start | bytes 245768 | tf_op jit(solution)/shard_map/ppermute | solution.py:602
  22.3 10.8 %collective-permute-start.11 = (f32[160,128]{1,0:T(8,128)S(1)}, f32[160,128]{1,0:T(8,128)S(1)}, u32[]{:S(2)}, u32[]{:S(2)}) collective-permute-start(f32[160,128]{1,0:T(8,128)S(1)} %get-tuple-element.186.refs_0_), channel_id=1, source_target_pairs={{0,4},{4,0},{8,12},{12,8},{16,20},{20,16},{24,28},{28,24},{1,5},{5... | collective-permute-start | bytes 245768 | tf_op jit(solution)/shard_map/ppermute | solution.py:602
  23.8 2.8 %collective-permute-start.4 = (f32[160,128]{1,0:T(8,128)S(1)}, f32[160,128]{1,0:T(8,128)S(1)}, u32[]{:S(2)}, u32[]{:S(2)}) collective-permute-start(f32[160,128]{1,0:T(8,128)S(1)} %get-tuple-element.169), channel_id=1, source_target_pairs={{0,1},{1,0},{2,3},{3,2},{4,5},{5,4},{6,7},{7,6},{8,9},{9,8},{10,11... | collective-permute-start | bytes 245768 | tf_op jit(solution)/shard_map/ppermute | solution.py:611
  23.9 4.2 %collective-permute-start.5 = (f32[160,128]{1,0:T(8,128)S(1)}, f32[160,128]{1,0:T(8,128)S(1)}, u32[]{:S(2)}, u32[]{:S(2)}) collective-permute-start(f32[160,128]{1,0:T(8,128)S(1)} %get-tuple-element.170), channel_id=1, source_target_pairs={{0,3},{1,2},{2,1},{3,0},{4,7},{5,6},{6,5},{7,4},{8,11},{9,10},{10,... | collective-permute-start | bytes 245768 | tf_op jit(solution)/shard_map/ppermute | solution.py:610
  28.4 6.3 %collective-permute-start.6 = (f32[160,128]{1,0:T(8,128)S(1)}, f32[160,128]{1,0:T(8,128)S(1)}, u32[]{:S(2)}, u32[]{:S(2)}) collective-permute-start(f32[160,128]{1,0:T(8,128)S(1)} %shard_map.99.refs_0_), channel_id=1, source_target_pairs={{0,12},{4,8},{8,4},{12,0},{16,28},{20,24},{24,20},{28,16},{1,13},{... | collective-permute-start | bytes 245768 | tf_op jit(solution)/shard_map/ppermute | solution.py:602
  30.9 4.9 %collective-permute-start.7 = (f32[160,128]{1,0:T(8,128)S(1)}, f32[160,128]{1,0:T(8,128)S(1)}, u32[]{:S(2)}, u32[]{:S(2)}) collective-permute-start(f32[160,128]{1,0:T(8,128)S(1)} %shard_map.99.refs_0_), channel_id=1, source_target_pairs={{0,8},{4,12},{8,0},{12,4},{16,24},{20,28},{24,16},{28,20},{1,9},{5... | collective-permute-start | bytes 245768 | tf_op jit(solution)/shard_map/ppermute | solution.py:602
  31.3 4.6 %collective-permute-start.8 = (f32[160,128]{1,0:T(8,128)S(1)}, f32[160,128]{1,0:T(8,128)S(1)}, u32[]{:S(2)}, u32[]{:S(2)}) collective-permute-start(f32[160,128]{1,0:T(8,128)S(1)} %shard_map.99.refs_0_), channel_id=1, source_target_pairs={{0,4},{4,0},{8,12},{12,8},{16,20},{20,16},{24,28},{28,24},{1,5},{5... | collective-permute-start | bytes 245768 | tf_op jit(solution)/shard_map/ppermute | solution.py:602
  36.2 6.6 %collective-permute-start.12 = (f32[160,128]{1,0:T(8,128)S(1)}, f32[160,128]{1,0:T(8,128)S(1)}, u32[]{:S(2)}, u32[]{:S(2)}) collective-permute-start(f32[160,128]{1,0:T(8,128)S(1)} %get-tuple-element.201), channel_id=1, source_target_pairs={{0,16},{4,20},{8,24},{12,28},{16,0},{20,4},{24,8},{28,12},{1,17},{... | collective-permute-start | bytes 245768 | tf_op jit(solution)/shard_map/ppermute | solution.py:602
  43.3 4.2 %collective-permute-start.14 = (f32[160,128]{1,0:T(8,128)S(1)}, f32[160,128]{1,0:T(8,128)S(1)}, u32[]{:S(2)}, u32[]{:S(2)}) collective-permute-start(f32[160,128]{1,0:T(8,128)S(1)} %get-tuple-element.208), channel_id=1, source_target_pairs={{0,3},{1,2},{2,1},{3,0},{4,7},{5,6},{6,5},{7,4},{8,11},{9,10},{10,... | collective-permute-start | bytes 245768 | tf_op jit(solution)/shard_map/ppermute | solution.py:610
  47.8 6.3 %collective-permute-start.15 = (f32[160,128]{1,0:T(8,128)S(1)}, f32[160,128]{1,0:T(8,128)S(1)}, u32[]{:S(2)}, u32[]{:S(2)}) collective-permute-start(f32[160,128]{1,0:T(8,128)S(1)} %shard_map.111.refs_0_), channel_id=1, source_target_pairs={{0,12},{4,8},{8,4},{12,0},{16,28},{20,24},{24,20},{28,16},{1,13},{... | collective-permute-start | bytes 245768 | tf_op jit(solution)/shard_map/ppermute | solution.py:602
  49.0 6.5 %collective-permute-start.16 = (f32[160,128]{1,0:T(8,128)S(1)}, f32[160,128]{1,0:T(8,128)S(1)}, u32[]{:S(2)}, u32[]{:S(2)}) collective-permute-start(f32[160,128]{1,0:T(8,128)S(1)} %shard_map.111.refs_0_), channel_id=1, source_target_pairs={{0,8},{4,12},{8,0},{12,4},{16,24},{20,28},{24,16},{28,20},{1,9},{5... | collective-permute-start | bytes 245768 | tf_op jit(solution)/shard_map/ppermute | solution.py:602
  51.0 4.4 %collective-permute-start.17 = (f32[160,128]{1,0:T(8,128)S(1)}, f32[160,128]{1,0:T(8,128)S(1)}, u32[]{:S(2)}, u32[]{:S(2)}) collective-permute-start(f32[160,128]{1,0:T(8,128)S(1)} %shard_map.111.refs_0_), channel_id=1, source_target_pairs={{0,4},{4,0},{8,12},{12,8},{16,20},{20,16},{24,28},{28,24},{1,5},{5... | collective-permute-start | bytes 245768 | tf_op jit(solution)/shard_map/ppermute | solution.py:602
  55.8 6.5 %collective-permute-start.18 = (f32[160,128]{1,0:T(8,128)S(1)}, f32[160,128]{1,0:T(8,128)S(1)}, u32[]{:S(2)}, u32[]{:S(2)}) collective-permute-start(f32[160,128]{1,0:T(8,128)S(1)} %get-tuple-element.225), channel_id=1, source_target_pairs={{0,16},{4,20},{8,24},{12,28},{16,0},{20,4},{24,8},{28,12},{1,17},{... | collective-permute-start | bytes 245768 | tf_op jit(solution)/shard_map/ppermute | solution.py:602
  62.7 2.8 %collective-permute-start.19 = (f32[160,128]{1,0:T(8,128)S(1)}, f32[160,128]{1,0:T(8,128)S(1)}, u32[]{:S(2)}, u32[]{:S(2)}) collective-permute-start(f32[160,128]{1,0:T(8,128)S(1)} %get-tuple-element.229), channel_id=1, source_target_pairs={{0,1},{1,0},{2,3},{3,2},{4,5},{5,4},{6,7},{7,6},{8,9},{9,8},{10,11... | collective-permute-start | bytes 245768 | tf_op jit(solution)/shard_map/ppermute | solution.py:611
  62.7 4.2 %collective-permute-start.20 = (f32[160,128]{1,0:T(8,128)S(1)}, f32[160,128]{1,0:T(8,128)S(1)}, u32[]{:S(2)}, u32[]{:S(2)}) collective-permute-start(f32[160,128]{1,0:T(8,128)S(1)} %get-tuple-element.230), channel_id=1, source_target_pairs={{0,3},{1,2},{2,1},{3,0},{4,7},{5,6},{6,5},{7,4},{8,11},{9,10},{10,... | collective-permute-start | bytes 245768 | tf_op jit(solution)/shard_map/ppermute | solution.py:610
  67.2 6.3 %collective-permute-start.21 = (f32[160,128]{1,0:T(8,128)S(1)}, f32[160,128]{1,0:T(8,128)S(1)}, u32[]{:S(2)}, u32[]{:S(2)}) collective-permute-start(f32[160,128]{1,0:T(8,128)S(1)} %shard_map.119.refs_0_), channel_id=1, source_target_pairs={{0,12},{4,8},{8,4},{12,0},{16,28},{20,24},{24,20},{28,16},{1,13},{... | collective-permute-start | bytes 245768 | tf_op jit(solution)/shard_map/ppermute | solution.py:602
  67.3 7.2 %collective-permute-start.22 = (f32[160,128]{1,0:T(8,128)S(1)}, f32[160,128]{1,0:T(8,128)S(1)}, u32[]{:S(2)}, u32[]{:S(2)}) collective-permute-start(f32[160,128]{1,0:T(8,128)S(1)} %shard_map.119.refs_0_), channel_id=1, source_target_pairs={{0,8},{4,12},{8,0},{12,4},{16,24},{20,28},{24,16},{28,20},{1,9},{5... | collective-permute-start | bytes 245768 | tf_op jit(solution)/shard_map/ppermute | solution.py:602
  70.1 4.7 %collective-permute-start.23 = (f32[160,128]{1,0:T(8,128)S(1)}, f32[160,128]{1,0:T(8,128)S(1)}, u32[]{:S(2)}, u32[]{:S(2)}) collective-permute-start(f32[160,128]{1,0:T(8,128)S(1)} %shard_map.119.refs_0_), channel_id=1, source_target_pairs={{0,4},{4,0},{8,12},{12,8},{16,20},{20,16},{24,28},{28,24},{1,5},{5... | collective-permute-start | bytes 245768 | tf_op jit(solution)/shard_map/ppermute | solution.py:602
  75.1 6.1 %collective-permute-start.24 = (f32[160,128]{1,0:T(8,128)S(1)}, f32[160,128]{1,0:T(8,128)S(1)}, u32[]{:S(2)}, u32[]{:S(2)}) collective-permute-start(f32[160,128]{1,0:T(8,128)S(1)} %get-tuple-element.246), channel_id=1, source_target_pairs={{0,16},{4,20},{8,24},{12,28},{16,0},{20,4},{24,8},{28,12},{1,17},{... | collective-permute-start | bytes 245768 | tf_op jit(solution)/shard_map/ppermute | solution.py:602
  (1 other events, 2.7 us)

commit v5 on v4

--- a/solution.py
+++ b/solution.py
@@ -419,8 +419,8 @@
     return size - 1 - digit if backward else digit
 
 
-def source_place(size, stride, backward, i):
-    digit, k = digit_of(size, stride), (size - i) % size
+def source_place(size, stride, backward, k):
+    digit = digit_of(size, stride)
     m = digit ^ k if size & (size - 1) == 0 else lax.rem(digit - k + size, size)
     return size - 1 - m if backward else m
 
@@ -442,15 +442,15 @@
     return state, below
 
 
-def fold_kernel(size, stride, backward, first, *refs):
+def fold_kernel(size, stride, backward, first, steps, *refs):
     parts, refs = refs[:size], refs[size:]
     if first:
         total, before, high, low, held = refs
     else:
         high, low, total, before, held = refs
     rows = total.shape[0]
-    for i, part in enumerate(parts):
-        m = source_place(size, stride, backward, i)
+    for k, part in zip(steps, parts):
+        m = source_place(size, stride, backward, k)
         held[m] = part[:rows, :]
         if first == "packed":
             store_packed(high, low, m, part[rows:, :], backward)
@@ -463,16 +463,16 @@
     total[...], before[...] = in_turn(size, place, held, high, low)
 
 
-def unpack_kernel(size, stride, backward, *refs):
+def unpack_kernel(size, stride, backward, steps, *refs):
     parts, (high, low) = refs[:size], refs[size:]
-    for i, part in enumerate(parts):
-        store_packed(high, low, source_place(size, stride, backward, i), part[...], backward)
-
-
-def total_kernel(size, stride, backward, *refs):
+    for k, part in zip(steps, parts):
+        store_packed(high, low, source_place(size, stride, backward, k), part[...], backward)
+
+
+def total_kernel(size, stride, backward, steps, *refs):
     parts, (high, low, total, held) = refs[:size], refs[size:]
-    for i, part in enumerate(parts):
-        held[source_place(size, stride, backward, i)] = part[...]
+    for k, part in zip(steps, parts):
+        held[source_place(size, stride, backward, k)] = part[...]
     below = jnp.concatenate([spread(held[m]) for m in range(size - 1)], axis=0)
     total[...] = held[size - 1] + map_times(high[...], low[...], below)
 
@@ -593,6 +593,10 @@
     return list(zip(sizes, strides))
 
 
+def steps_of(size):
+    return (0, 2, 1, 3) if size == 4 else tuple(range(size))
+
+
 def exchange(block, axis, size, stride, k):
     pairs = []
     for i in range(lax.axis_size(axis)):
@@ -687,9 +691,8 @@
             16 * unit,
         )
 
-    def parts_of(block, size, stride):
-        sent = [exchange(block, "stream", size, stride, k) for k in reversed(range(1, size))]
-        return [block] + sent
+    def parts_of(block, size, stride, steps):
+        return [block] + [exchange(block, "stream", size, stride, k) for k in steps[1:]]
 
     def passage(key, size, stride):
         backward, level = key
@@ -714,19 +717,20 @@
                 first = "whole" if level else "packed"
                 if level:
                     total = jnp.concatenate([total, *store["whole", (backward, level - 1)]], axis=0)
-            parts = parts_of(total, size, stride)
+            steps = steps_of(size)
+            parts = parts_of(total, size, stride, steps)
             if level == 0:
                 parts, done = lax.optimization_barrier((parts, beside()))
             held = shape(size, rows, columns)
             scratch = [pltpu.VMEM(held.shape, F32)]
-            body = partial(fold_kernel, size, stride, backward, first)
+            body = partial(fold_kernel, size, stride, backward, first, steps)
             if first:
                 outs = [trace, trace, *pair(size, rows, 2 * LANES)]
                 total, before, *kept = call(body, outs, parts, unit, scratch)
                 store["maps", key] = tuple(kept)
                 passage(key, size, stride)
             elif ("suffix", key) in store:
-                body = partial(total_kernel, size, stride, backward)
+                body = partial(total_kernel, size, stride, backward, steps)
                 total, held = call(body, [trace, held], (*parts, *store["suffix", key]), unit)
                 body = partial(before_kernel, size, stride, backward)
                 (before,) = call(body, [trace], (held, *store["maps", key]), unit)
@@ -755,11 +759,11 @@
         size, stride = levels[0]
         after = store["pass", (False, 0)]
         block, store["pass", (False, 0)] = lax.optimization_barrier((block, after))
-        return parts_of(block, size, stride)
+        return parts_of(block, size, stride, steps_of(size))
 
     def take_maps(parts):
         size, stride = levels[0]
-        body = partial(unpack_kernel, size, stride, True)
+        body = partial(unpack_kernel, size, stride, True, steps_of(size))
         store["maps", (True, 0)] = tuple(call(body, pair(size, rows, 2 * LANES), parts, unit))
         passage((True, 0), size, stride)
 

time: 82.4 us -> 80.3 us (0.975)
  waiting for transfers between devices: 25.9 us -> 21.1 us
  starting transfers between devices: 30.4 us -> 33.1 us
    ppermute x19, waiting for transfers between devices: 21.2 us -> 16.5 us  [exchange(): return lax.ppermute(block, axis, pairs)]
    ppermute x19, starting transfers between devices: 25.3 us -> 27.9 us  [exchange(): return lax.ppermute(block, axis, pairs)]
  transfers between devices with their start and end apart: 25 -> 25, of which waited for: 14 -> 13; matrix products, arithmetic and copies ran while one was open for 0% -> 0% of each run, Pallas kernels for 22% -> 23%
where the time goes in v5:
time: 80.3 us; the launch traced here: 80.1 us
  starting transfers between devices  33.1 us (41%)
  Pallas kernels  24.9 us (31%)
  waiting for transfers between devices  21.1 us (26%)
  between operations  0.98 us (1%)
    ppermute x19, starting transfers between devices, exchange(): return lax.ppermute(block, axis, pairs)  27.9 us
    pallas_call x36, Pallas kernels, call(): pl.pallas_call(body, out_shape=list(outs), in_specs=spaces or [vmem] * le...  24.9 us
    ppermute x19, waiting for transfers between devices, exchange(): return lax.ppermute(block, axis, pairs)  16.5 us
    ppermute x3, starting transfers between devices, side_exchange(): second = lax.ppermute(second, 'span', across)  4.93 us
    ppermute x3, waiting for transfers between devices, side_exchange(): second = lax.ppermute(second, 'span', across)  4.63 us
  transfers between devices with their start and end apart: 25, of which 13 were waited for; matrix products, arithmetic and copies ran while one was open for 0% of the time, Pallas kernels for 23%

profile of v5, /device:TPU:0, one launch (start us, length us, event | category | flops | bytes accessed | tf_op | source)
XLA Modules:
  0.0 80.1 jit_solution(8909515507053890510)
XLA Ops:
  0.7 2.8 %shard_map.91 = (f32[320,128]{1,0:T(8,128)S(1)}, f32[8,128]{1,0:T(8,128)S(1)}) custom-call(s32[2]{0:T(128)} %bitcast.20, s32[1]{0:T(128)} %bitcast.10.count_in, s32[2,2]{1,0:T(2,128)} %bitcast.17, s32[2,2]{1,0:T(2,128)} %bitcast.18, f32[2,320,128]{2,1,0:T(8,128)} %bitcast.13, bf16[2,320,320]{2,1,0:T(8,128)(2,1)} %bitcast.11, bf16[6,320,320]{2,1,0:T(8,128)(2,1)} %table_in.3, ...), custom_call_target="tpu_custom_call" | custom-call | flops 524288000 | bytes 2543660 | tf_op jit(solution)/shard_map/pallas_call | solution.py:104
  3.5 3.1 %collective-permute-start = (f32[320,128]{1,0:T(8,128)S(1)}, f32[320,128]{1,0:T(8,128)S(1)}, u32[]{:S(2)}, u32[]{:S(2)}) collective-permute-start(f32[320,128]{1,0:T(8,128)S(1)} %get-tuple-element.142.refs_0_), channel_id=1, source_target_pairs={{0,8},{4,12},{8,0},{12,4},{16,24},{20,28},{24,16},{28,20},{1,9},{5... | collective-permute-start | bytes 491528 | tf_op jit(solution)/shard_map/ppermute | solution.py:606
  6.6 1.5 %collective-permute-start.1 = (f32[320,128]{1,0:T(8,128)S(1)}, f32[320,128]{1,0:T(8,128)S(1)}, u32[]{:S(2)}, u32[]{:S(2)}) collective-permute-start(f32[320,128]{1,0:T(8,128)S(1)} %get-tuple-element.142.refs_0_), channel_id=1, source_target_pairs={{0,4},{4,0},{8,12},{12,8},{16,20},{20,16},{24,28},{28,24},{1,5},{5... | collective-permute-start | bytes 491528 | tf_op jit(solution)/shard_map/ppermute | solution.py:606
  8.1 5.6 %shard_map.92 = (bf16[4,80,320]{2,1,0:T(8,128)(2,1)S(1)}, f32[2,320,128]{2,1,0:T(8,128)S(1)}, bf16[2,320,512]{2,1,0:T(8,128)(2,1)S(1)}, bf16[2,320,512]{2,1,0:T(...) custom-call(s32[2]{0:T(128)} %bitcast.21, ...), custom_call_target="tpu_custom_call" | custom-call | flops 1310720000 | bytes 6107160 | tf_op jit(solution)/shard_map/pallas_call | solution.py:104
  13.7 2.1 %collective-permute-done.1.refs_2_ = f32[320,128]{1,0:T(8,128)S(1)} collective-permute-done((f32[320,128]{1,0:T(8,128)S(1)}, f32[320,128]{1,0:T(8,128)S(1)}, u32[]{:S(2)}, u32[]{:S(2)}) %collective-permute-start.1) | collective-permute-done | bytes 163872 | tf_op jit(solution)/shard_map/ppermute | solution.py:606
  16.5 2.7 %collective-permute-start.3 = (f32[160,128]{1,0:T(8,128)S(1)}, f32[160,128]{1,0:T(8,128)S(1)}, u32[]{:S(2)}, u32[]{:S(2)}) collective-permute-start(f32[160,128]{1,0:T(8,128)S(1)} %get-tuple-element.158), channel_id=1, source_target_pairs={{0,16},{4,20},{8,24},{12,28},{16,0},{20,4},{24,8},{28,12},{1,17},{... | collective-permute-start | bytes 245768 | tf_op jit(solution)/shard_map/ppermute | solution.py:606
  21.7 1.6 %collective-permute-start.11 = (f32[160,128]{1,0:T(8,128)S(1)}, f32[160,128]{1,0:T(8,128)S(1)}, u32[]{:S(2)}, u32[]{:S(2)}) collective-permute-start(f32[160,128]{1,0:T(8,128)S(1)} %get-tuple-element.186.refs_0_), channel_id=1, source_target_pairs={{0,12},{4,8},{8,4},{12,0},{16,28},{20,24},{24,20},{28,16},{1,13},{... | collective-permute-start | bytes 245768 | tf_op jit(solution)/shard_map/ppermute | solution.py:606
  24.2 1.6 %collective-permute-start.5 = (f32[160,128]{1,0:T(8,128)S(1)}, f32[160,128]{1,0:T(8,128)S(1)}, u32[]{:S(2)}, u32[]{:S(2)}) collective-permute-start(f32[160,128]{1,0:T(8,128)S(1)} %get-tuple-element.170), channel_id=1, source_target_pairs={{0,3},{1,2},{2,1},{3,0},{4,7},{5,6},{6,5},{7,4},{8,11},{9,10},{10,... | collective-permute-start | bytes 245768 | tf_op jit(solution)/shard_map/ppermute | solution.py:614
  26.9 1.5 %collective-permute-done.5.second.refs_2_ = f32[160,128]{1,0:T(8,128)S(1)} collective-permute-done((f32[160,128]{1,0:T(8,128)S(1)}, f32[160,128]{1,0:T(8,128)S(1)}, u32[]{:S(2)}, u32[]{:S(2)}) %collective-permute-start.5) | collective-permute-done | bytes 81952 | tf_op jit(solution)/shard_map/ppermute | solution.py:614
  28.7 1.3 %collective-permute-start.6 = (f32[160,128]{1,0:T(8,128)S(1)}, f32[160,128]{1,0:T(8,128)S(1)}, u32[]{:S(2)}, u32[]{:S(2)}) collective-permute-start(f32[160,128]{1,0:T(8,128)S(1)} %shard_map.99.refs_0_), channel_id=1, source_target_pairs={{0,8},{4,12},{8,0},{12,4},{16,24},{20,28},{24,16},{28,20},{1,9},{5... | collective-permute-start | bytes 245768 | tf_op jit(solution)/shard_map/ppermute | solution.py:606
  30.7 1.6 %collective-permute-start.8 = (f32[160,128]{1,0:T(8,128)S(1)}, f32[160,128]{1,0:T(8,128)S(1)}, u32[]{:S(2)}, u32[]{:S(2)}) collective-permute-start(f32[160,128]{1,0:T(8,128)S(1)} %shard_map.99.refs_0_), channel_id=1, source_target_pairs={{0,12},{4,8},{8,4},{12,0},{16,28},{20,24},{24,20},{28,16},{1,13},{... | collective-permute-start | bytes 245768 | tf_op jit(solution)/shard_map/ppermute | solution.py:606
  36.5 1.6 %collective-permute-start.12 = (f32[160,128]{1,0:T(8,128)S(1)}, f32[160,128]{1,0:T(8,128)S(1)}, u32[]{:S(2)}, u32[]{:S(2)}) collective-permute-start(f32[160,128]{1,0:T(8,128)S(1)} %get-tuple-element.201), channel_id=1, source_target_pairs={{0,16},{4,20},{8,24},{12,28},{16,0},{20,4},{24,8},{28,12},{1,17},{... | collective-permute-start | bytes 245768 | tf_op jit(solution)/shard_map/ppermute | solution.py:606
  39.6 2.4 %collective-permute-done.12.arrived = f32[160,128]{1,0:T(8,128)S(1)} collective-permute-done((f32[160,128]{1,0:T(8,128)S(1)}, f32[160,128]{1,0:T(8,128)S(1)}, u32[]{:S(2)}, u32[]{:S(2)}) %collective-permute-start.12) | collective-permute-done | bytes 81952 | tf_op jit(solution)/shard_map/ppermute | solution.py:606
  42.4 1.6 %collective-permute-start.14 = (f32[160,128]{1,0:T(8,128)S(1)}, f32[160,128]{1,0:T(8,128)S(1)}, u32[]{:S(2)}, u32[]{:S(2)}) collective-permute-start(f32[160,128]{1,0:T(8,128)S(1)} %get-tuple-element.208), channel_id=1, source_target_pairs={{0,3},{1,2},{2,1},{3,0},{4,7},{5,6},{6,5},{7,4},{8,11},{9,10},{10,... | collective-permute-start | bytes 245768 | tf_op jit(solution)/shard_map/ppermute | solution.py:614
  45.1 1.6 %collective-permute-done.14.second.refs_2_ = f32[160,128]{1,0:T(8,128)S(1)} collective-permute-done((f32[160,128]{1,0:T(8,128)S(1)}, f32[160,128]{1,0:T(8,128)S(1)}, u32[]{:S(2)}, u32[]{:S(2)}) %collective-permute-start.14) | collective-permute-done | bytes 81952 | tf_op jit(solution)/shard_map/ppermute | solution.py:614
  46.9 1.5 %collective-permute-start.15 = (f32[160,128]{1,0:T(8,128)S(1)}, f32[160,128]{1,0:T(8,128)S(1)}, u32[]{:S(2)}, u32[]{:S(2)}) collective-permute-start(f32[160,128]{1,0:T(8,128)S(1)} %shard_map.111.refs_0_), channel_id=1, source_target_pairs={{0,8},{4,12},{8,0},{12,4},{16,24},{20,28},{24,16},{28,20},{1,9},{5... | collective-permute-start | bytes 245768 | tf_op jit(solution)/shard_map/ppermute | solution.py:606
  53.2 1.6 %collective-permute-done.17.refs_3_ = f32[160,128]{1,0:T(8,128)S(1)} collective-permute-done((f32[160,128]{1,0:T(8,128)S(1)}, f32[160,128]{1,0:T(8,128)S(1)}, u32[]{:S(2)}, u32[]{:S(2)}) %collective-permute-start.17) | collective-permute-done | bytes 81952 | tf_op jit(solution)/shard_map/ppermute | solution.py:606
  55.2 2.1 %collective-permute-start.18 = (f32[160,128]{1,0:T(8,128)S(1)}, f32[160,128]{1,0:T(8,128)S(1)}, u32[]{:S(2)}, u32[]{:S(2)}) collective-permute-start(f32[160,128]{1,0:T(8,128)S(1)} %get-tuple-element.225), channel_id=1, source_target_pairs={{0,16},{4,20},{8,24},{12,28},{16,0},{20,4},{24,8},{28,12},{1,17},{... | collective-permute-start | bytes 245768 | tf_op jit(solution)/shard_map/ppermute | solution.py:606
  57.9 3.7 %collective-permute-done.18.arrived = f32[160,128]{1,0:T(8,128)S(1)} collective-permute-done((f32[160,128]{1,0:T(8,128)S(1)}, f32[160,128]{1,0:T(8,128)S(1)}, u32[]{:S(2)}, u32[]{:S(2)}) %collective-permute-start.18) | collective-permute-done | bytes 81952 | tf_op jit(solution)/shard_map/ppermute | solution.py:606
  62.0 1.7 %collective-permute-start.20 = (f32[160,128]{1,0:T(8,128)S(1)}, f32[160,128]{1,0:T(8,128)S(1)}, u32[]{:S(2)}, u32[]{:S(2)}) collective-permute-start(f32[160,128]{1,0:T(8,128)S(1)} %get-tuple-element.230), channel_id=1, source_target_pairs={{0,3},{1,2},{2,1},{3,0},{4,7},{5,6},{6,5},{7,4},{8,11},{9,10},{10,... | collective-permute-start | bytes 245768 | tf_op jit(solution)/shard_map/ppermute | solution.py:614
  64.7 1.5 %collective-permute-done.20.second.refs_2_ = f32[160,128]{1,0:T(8,128)S(1)} collective-permute-done((f32[160,128]{1,0:T(8,128)S(1)}, f32[160,128]{1,0:T(8,128)S(1)}, u32[]{:S(2)}, u32[]{:S(2)}) %collective-permute-start.20) | collective-permute-done | bytes 81952 | tf_op jit(solution)/shard_map/ppermute | solution.py:614
  68.0 2.1 %collective-permute-start.23 = (f32[160,128]{1,0:T(8,128)S(1)}, f32[160,128]{1,0:T(8,128)S(1)}, u32[]{:S(2)}, u32[]{:S(2)}) collective-permute-start(f32[160,128]{1,0:T(8,128)S(1)} %shard_map.119.refs_0_), channel_id=1, source_target_pairs={{0,12},{4,8},{8,4},{12,0},{16,28},{20,24},{24,20},{28,16},{1,13},{... | collective-permute-start | bytes 245768 | tf_op jit(solution)/shard_map/ppermute | solution.py:606
  73.7 2.6 %collective-permute-start.24 = (f32[160,128]{1,0:T(8,128)S(1)}, f32[160,128]{1,0:T(8,128)S(1)}, u32[]{:S(2)}, u32[]{:S(2)}) collective-permute-start(f32[160,128]{1,0:T(8,128)S(1)} %get-tuple-element.246), channel_id=1, source_target_pairs={{0,16},{4,20},{8,24},{12,28},{16,0},{20,4},{24,8},{28,12},{1,17},{... | collective-permute-start | bytes 245768 | tf_op jit(solution)/shard_map/ppermute | solution.py:606
  77.5 1.6 %collective-permute-done.24.arrived = f32[160,128]{1,0:T(8,128)S(1)} collective-permute-done((f32[160,128]{1,0:T(8,128)S(1)}, f32[160,128]{1,0:T(8,128)S(1)}, u32[]{:S(2)}, u32[]{:S(2)}) %collective-permute-start.24) | collective-permute-done | bytes 81952 | tf_op jit(solution)/shard_map/ppermute | solution.py:606
  (63 shorter events, 28.2 us)
Async XLA Ops:
  3.5 10.2 %collective-permute-start = (f32[320,128]{1,0:T(8,128)S(1)}, f32[320,128]{1,0:T(8,128)S(1)}, u32[]{:S(2)}, u32[]{:S(2)}) collective-permute-start(f32[320,128]{1,0:T(8,128)S(1)} %get-tuple-element.142.refs_0_), channel_id=1, source_target_pairs={{0,8},{4,12},{8,0},{12,4},{16,24},{20,28},{24,16},{28,20},{1,9},{5... | collective-permute-start | bytes 491528 | tf_op jit(solution)/shard_map/ppermute | solution.py:606
  6.6 9.2 %collective-permute-start.1 = (f32[320,128]{1,0:T(8,128)S(1)}, f32[320,128]{1,0:T(8,128)S(1)}, u32[]{:S(2)}, u32[]{:S(2)}) collective-permute-start(f32[320,128]{1,0:T(8,128)S(1)} %get-tuple-element.142.refs_0_), channel_id=1, source_target_pairs={{0,4},{4,0},{8,12},{12,8},{16,20},{20,16},{24,28},{28,24},{1,5},{5... | collective-permute-start | bytes 491528 | tf_op jit(solution)/shard_map/ppermute | solution.py:606
  8.1 7.7 %collective-permute-start.2 = (f32[320,128]{1,0:T(8,128)S(1)}, f32[320,128]{1,0:T(8,128)S(1)}, u32[]{:S(2)}, u32[]{:S(2)}) collective-permute-start(f32[320,128]{1,0:T(8,128)S(1)} %get-tuple-element.142.refs_0_), channel_id=1, source_target_pairs={{0,12},{4,8},{8,4},{12,0},{16,28},{20,24},{24,20},{28,16},{1,13},{... | collective-permute-start | bytes 491528 | tf_op jit(solution)/shard_map/ppermute | solution.py:606
  16.5 7.3 %collective-permute-start.3 = (f32[160,128]{1,0:T(8,128)S(1)}, f32[160,128]{1,0:T(8,128)S(1)}, u32[]{:S(2)}, u32[]{:S(2)}) collective-permute-start(f32[160,128]{1,0:T(8,128)S(1)} %get-tuple-element.158), channel_id=1, source_target_pairs={{0,16},{4,20},{8,24},{12,28},{16,0},{20,4},{24,8},{28,12},{1,17},{... | collective-permute-start | bytes 245768 | tf_op jit(solution)/shard_map/ppermute | solution.py:606
  19.7 11.0 %collective-permute-start.9 = (f32[160,128]{1,0:T(8,128)S(1)}, f32[160,128]{1,0:T(8,128)S(1)}, u32[]{:S(2)}, u32[]{:S(2)}) collective-permute-start(f32[160,128]{1,0:T(8,128)S(1)} %get-tuple-element.186.refs_0_), channel_id=1, source_target_pairs={{0,8},{4,12},{8,0},{12,4},{16,24},{20,28},{24,16},{28,20},{1,9},{5... | collective-permute-start | bytes 245768 | tf_op jit(solution)/shard_map/ppermute | solution.py:606
  20.9 12.5 %collective-permute-start.10 = (f32[160,128]{1,0:T(8,128)S(1)}, f32[160,128]{1,0:T(8,128)S(1)}, u32[]{:S(2)}, u32[]{:S(2)}) collective-permute-start(f32[160,128]{1,0:T(8,128)S(1)} %get-tuple-element.186.refs_0_), channel_id=1, source_target_pairs={{0,4},{4,0},{8,12},{12,8},{16,20},{20,16},{24,28},{28,24},{1,5},{5... | collective-permute-start | bytes 245768 | tf_op jit(solution)/shard_map/ppermute | solution.py:606
  21.7 11.7 %collective-permute-start.11 = (f32[160,128]{1,0:T(8,128)S(1)}, f32[160,128]{1,0:T(8,128)S(1)}, u32[]{:S(2)}, u32[]{:S(2)}) collective-permute-start(f32[160,128]{1,0:T(8,128)S(1)} %get-tuple-element.186.refs_0_), channel_id=1, source_target_pairs={{0,12},{4,8},{8,4},{12,0},{16,28},{20,24},{24,20},{28,16},{1,13},{... | collective-permute-start | bytes 245768 | tf_op jit(solution)/shard_map/ppermute | solution.py:606
  24.1 2.8 %collective-permute-start.4 = (f32[160,128]{1,0:T(8,128)S(1)}, f32[160,128]{1,0:T(8,128)S(1)}, u32[]{:S(2)}, u32[]{:S(2)}) collective-permute-start(f32[160,128]{1,0:T(8,128)S(1)} %get-tuple-element.169), channel_id=1, source_target_pairs={{0,1},{1,0},{2,3},{3,2},{4,5},{5,4},{6,7},{7,6},{8,9},{9,8},{10,11... | collective-permute-start | bytes 245768 | tf_op jit(solution)/shard_map/ppermute | solution.py:615
  24.2 4.2 %collective-permute-start.5 = (f32[160,128]{1,0:T(8,128)S(1)}, f32[160,128]{1,0:T(8,128)S(1)}, u32[]{:S(2)}, u32[]{:S(2)}) collective-permute-start(f32[160,128]{1,0:T(8,128)S(1)} %get-tuple-element.170), channel_id=1, source_target_pairs={{0,3},{1,2},{2,1},{3,0},{4,7},{5,6},{6,5},{7,4},{8,11},{9,10},{10,... | collective-permute-start | bytes 245768 | tf_op jit(solution)/shard_map/ppermute | solution.py:614
  28.7 6.2 %collective-permute-start.6 = (f32[160,128]{1,0:T(8,128)S(1)}, f32[160,128]{1,0:T(8,128)S(1)}, u32[]{:S(2)}, u32[]{:S(2)}) collective-permute-start(f32[160,128]{1,0:T(8,128)S(1)} %shard_map.99.refs_0_), channel_id=1, source_target_pairs={{0,8},{4,12},{8,0},{12,4},{16,24},{20,28},{24,16},{28,20},{1,9},{5... | collective-permute-start | bytes 245768 | tf_op jit(solution)/shard_map/ppermute | solution.py:606
  30.0 5.0 %collective-permute-start.7 = (f32[160,128]{1,0:T(8,128)S(1)}, f32[160,128]{1,0:T(8,128)S(1)}, u32[]{:S(2)}, u32[]{:S(2)}) collective-permute-start(f32[160,128]{1,0:T(8,128)S(1)} %shard_map.99.refs_0_), channel_id=1, source_target_pairs={{0,4},{4,0},{8,12},{12,8},{16,20},{20,16},{24,28},{28,24},{1,5},{5... | collective-permute-start | bytes 245768 | tf_op jit(solution)/shard_map/ppermute | solution.py:606
  30.7 5.5 %collective-permute-start.8 = (f32[160,128]{1,0:T(8,128)S(1)}, f32[160,128]{1,0:T(8,128)S(1)}, u32[]{:S(2)}, u32[]{:S(2)}) collective-permute-start(f32[160,128]{1,0:T(8,128)S(1)} %shard_map.99.refs_0_), channel_id=1, source_target_pairs={{0,12},{4,8},{8,4},{12,0},{16,28},{20,24},{24,20},{28,16},{1,13},{... | collective-permute-start | bytes 245768 | tf_op jit(solution)/shard_map/ppermute | solution.py:606
  36.5 5.5 %collective-permute-start.12 = (f32[160,128]{1,0:T(8,128)S(1)}, f32[160,128]{1,0:T(8,128)S(1)}, u32[]{:S(2)}, u32[]{:S(2)}) collective-permute-start(f32[160,128]{1,0:T(8,128)S(1)} %get-tuple-element.201), channel_id=1, source_target_pairs={{0,16},{4,20},{8,24},{12,28},{16,0},{20,4},{24,8},{28,12},{1,17},{... | collective-permute-start | bytes 245768 | tf_op jit(solution)/shard_map/ppermute | solution.py:606
  42.4 4.2 %collective-permute-start.14 = (f32[160,128]{1,0:T(8,128)S(1)}, f32[160,128]{1,0:T(8,128)S(1)}, u32[]{:S(2)}, u32[]{:S(2)}) collective-permute-start(f32[160,128]{1,0:T(8,128)S(1)} %get-tuple-element.208), channel_id=1, source_target_pairs={{0,3},{1,2},{2,1},{3,0},{4,7},{5,6},{6,5},{7,4},{8,11},{9,10},{10,... | collective-permute-start | bytes 245768 | tf_op jit(solution)/shard_map/ppermute | solution.py:614
  46.9 5.1 %collective-permute-start.15 = (f32[160,128]{1,0:T(8,128)S(1)}, f32[160,128]{1,0:T(8,128)S(1)}, u32[]{:S(2)}, u32[]{:S(2)}) collective-permute-start(f32[160,128]{1,0:T(8,128)S(1)} %shard_map.111.refs_0_), channel_id=1, source_target_pairs={{0,8},{4,12},{8,0},{12,4},{16,24},{20,28},{24,16},{28,20},{1,9},{5... | collective-permute-start | bytes 245768 | tf_op jit(solution)/shard_map/ppermute | solution.py:606
  48.4 4.8 %collective-permute-start.16 = (f32[160,128]{1,0:T(8,128)S(1)}, f32[160,128]{1,0:T(8,128)S(1)}, u32[]{:S(2)}, u32[]{:S(2)}) collective-permute-start(f32[160,128]{1,0:T(8,128)S(1)} %shard_map.111.refs_0_), channel_id=1, source_target_pairs={{0,4},{4,0},{8,12},{12,8},{16,20},{20,16},{24,28},{28,24},{1,5},{5... | collective-permute-start | bytes 245768 | tf_op jit(solution)/shard_map/ppermute | solution.py:606
  49.3 5.5 %collective-permute-start.17 = (f32[160,128]{1,0:T(8,128)S(1)}, f32[160,128]{1,0:T(8,128)S(1)}, u32[]{:S(2)}, u32[]{:S(2)}) collective-permute-start(f32[160,128]{1,0:T(8,128)S(1)} %shard_map.111.refs_0_), channel_id=1, source_target_pairs={{0,12},{4,8},{8,4},{12,0},{16,28},{20,24},{24,20},{28,16},{1,13},{... | collective-permute-start | bytes 245768 | tf_op jit(solution)/shard_map/ppermute | solution.py:606
  55.2 6.5 %collective-permute-start.18 = (f32[160,128]{1,0:T(8,128)S(1)}, f32[160,128]{1,0:T(8,128)S(1)}, u32[]{:S(2)}, u32[]{:S(2)}) collective-permute-start(f32[160,128]{1,0:T(8,128)S(1)} %get-tuple-element.225), channel_id=1, source_target_pairs={{0,16},{4,20},{8,24},{12,28},{16,0},{20,4},{24,8},{28,12},{1,17},{... | collective-permute-start | bytes 245768 | tf_op jit(solution)/shard_map/ppermute | solution.py:606
  62.0 2.8 %collective-permute-start.19 = (f32[160,128]{1,0:T(8,128)S(1)}, f32[160,128]{1,0:T(8,128)S(1)}, u32[]{:S(2)}, u32[]{:S(2)}) collective-permute-start(f32[160,128]{1,0:T(8,128)S(1)} %get-tuple-element.229), channel_id=1, source_target_pairs={{0,1},{1,0},{2,3},{3,2},{4,5},{5,4},{6,7},{7,6},{8,9},{9,8},{10,11... | collective-permute-start | bytes 245768 | tf_op jit(solution)/shard_map/ppermute | solution.py:615
  62.0 4.2 %collective-permute-start.20 = (f32[160,128]{1,0:T(8,128)S(1)}, f32[160,128]{1,0:T(8,128)S(1)}, u32[]{:S(2)}, u32[]{:S(2)}) collective-permute-start(f32[160,128]{1,0:T(8,128)S(1)} %get-tuple-element.230), channel_id=1, source_target_pairs={{0,3},{1,2},{2,1},{3,0},{4,7},{5,6},{6,5},{7,4},{8,11},{9,10},{10,... | collective-permute-start | bytes 245768 | tf_op jit(solution)/shard_map/ppermute | solution.py:614
  66.5 5.2 %collective-permute-start.21 = (f32[160,128]{1,0:T(8,128)S(1)}, f32[160,128]{1,0:T(8,128)S(1)}, u32[]{:S(2)}, u32[]{:S(2)}) collective-permute-start(f32[160,128]{1,0:T(8,128)S(1)} %shard_map.119.refs_0_), channel_id=1, source_target_pairs={{0,8},{4,12},{8,0},{12,4},{16,24},{20,28},{24,16},{28,20},{1,9},{5... | collective-permute-start | bytes 245768 | tf_op jit(solution)/shard_map/ppermute | solution.py:606
  67.1 5.3 %collective-permute-start.22 = (f32[160,128]{1,0:T(8,128)S(1)}, f32[160,128]{1,0:T(8,128)S(1)}, u32[]{:S(2)}, u32[]{:S(2)}) collective-permute-start(f32[160,128]{1,0:T(8,128)S(1)} %shard_map.119.refs_0_), channel_id=1, source_target_pairs={{0,4},{4,0},{8,12},{12,8},{16,20},{20,16},{24,28},{28,24},{1,5},{5... | collective-permute-start | bytes 245768 | tf_op jit(solution)/shard_map/ppermute | solution.py:606
  68.0 5.3 %collective-permute-start.23 = (f32[160,128]{1,0:T(8,128)S(1)}, f32[160,128]{1,0:T(8,128)S(1)}, u32[]{:S(2)}, u32[]{:S(2)}) collective-permute-start(f32[160,128]{1,0:T(8,128)S(1)} %shard_map.119.refs_0_), channel_id=1, source_target_pairs={{0,12},{4,8},{8,4},{12,0},{16,28},{20,24},{24,20},{28,16},{1,13},{... | collective-permute-start | bytes 245768 | tf_op jit(solution)/shard_map/ppermute | solution.py:606
  73.7 5.4 %collective-permute-start.24 = (f32[160,128]{1,0:T(8,128)S(1)}, f32[160,128]{1,0:T(8,128)S(1)}, u32[]{:S(2)}, u32[]{:S(2)}) collective-permute-start(f32[160,128]{1,0:T(8,128)S(1)} %get-tuple-element.246), channel_id=1, source_target_pairs={{0,16},{4,20},{8,24},{12,28},{16,0},{20,4},{24,8},{28,12},{1,17},{... | collective-permute-start | bytes 245768 | tf_op jit(solution)/shard_map/ppermute | solution.py:606
  (1 other events, 2.8 us)

commit v6 on v5

--- a/solution.py
+++ b/solution.py
@@ -174,14 +174,17 @@
         for m in range(faces):
             row = 2 + q * faces + m
             flags[row : row + 1, :] = jnp.full((1, LANES), (links[s, m] < 2).astype(F32))
-    for c in copies:
-        c.wait()
+    copies[0].wait()
+    copies[1].wait()
     far = mm(trace[...], inverse[b]) * alive
-    start = jnp.concatenate([exact_times(inverse[a], rhs[a]), mm_t(inverse[a], head[...])], axis=1)
+    far_high, far_low = two(far)
+    copies[2].wait()
+    lifted = mm_t(far_high, head[...]) + mm_t(far_low, head[...])
+    answer = mm_t(inverse[a], head[...])
+    copies[3].wait()
+    start = jnp.concatenate([exact_times(inverse[a], rhs[a]), answer], axis=1)
     near = exact_times(trace[...], start)
     packed[pl.ds(pl.multiple_of(a * width, 8), width), :] = near[:, :columns]
-    far_high, far_low = two(far)
-    lifted = mm_t(far_high, head[...]) + mm_t(far_low, head[...])
     shown = map_times(far_high, far_low, rhs[b])
     met = None
     for m in range(faces):

time: 80.3 us -> 80.5 us (level)
  no operation moved by 1% of the time
where the time goes in v6:
time: 80.5 us; the launch traced here: 80.3 us
  starting transfers between devices  33.1 us (41%)
  Pallas kernels  25.1 us (31%)
  waiting for transfers between devices  21.1 us (26%)
  between operations  0.98 us (1%)
    ppermute x19, starting transfers between devices, exchange(): return lax.ppermute(block, axis, pairs)  27.9 us
    pallas_call x36, Pallas kernels, call(): pl.pallas_call(body, out_shape=list(outs), in_specs=spaces or [vmem] * le...  25.1 us
    ppermute x19, waiting for transfers between devices, exchange(): return lax.ppermute(block, axis, pairs)  16.5 us
    ppermute x3, starting transfers between devices, side_exchange(): second = lax.ppermute(second, 'span', across)  4.95 us
    ppermute x3, waiting for transfers between devices, side_exchange(): second = lax.ppermute(second, 'span', across)  4.61 us
  transfers between devices with their start and end apart: 25, of which 13 were waited for; matrix products, arithmetic and copies ran while one was open for 0% of the time, Pallas kernels for 23%

profile of v6, /device:TPU:0, one launch (start us, length us, event | category | flops | bytes accessed | tf_op | source)
XLA Modules:
  0.0 80.3 jit_solution(15502982045681004160)
XLA Ops:
  0.7 3.0 %shard_map.91 = (f32[320,128]{1,0:T(8,128)S(1)}, f32[8,128]{1,0:T(8,128)S(1)}) custom-call(s32[2]{0:T(128)} %bitcast.20, s32[1]{0:T(128)} %bitcast.10.count_in, s32[2,2]{1,0:T(2,128)} %bitcast.17, s32[2,2]{1,0:T(2,128)} %bitcast.18, f32[2,320,128]{2,1,0:T(8,128)} %bitcast.13, bf16[2,320,320]{2,1,0:T(8,128)(2,1)} %bitcast.11, bf16[6,320,320]{2,1,0:T(8,128)(2,1)} %table_in.3, ...), custom_call_target="tpu_custom_call" | custom-call | flops 524288000 | bytes 2543660 | tf_op jit(solution)/shard_map/pallas_call | solution.py:104
  3.6 3.1 %collective-permute-start = (f32[320,128]{1,0:T(8,128)S(1)}, f32[320,128]{1,0:T(8,128)S(1)}, u32[]{:S(2)}, u32[]{:S(2)}) collective-permute-start(f32[320,128]{1,0:T(8,128)S(1)} %get-tuple-element.142.refs_0_), channel_id=1, source_target_pairs={{0,8},{4,12},{8,0},{12,4},{16,24},{20,28},{24,16},{28,20},{1,9},{5... | collective-permute-start | bytes 491528 | tf_op jit(solution)/shard_map/ppermute | solution.py:609
  6.7 1.5 %collective-permute-start.1 = (f32[320,128]{1,0:T(8,128)S(1)}, f32[320,128]{1,0:T(8,128)S(1)}, u32[]{:S(2)}, u32[]{:S(2)}) collective-permute-start(f32[320,128]{1,0:T(8,128)S(1)} %get-tuple-element.142.refs_0_), channel_id=1, source_target_pairs={{0,4},{4,0},{8,12},{12,8},{16,20},{20,16},{24,28},{28,24},{1,5},{5... | collective-permute-start | bytes 491528 | tf_op jit(solution)/shard_map/ppermute | solution.py:609
  8.3 5.6 %shard_map.92 = (bf16[4,80,320]{2,1,0:T(8,128)(2,1)S(1)}, f32[2,320,128]{2,1,0:T(8,128)S(1)}, bf16[2,320,512]{2,1,0:T(8,128)(2,1)S(1)}, bf16[2,320,512]{2,1,0:T(...) custom-call(s32[2]{0:T(128)} %bitcast.21, ...), custom_call_target="tpu_custom_call" | custom-call | flops 1310720000 | bytes 6107160 | tf_op jit(solution)/shard_map/pallas_call | solution.py:104
  13.9 2.0 %collective-permute-done.1.refs_2_ = f32[320,128]{1,0:T(8,128)S(1)} collective-permute-done((f32[320,128]{1,0:T(8,128)S(1)}, f32[320,128]{1,0:T(8,128)S(1)}, u32[]{:S(2)}, u32[]{:S(2)}) %collective-permute-start.1) | collective-permute-done | bytes 163872 | tf_op jit(solution)/shard_map/ppermute | solution.py:609
  16.7 2.7 %collective-permute-start.3 = (f32[160,128]{1,0:T(8,128)S(1)}, f32[160,128]{1,0:T(8,128)S(1)}, u32[]{:S(2)}, u32[]{:S(2)}) collective-permute-start(f32[160,128]{1,0:T(8,128)S(1)} %get-tuple-element.158), channel_id=1, source_target_pairs={{0,16},{4,20},{8,24},{12,28},{16,0},{20,4},{24,8},{28,12},{1,17},{... | collective-permute-start | bytes 245768 | tf_op jit(solution)/shard_map/ppermute | solution.py:609
  21.9 1.5 %collective-permute-start.11 = (f32[160,128]{1,0:T(8,128)S(1)}, f32[160,128]{1,0:T(8,128)S(1)}, u32[]{:S(2)}, u32[]{:S(2)}) collective-permute-start(f32[160,128]{1,0:T(8,128)S(1)} %get-tuple-element.186.refs_0_), channel_id=1, source_target_pairs={{0,12},{4,8},{8,4},{12,0},{16,28},{20,24},{24,20},{28,16},{1,13},{... | collective-permute-start | bytes 245768 | tf_op jit(solution)/shard_map/ppermute | solution.py:609
  24.4 1.6 %collective-permute-start.5 = (f32[160,128]{1,0:T(8,128)S(1)}, f32[160,128]{1,0:T(8,128)S(1)}, u32[]{:S(2)}, u32[]{:S(2)}) collective-permute-start(f32[160,128]{1,0:T(8,128)S(1)} %get-tuple-element.170), channel_id=1, source_target_pairs={{0,3},{1,2},{2,1},{3,0},{4,7},{5,6},{6,5},{7,4},{8,11},{9,10},{10,... | collective-permute-start | bytes 245768 | tf_op jit(solution)/shard_map/ppermute | solution.py:617
  27.1 1.5 %collective-permute-done.5.second.refs_2_ = f32[160,128]{1,0:T(8,128)S(1)} collective-permute-done((f32[160,128]{1,0:T(8,128)S(1)}, f32[160,128]{1,0:T(8,128)S(1)}, u32[]{:S(2)}, u32[]{:S(2)}) %collective-permute-start.5) | collective-permute-done | bytes 81952 | tf_op jit(solution)/shard_map/ppermute | solution.py:617
  28.9 1.3 %collective-permute-start.6 = (f32[160,128]{1,0:T(8,128)S(1)}, f32[160,128]{1,0:T(8,128)S(1)}, u32[]{:S(2)}, u32[]{:S(2)}) collective-permute-start(f32[160,128]{1,0:T(8,128)S(1)} %shard_map.99.refs_0_), channel_id=1, source_target_pairs={{0,8},{4,12},{8,0},{12,4},{16,24},{20,28},{24,16},{28,20},{1,9},{5... | collective-permute-start | bytes 245768 | tf_op jit(solution)/shard_map/ppermute | solution.py:609
  30.9 1.5 %collective-permute-start.8 = (f32[160,128]{1,0:T(8,128)S(1)}, f32[160,128]{1,0:T(8,128)S(1)}, u32[]{:S(2)}, u32[]{:S(2)}) collective-permute-start(f32[160,128]{1,0:T(8,128)S(1)} %shard_map.99.refs_0_), channel_id=1, source_target_pairs={{0,12},{4,8},{8,4},{12,0},{16,28},{20,24},{24,20},{28,16},{1,13},{... | collective-permute-start | bytes 245768 | tf_op jit(solution)/shard_map/ppermute | solution.py:609
  36.7 1.6 %collective-permute-start.12 = (f32[160,128]{1,0:T(8,128)S(1)}, f32[160,128]{1,0:T(8,128)S(1)}, u32[]{:S(2)}, u32[]{:S(2)}) collective-permute-start(f32[160,128]{1,0:T(8,128)S(1)} %get-tuple-element.201), channel_id=1, source_target_pairs={{0,16},{4,20},{8,24},{12,28},{16,0},{20,4},{24,8},{28,12},{1,17},{... | collective-permute-start | bytes 245768 | tf_op jit(solution)/shard_map/ppermute | solution.py:609
  39.8 2.4 %collective-permute-done.12.arrived = f32[160,128]{1,0:T(8,128)S(1)} collective-permute-done((f32[160,128]{1,0:T(8,128)S(1)}, f32[160,128]{1,0:T(8,128)S(1)}, u32[]{:S(2)}, u32[]{:S(2)}) %collective-permute-start.12) | collective-permute-done | bytes 81952 | tf_op jit(solution)/shard_map/ppermute | solution.py:609
  42.6 1.6 %collective-permute-start.14 = (f32[160,128]{1,0:T(8,128)S(1)}, f32[160,128]{1,0:T(8,128)S(1)}, u32[]{:S(2)}, u32[]{:S(2)}) collective-permute-start(f32[160,128]{1,0:T(8,128)S(1)} %get-tuple-element.208), channel_id=1, source_target_pairs={{0,3},{1,2},{2,1},{3,0},{4,7},{5,6},{6,5},{7,4},{8,11},{9,10},{10,... | collective-permute-start | bytes 245768 | tf_op jit(solution)/shard_map/ppermute | solution.py:617
  45.3 1.5 %collective-permute-done.14.second.refs_2_ = f32[160,128]{1,0:T(8,128)S(1)} collective-permute-done((f32[160,128]{1,0:T(8,128)S(1)}, f32[160,128]{1,0:T(8,128)S(1)}, u32[]{:S(2)}, u32[]{:S(2)}) %collective-permute-start.14) | collective-permute-done | bytes 81952 | tf_op jit(solution)/shard_map/ppermute | solution.py:617
  47.1 1.5 %collective-permute-start.15 = (f32[160,128]{1,0:T(8,128)S(1)}, f32[160,128]{1,0:T(8,128)S(1)}, u32[]{:S(2)}, u32[]{:S(2)}) collective-permute-start(f32[160,128]{1,0:T(8,128)S(1)} %shard_map.111.refs_0_), channel_id=1, source_target_pairs={{0,8},{4,12},{8,0},{12,4},{16,24},{20,28},{24,16},{28,20},{1,9},{5... | collective-permute-start | bytes 245768 | tf_op jit(solution)/shard_map/ppermute | solution.py:609
  53.4 1.6 %collective-permute-done.17.refs_3_ = f32[160,128]{1,0:T(8,128)S(1)} collective-permute-done((f32[160,128]{1,0:T(8,128)S(1)}, f32[160,128]{1,0:T(8,128)S(1)}, u32[]{:S(2)}, u32[]{:S(2)}) %collective-permute-start.17) | collective-permute-done | bytes 81952 | tf_op jit(solution)/shard_map/ppermute | solution.py:609
  55.4 2.1 %collective-permute-start.18 = (f32[160,128]{1,0:T(8,128)S(1)}, f32[160,128]{1,0:T(8,128)S(1)}, u32[]{:S(2)}, u32[]{:S(2)}) collective-permute-start(f32[160,128]{1,0:T(8,128)S(1)} %get-tuple-element.225), channel_id=1, source_target_pairs={{0,16},{4,20},{8,24},{12,28},{16,0},{20,4},{24,8},{28,12},{1,17},{... | collective-permute-start | bytes 245768 | tf_op jit(solution)/shard_map/ppermute | solution.py:609
  58.1 3.7 %collective-permute-done.18.arrived = f32[160,128]{1,0:T(8,128)S(1)} collective-permute-done((f32[160,128]{1,0:T(8,128)S(1)}, f32[160,128]{1,0:T(8,128)S(1)}, u32[]{:S(2)}, u32[]{:S(2)}) %collective-permute-start.18) | collective-permute-done | bytes 81952 | tf_op jit(solution)/shard_map/ppermute | solution.py:609
  62.2 1.7 %collective-permute-start.20 = (f32[160,128]{1,0:T(8,128)S(1)}, f32[160,128]{1,0:T(8,128)S(1)}, u32[]{:S(2)}, u32[]{:S(2)}) collective-permute-start(f32[160,128]{1,0:T(8,128)S(1)} %get-tuple-element.230), channel_id=1, source_target_pairs={{0,3},{1,2},{2,1},{3,0},{4,7},{5,6},{6,5},{7,4},{8,11},{9,10},{10,... | collective-permute-start | bytes 245768 | tf_op jit(solution)/shard_map/ppermute | solution.py:617
  64.9 1.5 %collective-permute-done.20.second.refs_2_ = f32[160,128]{1,0:T(8,128)S(1)} collective-permute-done((f32[160,128]{1,0:T(8,128)S(1)}, f32[160,128]{1,0:T(8,128)S(1)}, u32[]{:S(2)}, u32[]{:S(2)}) %collective-permute-start.20) | collective-permute-done | bytes 81952 | tf_op jit(solution)/shard_map/ppermute | solution.py:617
  68.1 2.2 %collective-permute-start.23 = (f32[160,128]{1,0:T(8,128)S(1)}, f32[160,128]{1,0:T(8,128)S(1)}, u32[]{:S(2)}, u32[]{:S(2)}) collective-permute-start(f32[160,128]{1,0:T(8,128)S(1)} %shard_map.119.refs_0_), channel_id=1, source_target_pairs={{0,12},{4,8},{8,4},{12,0},{16,28},{20,24},{24,20},{28,16},{1,13},{... | collective-permute-start | bytes 245768 | tf_op jit(solution)/shard_map/ppermute | solution.py:609
  73.8 2.6 %collective-permute-start.24 = (f32[160,128]{1,0:T(8,128)S(1)}, f32[160,128]{1,0:T(8,128)S(1)}, u32[]{:S(2)}, u32[]{:S(2)}) collective-permute-start(f32[160,128]{1,0:T(8,128)S(1)} %get-tuple-element.246), channel_id=1, source_target_pairs={{0,16},{4,20},{8,24},{12,28},{16,0},{20,4},{24,8},{28,12},{1,17},{... | collective-permute-start | bytes 245768 | tf_op jit(solution)/shard_map/ppermute | solution.py:609
  77.7 1.6 %collective-permute-done.24.arrived = f32[160,128]{1,0:T(8,128)S(1)} collective-permute-done((f32[160,128]{1,0:T(8,128)S(1)}, f32[160,128]{1,0:T(8,128)S(1)}, u32[]{:S(2)}, u32[]{:S(2)}) %collective-permute-start.24) | collective-permute-done | bytes 81952 | tf_op jit(solution)/shard_map/ppermute | solution.py:609
  (63 shorter events, 28.2 us)
Async XLA Ops:
  3.6 10.2 %collective-permute-start = (f32[320,128]{1,0:T(8,128)S(1)}, f32[320,128]{1,0:T(8,128)S(1)}, u32[]{:S(2)}, u32[]{:S(2)}) collective-permute-start(f32[320,128]{1,0:T(8,128)S(1)} %get-tuple-element.142.refs_0_), channel_id=1, source_target_pairs={{0,8},{4,12},{8,0},{12,4},{16,24},{20,28},{24,16},{28,20},{1,9},{5... | collective-permute-start | bytes 491528 | tf_op jit(solution)/shard_map/ppermute | solution.py:609
  6.7 9.2 %collective-permute-start.1 = (f32[320,128]{1,0:T(8,128)S(1)}, f32[320,128]{1,0:T(8,128)S(1)}, u32[]{:S(2)}, u32[]{:S(2)}) collective-permute-start(f32[320,128]{1,0:T(8,128)S(1)} %get-tuple-element.142.refs_0_), channel_id=1, source_target_pairs={{0,4},{4,0},{8,12},{12,8},{16,20},{20,16},{24,28},{28,24},{1,5},{5... | collective-permute-start | bytes 491528 | tf_op jit(solution)/shard_map/ppermute | solution.py:609
  8.2 7.7 %collective-permute-start.2 = (f32[320,128]{1,0:T(8,128)S(1)}, f32[320,128]{1,0:T(8,128)S(1)}, u32[]{:S(2)}, u32[]{:S(2)}) collective-permute-start(f32[320,128]{1,0:T(8,128)S(1)} %get-tuple-element.142.refs_0_), channel_id=1, source_target_pairs={{0,12},{4,8},{8,4},{12,0},{16,28},{20,24},{24,20},{28,16},{1,13},{... | collective-permute-start | bytes 491528 | tf_op jit(solution)/shard_map/ppermute | solution.py:609
  16.7 7.3 %collective-permute-start.3 = (f32[160,128]{1,0:T(8,128)S(1)}, f32[160,128]{1,0:T(8,128)S(1)}, u32[]{:S(2)}, u32[]{:S(2)}) collective-permute-start(f32[160,128]{1,0:T(8,128)S(1)} %get-tuple-element.158), channel_id=1, source_target_pairs={{0,16},{4,20},{8,24},{12,28},{16,0},{20,4},{24,8},{28,12},{1,17},{... | collective-permute-start | bytes 245768 | tf_op jit(solution)/shard_map/ppermute | solution.py:609
  19.9 11.1 %collective-permute-start.9 = (f32[160,128]{1,0:T(8,128)S(1)}, f32[160,128]{1,0:T(8,128)S(1)}, u32[]{:S(2)}, u32[]{:S(2)}) collective-permute-start(f32[160,128]{1,0:T(8,128)S(1)} %get-tuple-element.186.refs_0_), channel_id=1, source_target_pairs={{0,8},{4,12},{8,0},{12,4},{16,24},{20,28},{24,16},{28,20},{1,9},{5... | collective-permute-start | bytes 245768 | tf_op jit(solution)/shard_map/ppermute | solution.py:609
  21.1 12.5 %collective-permute-start.10 = (f32[160,128]{1,0:T(8,128)S(1)}, f32[160,128]{1,0:T(8,128)S(1)}, u32[]{:S(2)}, u32[]{:S(2)}) collective-permute-start(f32[160,128]{1,0:T(8,128)S(1)} %get-tuple-element.186.refs_0_), channel_id=1, source_target_pairs={{0,4},{4,0},{8,12},{12,8},{16,20},{20,16},{24,28},{28,24},{1,5},{5... | collective-permute-start | bytes 245768 | tf_op jit(solution)/shard_map/ppermute | solution.py:609
  21.9 11.7 %collective-permute-start.11 = (f32[160,128]{1,0:T(8,128)S(1)}, f32[160,128]{1,0:T(8,128)S(1)}, u32[]{:S(2)}, u32[]{:S(2)}) collective-permute-start(f32[160,128]{1,0:T(8,128)S(1)} %get-tuple-element.186.refs_0_), channel_id=1, source_target_pairs={{0,12},{4,8},{8,4},{12,0},{16,28},{20,24},{24,20},{28,16},{1,13},{... | collective-permute-start | bytes 245768 | tf_op jit(solution)/shard_map/ppermute | solution.py:609
  24.3 2.8 %collective-permute-start.4 = (f32[160,128]{1,0:T(8,128)S(1)}, f32[160,128]{1,0:T(8,128)S(1)}, u32[]{:S(2)}, u32[]{:S(2)}) collective-permute-start(f32[160,128]{1,0:T(8,128)S(1)} %get-tuple-element.169), channel_id=1, source_target_pairs={{0,1},{1,0},{2,3},{3,2},{4,5},{5,4},{6,7},{7,6},{8,9},{9,8},{10,11... | collective-permute-start | bytes 245768 | tf_op jit(solution)/shard_map/ppermute | solution.py:618
  24.4 4.2 %collective-permute-start.5 = (f32[160,128]{1,0:T(8,128)S(1)}, f32[160,128]{1,0:T(8,128)S(1)}, u32[]{:S(2)}, u32[]{:S(2)}) collective-permute-start(f32[160,128]{1,0:T(8,128)S(1)} %get-tuple-element.170), channel_id=1, source_target_pairs={{0,3},{1,2},{2,1},{3,0},{4,7},{5,6},{6,5},{7,4},{8,11},{9,10},{10,... | collective-permute-start | bytes 245768 | tf_op jit(solution)/shard_map/ppermute | solution.py:617
  28.9 6.2 %collective-permute-start.6 = (f32[160,128]{1,0:T(8,128)S(1)}, f32[160,128]{1,0:T(8,128)S(1)}, u32[]{:S(2)}, u32[]{:S(2)}) collective-permute-start(f32[160,128]{1,0:T(8,128)S(1)} %shard_map.99.refs_0_), channel_id=1, source_target_pairs={{0,8},{4,12},{8,0},{12,4},{16,24},{20,28},{24,16},{28,20},{1,9},{5... | collective-permute-start | bytes 245768 | tf_op jit(solution)/shard_map/ppermute | solution.py:609
  30.2 5.0 %collective-permute-start.7 = (f32[160,128]{1,0:T(8,128)S(1)}, f32[160,128]{1,0:T(8,128)S(1)}, u32[]{:S(2)}, u32[]{:S(2)}) collective-permute-start(f32[160,128]{1,0:T(8,128)S(1)} %shard_map.99.refs_0_), channel_id=1, source_target_pairs={{0,4},{4,0},{8,12},{12,8},{16,20},{20,16},{24,28},{28,24},{1,5},{5... | collective-permute-start | bytes 245768 | tf_op jit(solution)/shard_map/ppermute | solution.py:609
  30.9 5.4 %collective-permute-start.8 = (f32[160,128]{1,0:T(8,128)S(1)}, f32[160,128]{1,0:T(8,128)S(1)}, u32[]{:S(2)}, u32[]{:S(2)}) collective-permute-start(f32[160,128]{1,0:T(8,128)S(1)} %shard_map.99.refs_0_), channel_id=1, source_target_pairs={{0,12},{4,8},{8,4},{12,0},{16,28},{20,24},{24,20},{28,16},{1,13},{... | collective-permute-start | bytes 245768 | tf_op jit(solution)/shard_map/ppermute | solution.py:609
  36.7 5.5 %collective-permute-start.12 = (f32[160,128]{1,0:T(8,128)S(1)}, f32[160,128]{1,0:T(8,128)S(1)}, u32[]{:S(2)}, u32[]{:S(2)}) collective-permute-start(f32[160,128]{1,0:T(8,128)S(1)} %get-tuple-element.201), channel_id=1, source_target_pairs={{0,16},{4,20},{8,24},{12,28},{16,0},{20,4},{24,8},{28,12},{1,17},{... | collective-permute-start | bytes 245768 | tf_op jit(solution)/shard_map/ppermute | solution.py:609
  42.6 4.2 %collective-permute-start.14 = (f32[160,128]{1,0:T(8,128)S(1)}, f32[160,128]{1,0:T(8,128)S(1)}, u32[]{:S(2)}, u32[]{:S(2)}) collective-permute-start(f32[160,128]{1,0:T(8,128)S(1)} %get-tuple-element.208), channel_id=1, source_target_pairs={{0,3},{1,2},{2,1},{3,0},{4,7},{5,6},{6,5},{7,4},{8,11},{9,10},{10,... | collective-permute-start | bytes 245768 | tf_op jit(solution)/shard_map/ppermute | solution.py:617
  47.1 5.1 %collective-permute-start.15 = (f32[160,128]{1,0:T(8,128)S(1)}, f32[160,128]{1,0:T(8,128)S(1)}, u32[]{:S(2)}, u32[]{:S(2)}) collective-permute-start(f32[160,128]{1,0:T(8,128)S(1)} %shard_map.111.refs_0_), channel_id=1, source_target_pairs={{0,8},{4,12},{8,0},{12,4},{16,24},{20,28},{24,16},{28,20},{1,9},{5... | collective-permute-start | bytes 245768 | tf_op jit(solution)/shard_map/ppermute | solution.py:609
  48.6 4.8 %collective-permute-start.16 = (f32[160,128]{1,0:T(8,128)S(1)}, f32[160,128]{1,0:T(8,128)S(1)}, u32[]{:S(2)}, u32[]{:S(2)}) collective-permute-start(f32[160,128]{1,0:T(8,128)S(1)} %shard_map.111.refs_0_), channel_id=1, source_target_pairs={{0,4},{4,0},{8,12},{12,8},{16,20},{20,16},{24,28},{28,24},{1,5},{5... | collective-permute-start | bytes 245768 | tf_op jit(solution)/shard_map/ppermute | solution.py:609
  49.5 5.5 %collective-permute-start.17 = (f32[160,128]{1,0:T(8,128)S(1)}, f32[160,128]{1,0:T(8,128)S(1)}, u32[]{:S(2)}, u32[]{:S(2)}) collective-permute-start(f32[160,128]{1,0:T(8,128)S(1)} %shard_map.111.refs_0_), channel_id=1, source_target_pairs={{0,12},{4,8},{8,4},{12,0},{16,28},{20,24},{24,20},{28,16},{1,13},{... | collective-permute-start | bytes 245768 | tf_op jit(solution)/shard_map/ppermute | solution.py:609
  55.4 6.5 %collective-permute-start.18 = (f32[160,128]{1,0:T(8,128)S(1)}, f32[160,128]{1,0:T(8,128)S(1)}, u32[]{:S(2)}, u32[]{:S(2)}) collective-permute-start(f32[160,128]{1,0:T(8,128)S(1)} %get-tuple-element.225), channel_id=1, source_target_pairs={{0,16},{4,20},{8,24},{12,28},{16,0},{20,4},{24,8},{28,12},{1,17},{... | collective-permute-start | bytes 245768 | tf_op jit(solution)/shard_map/ppermute | solution.py:609
  62.1 2.8 %collective-permute-start.19 = (f32[160,128]{1,0:T(8,128)S(1)}, f32[160,128]{1,0:T(8,128)S(1)}, u32[]{:S(2)}, u32[]{:S(2)}) collective-permute-start(f32[160,128]{1,0:T(8,128)S(1)} %get-tuple-element.229), channel_id=1, source_target_pairs={{0,1},{1,0},{2,3},{3,2},{4,5},{5,4},{6,7},{7,6},{8,9},{9,8},{10,11... | collective-permute-start | bytes 245768 | tf_op jit(solution)/shard_map/ppermute | solution.py:618
  62.2 4.2 %collective-permute-start.20 = (f32[160,128]{1,0:T(8,128)S(1)}, f32[160,128]{1,0:T(8,128)S(1)}, u32[]{:S(2)}, u32[]{:S(2)}) collective-permute-start(f32[160,128]{1,0:T(8,128)S(1)} %get-tuple-element.230), channel_id=1, source_target_pairs={{0,3},{1,2},{2,1},{3,0},{4,7},{5,6},{6,5},{7,4},{8,11},{9,10},{10,... | collective-permute-start | bytes 245768 | tf_op jit(solution)/shard_map/ppermute | solution.py:617
  66.7 5.2 %collective-permute-start.21 = (f32[160,128]{1,0:T(8,128)S(1)}, f32[160,128]{1,0:T(8,128)S(1)}, u32[]{:S(2)}, u32[]{:S(2)}) collective-permute-start(f32[160,128]{1,0:T(8,128)S(1)} %shard_map.119.refs_0_), channel_id=1, source_target_pairs={{0,8},{4,12},{8,0},{12,4},{16,24},{20,28},{24,16},{28,20},{1,9},{5... | collective-permute-start | bytes 245768 | tf_op jit(solution)/shard_map/ppermute | solution.py:609
  67.3 5.4 %collective-permute-start.22 = (f32[160,128]{1,0:T(8,128)S(1)}, f32[160,128]{1,0:T(8,128)S(1)}, u32[]{:S(2)}, u32[]{:S(2)}) collective-permute-start(f32[160,128]{1,0:T(8,128)S(1)} %shard_map.119.refs_0_), channel_id=1, source_target_pairs={{0,4},{4,0},{8,12},{12,8},{16,20},{20,16},{24,28},{28,24},{1,5},{5... | collective-permute-start | bytes 245768 | tf_op jit(solution)/shard_map/ppermute | solution.py:609
  68.1 5.4 %collective-permute-start.23 = (f32[160,128]{1,0:T(8,128)S(1)}, f32[160,128]{1,0:T(8,128)S(1)}, u32[]{:S(2)}, u32[]{:S(2)}) collective-permute-start(f32[160,128]{1,0:T(8,128)S(1)} %shard_map.119.refs_0_), channel_id=1, source_target_pairs={{0,12},{4,8},{8,4},{12,0},{16,28},{20,24},{24,20},{28,16},{1,13},{... | collective-permute-start | bytes 245768 | tf_op jit(solution)/shard_map/ppermute | solution.py:609
  73.8 5.4 %collective-permute-start.24 = (f32[160,128]{1,0:T(8,128)S(1)}, f32[160,128]{1,0:T(8,128)S(1)}, u32[]{:S(2)}, u32[]{:S(2)}) collective-permute-start(f32[160,128]{1,0:T(8,128)S(1)} %get-tuple-element.246), channel_id=1, source_target_pairs={{0,16},{4,20},{8,24},{12,28},{16,0},{20,4},{24,8},{28,12},{1,17},{... | collective-permute-start | bytes 245768 | tf_op jit(solution)/shard_map/ppermute | solution.py:609
  (1 other events, 2.8 us)
